TPU v7x, 128 devices: a whole 4x4x4 slice. The times are simulated.
128 devices in a mesh: wide: 16 (over y_lo, x, core), narrow: 8 (over y_hi, z).
Axes of the slice: x: 4, y: 4 (y_hi: 2, y_lo: 2; y = y_hi * 2 + y_lo), z: 4, core: 2. Of those that a mesh axis runs over, the one named last changes fastest.
Arguments:
- fine_input: bfloat16 [4, 512, 128, 256], P(None, 'wide', 'narrow'), may hold values from -8 to 8
- gain_fine: float32 [256], replicated, may hold values from 0.1 to 1.9
- kernel_fine: bfloat16 [3, 3, 256, 256], replicated, may hold values from -0.125 to 0.125
- down_mid: bfloat16 [256, 512], replicated, may hold values from -1.5 to 1.5
- gain_mid: float32 [512], replicated, may hold values from 0.1 to 1.9
- kernel_mid: bfloat16 [3, 3, 512, 512], replicated, may hold values from -0.09375 to 0.09375
- down_coarse: bfloat16 [512, 512], replicated, may hold values from -1 to 1
- gain_coarse: float32 [512], replicated, may hold values from 0.1 to 1.9
- kernel_coarse: bfloat16 [3, 3, 512, 512], replicated, may hold values from -0.09375 to 0.09375
- up_coarse: bfloat16 [512, 512], replicated, may hold values from -0.25 to 0.25
- up_mid: bfloat16 [512, 256], replicated, may hold values from -0.25 to 0.25
- grad_out: bfloat16 [4, 512, 128, 256], P(None, 'wide', 'narrow'), may hold values from -6 to 6
Outputs:
- fine_output: bfloat16 [4, 512, 128, 256], P(None, 'wide', 'narrow')
- grad_input: float32 [4, 512, 128, 256], P(None, 'wide', 'narrow')
All inputs are finite; a program needn't handle non-finite values.
Results may differ from a plain program's by a relative error of at most 0.022.
Values may be sent and summed in bfloat16 or wider, within the bound.
A program may use at most 128 MiB of HBM per device.

v0:
```python
import jax
import jax.numpy as jnp
from jax import lax
from jax.sharding import PartitionSpec as P

GROUPS = 32


epsilon = 1e-05


def with_halo(block, sides, width):
    for axis, dim in sides:
        count = lax.axis_size(axis)
        forward = [(i, i + 1) for i in range(count - 1)]
        backward = [(target, source) for source, target in forward]
        low = lax.ppermute(
            lax.slice_in_dim(block, block.shape[dim] - width, None, axis=dim), axis, forward
        )
        high = lax.ppermute(lax.slice_in_dim(block, 0, width, axis=dim), axis, backward)
        block = jnp.concatenate([low, block, high], axis=dim)
    return block


def convolve(padded, kernel):
    return lax.conv_general_dilated(
        padded,
        kernel,
        (1, 1),
        "VALID",
        dimension_numbers=("NHWC", "HWIO", "NHWC"),
        preferred_element_type=jnp.float32,
    )


def group_sums(values):
    per_channel = jnp.sum(values, axis=(0, 1, 2))
    return jnp.sum(per_channel.reshape(GROUPS, -1), axis=1)


def spread(vector, channels):
    return jnp.broadcast_to(vector[:, None], (GROUPS, channels // GROUPS)).reshape(channels)


def average_blocks(tensor):
    frames, height, breadth, channels = tensor.shape
    return jnp.mean(
        tensor.astype(jnp.float32).reshape(frames, height // 4, 4, breadth // 4, 4, channels),
        axis=(2, 4),
    )


def sum_blocks(tensor):
    frames, height, breadth, channels = tensor.shape
    return jnp.sum(tensor.reshape(frames, height // 4, 4, breadth // 4, 4, channels), axis=(2, 4))


def enlarge(tensor):
    frames, height, breadth, channels = tensor.shape
    return jnp.broadcast_to(
        tensor[:, :, None, :, None, :], (frames, height, 4, breadth, 4, channels)
    ).reshape(frames, height * 4, breadth * 4, channels)


def project(tensor, matrix):
    return jnp.dot(tensor, matrix, preferred_element_type=jnp.float32)


def fine_pad(tensor):
    return with_halo(tensor, (("wide", 1), ("narrow", 2)), 1)


def fine_total(partial_value):
    return lax.psum((partial_value[0], partial_value[1]), ("wide", "narrow"))


def middle_pad(tensor):
    return with_halo(tensor, (("wide", 1), ("narrow", 2)), 1)


def middle_total(partial_value):
    return lax.psum((partial_value[0], partial_value[1]), ("wide", "narrow"))


def coarse_whole(tensor):
    pieces = lax.all_gather(tensor[None], ("wide", "narrow"), axis=0, tiled=True)
    wide_count = lax.axis_size("wide")
    narrow_count = lax.axis_size("narrow")
    frames, height, breadth, channels = tensor.shape
    arranged = pieces.reshape(wide_count, narrow_count, frames, height, breadth, channels)
    return arranged.transpose(2, 0, 3, 1, 4, 5).reshape(
        frames, wide_count * height, narrow_count * breadth, channels
    )


def local_pad(tensor):
    return jnp.pad(tensor, ((0, 0), (1, 1), (1, 1), (0, 0)))


def local_total(partial_value):
    return partial_value


def tile_part(whole_grid, height, breadth):
    starts = (0, lax.axis_index("wide") * height, lax.axis_index("narrow") * breadth, 0)
    return lax.dynamic_slice(
        whole_grid, starts, (whole_grid.shape[0], height, breadth, whole_grid.shape[3])
    )


def block_forward(inputs, scaling, kernel, pad_fn, total_fn, copies):
    values = inputs.astype(jnp.float32)
    channels = inputs.shape[-1]
    number = values.size // GROUPS * copies
    totals, square = total_fn((group_sums(values), group_sums(values * values)))
    center = totals / number
    inverse = lax.rsqrt(square / number - center * center + epsilon)
    scaled = (values - spread(center, channels)) * spread(inverse, channels)
    normed = scaled * scaling
    activated = jax.nn.silu(normed).astype(jnp.bfloat16)
    result = (values + convolve(pad_fn(activated), kernel)).astype(jnp.bfloat16)
    return (result, center, inverse)


def block_backward(inputs, scaling, kernel, center, inverse, upstream, pad_fn, total_fn, copies):
    values = inputs.astype(jnp.float32)
    channels = inputs.shape[-1]
    number = values.size // GROUPS * copies
    flipped = jnp.transpose(kernel[::-1, ::-1], (0, 1, 3, 2))
    act_grad = convolve(pad_fn(upstream), flipped)
    scaled = (values - spread(center, channels)) * spread(inverse, channels)
    normed = scaled * scaling
    logistic = jax.nn.sigmoid(normed)
    normed_grad = act_grad * logistic * (1.0 + normed * (1.0 - logistic)) * scaling
    first_sum, second_sum = total_fn((group_sums(normed_grad), group_sums(normed_grad * scaled)))
    return upstream.astype(jnp.float32) + spread(inverse, channels) * (
        normed_grad
        - spread(first_sum / number, channels)
        - scaled * spread(second_sum / number, channels)
    )


def shards(
    fine_input,
    gain_fine,
    kernel_fine,
    down_mid,
    gain_mid,
    kernel_mid,
    down_coarse,
    gain_coarse,
    kernel_coarse,
    up_coarse,
    up_mid,
    grad_out,
):
    wide_count = lax.axis_size("wide")
    narrow_count = lax.axis_size("narrow")
    all_count = wide_count * narrow_count
    coarse_copies = 1
    fine_block, fine_center, fine_inverse = block_forward(
        fine_input, gain_fine, kernel_fine, fine_pad, fine_total, all_count
    )
    mid_in = project(average_blocks(fine_block).astype(jnp.bfloat16), down_mid).astype(jnp.bfloat16)
    mid_result, mid_center, mid_inverse = block_forward(
        mid_in, gain_mid, kernel_mid, middle_pad, middle_total, all_count
    )
    coarse_in = project(average_blocks(mid_result).astype(jnp.bfloat16), down_coarse).astype(
        jnp.bfloat16
    )
    coarse_height, coarse_breadth = (coarse_in.shape[1], coarse_in.shape[2])
    coarse_spread = coarse_whole(coarse_in)
    coarse_result, coarse_center, coarse_inverse = block_forward(
        coarse_spread, gain_coarse, kernel_coarse, local_pad, local_total, coarse_copies
    )
    coarse_block = tile_part(coarse_result, coarse_height, coarse_breadth)
    coarse_up = project(coarse_block, up_coarse).astype(jnp.bfloat16)
    mid_sum = (mid_result.astype(jnp.float32) + enlarge(coarse_up.astype(jnp.float32))).astype(
        jnp.bfloat16
    )
    mid_up = project(mid_sum, up_mid).astype(jnp.bfloat16)
    fine_output = (fine_block.astype(jnp.float32) + enlarge(mid_up.astype(jnp.float32))).astype(
        jnp.bfloat16
    )
    upstream = grad_out.astype(jnp.float32)
    up_mid_grad = sum_blocks(upstream).astype(jnp.bfloat16)
    mid_sum_grad = project(up_mid_grad, up_mid.T)
    up_coarse_grad = sum_blocks(mid_sum_grad).astype(jnp.bfloat16)
    coarse_grad = project(up_coarse_grad, up_coarse.T).astype(jnp.bfloat16)
    coarse_grad_spread = coarse_whole(coarse_grad)
    coarse_back = block_backward(
        coarse_spread,
        gain_coarse,
        kernel_coarse,
        coarse_center,
        coarse_inverse,
        coarse_grad_spread,
        local_pad,
        local_total,
        coarse_copies,
    )
    coarse_in_grad = tile_part(coarse_back, coarse_height, coarse_breadth)
    mid_pool_grad = project(coarse_in_grad.astype(jnp.bfloat16), down_coarse.T)
    mid_grad = (mid_sum_grad + 0.0625 * enlarge(mid_pool_grad)).astype(jnp.bfloat16)
    mid_back = block_backward(
        mid_in,
        gain_mid,
        kernel_mid,
        mid_center,
        mid_inverse,
        mid_grad,
        middle_pad,
        middle_total,
        all_count,
    )
    fine_pool_grad = project(mid_back.astype(jnp.bfloat16), down_mid.T)
    fine_grad = (upstream + 0.0625 * enlarge(fine_pool_grad)).astype(jnp.bfloat16)
    grad_input = block_backward(
        fine_input,
        gain_fine,
        kernel_fine,
        fine_center,
        fine_inverse,
        fine_grad,
        fine_pad,
        fine_total,
        all_count,
    )
    return (fine_output, grad_input)


def solution(mesh):
    in_specs = (
        P(None, "wide", "narrow", None),
        P(),
        P(),
        P(),
        P(),
        P(),
        P(),
        P(),
        P(),
        P(),
        P(),
        P(None, "wide", "narrow", None),
    )
    out_specs = (P(None, "wide", "narrow", None), P(None, "wide", "narrow", None))
    return jax.shard_map(shards, mesh=mesh, in_specs=in_specs, out_specs=out_specs, check_vma=False)
```

profile of v0, /device:TPU:0, one launch (start us, length us, event | category | flops | bytes accessed | tf_op | source)
XLA Modules:
  0.0 945.2 jit_solution(17383125747391410789)
XLA Ops:
  9.5 68.2 %all-reduce.3 = (f32[32]{0:T(128)S(1)}, f32[32]{0:T(128)S(1)}) all-reduce(f32[32]{0:T(128)S(1)} %reduce_sum.269, f32[32]{0:T(128)S(1)} %reduce_sum.267), channel_id=1, replica_groups=mesh['wide'=16,'narrow'=8] {'wide','narrow'}, use_global_device_ids=true, to_apply=%region_5.0 | all-reduce | flops 64 | bytes 512 | tf_op jit(solution)/shard_map/psum | solution.py:74
  80.8 2.1 collective-permute-start
  85.9 2.9 reshape.165
  88.8 2.3 reduce_sum.282
  97.3 4.5 collective-permute-done.3
  107.1 4.1 fusion.31
  114.9 2.9 reshape.158
  117.7 2.3 reduce_sum.270
  120.7 70.8 %all-reduce.2 = (f32[32]{0:T(128)S(1)}, f32[32]{0:T(128)S(1)}) all-reduce(f32[32]{0:T(128)S(1)} %reduce_sum.274, f32[32]{0:T(128)S(1)} %reduce_sum.272), channel_id=1, replica_groups=mesh['wide'=16,'narrow'=8] {'wide','narrow'}, use_global_device_ids=true, to_apply=%region_12.13 | all-reduce | flops 64 | bytes 512 | tf_op jit(solution)/shard_map/psum | solution.py:82
  196.9 2.5 collective-permute-start.6
  201.3 4.3 collective-permute-done.7
  205.8 3.8 fusion.58
  214.2 179.0 %all-gather.7.cloned.1.call-done = bf16[512,2,512]{2,1,0:T(2,128)(2,1)} async-done(((bf16[4,2,512]{2,1,0:T(2,128)(2,1)}), bf16[512,2,512]{2,1,0:T(2,128)(2,1)}) %all-gather.7.cloned.1.call-update) | async-done | bytes 1048592 | tf_op jit(solution)/shard_map/all_gather | solution.py:86
  393.2 2.8 copy.79
  396.0 291.4 %all-gather.5.cloned.1.call-done = bf16[512,2,512]{2,1,0:T(2,128)(2,1)} async-done(((bf16[4,2,512]{2,1,0:T(2,128)(2,1)}), bf16[512,2,512]{2,1,0:T(2,128)(2,1)}) %all-gather.5.cloned.1.call-update) | async-done | bytes 1048592 | tf_op jit(solution)/shard_map/all_gather | solution.py:86
  687.4 3.5 convert_reduce_fusion.1
  701.1 13.8 %fusion.87 = (f32[512]{0:T(512)}, f32[512]{0:T(512)}, f32[4,32,8,512]{3,0,2,1:T(4,128)}) fusion(f32[4,32,8,512]{3,0,2,1:T(4,128)S(1)} %subtract_multiply_fusion, f32[512]{0:T(512)S(1)} %copy-done.26, bf16[4,32,8,512]{3,0,2,1:T(4,128)(2,1)S(1)} %bitcast.104, bf16[3,3,512,512]{3,2,1,0:T(8,128)(2,1)} %param.20), kind=kOutput, calls=%fused_computation.147 | convolution fusion | flops 4343725056 | bytes 9967616 | tf_op jit(solution)/shard_map/conv_general_dilated | solution.py:26
  722.6 2.1 collective-permute-start.8
  726.6 9.9 %fusion.40 = f32[4,32,8,512]{3,0,2,1:T(4,128)S(1)} fusion(bf16[3,3,512,512]{3,2,1,0:T(8,128)(2,1)} %param.20, f32[4,32,8,512]{3,0,2,1:T(4,128)} %copy-done.4, f32[512]{0:T(512)} %param.19), kind=kOutput, calls=%fused_computation.60 | convolution fusion | flops 4340056064 | bytes 8914944 | tf_op jit(solution)/shard_map/conv_general_dilated | solution.py:26
  736.7 3.9 collective-permute-start.10
  742.8 4.3 collective-permute-done.11
  750.0 70.1 %all-reduce.1 = (f32[32]{0:T(128)S(1)}, f32[32]{0:T(128)S(1)}) all-reduce(f32[32]{0:T(128)S(1)} %reduce_sum.293, f32[32]{0:T(128)S(1)} %reduce_sum.291), channel_id=1, replica_groups=mesh['wide'=16,'narrow'=8] {'wide','narrow'}, use_global_device_ids=true, to_apply=%region_31.32 | all-reduce | flops 64 | bytes 512 | tf_op jit(solution)/shard_map/psum | solution.py:82
  822.5 2.9 mul.284
  825.5 2.4 add_convert_fusion
  833.5 3.0 reshape.164
  839.6 3.6 add_convert_fusion.1
  848.9 4.2 fusion.34
  854.9 2.6 fusion.86
  857.9 3.0 copy.86
  860.9 71.9 %all-reduce = (f32[32]{0:T(128)S(1)}, f32[32]{0:T(128)S(1)}) all-reduce(f32[32]{0:T(128)S(1)} %reduce_sum.297, f32[32]{0:T(128)S(1)} %reduce_sum.295), channel_id=1, replica_groups=mesh['wide'=16,'narrow'=8] {'wide','narrow'}, use_global_device_ids=true, to_apply=%region_37.38 | all-reduce | flops 64 | bytes 512 | tf_op jit(solution)/shard_map/psum | solution.py:74
  933.2 2.4 fusion.27
  935.6 2.5 copy.87
  (203 shorter events, 80.0 us)
Async XLA Ops:
  7.2 99.9 %copy-start = (bf16[3,3,256,256]{3,2,1,0:T(8,128)(2,1)S(1)}, bf16[3,3,256,256]{3,2,1,0:T(8,128)(2,1)}, u32[]{:S(2)}) copy-start(bf16[3,3,256,256]{3,2,1,0:T(8,128)(2,1)} %param.14) | copy-start | bytes 3538948
  7.2 77.0 %copy-start.3 = (bf16[4,32,16,256]{3,2,1,0:T(8,128)(2,1)S(1)}, bf16[4,32,16,256]{3,2,1,0:T(8,128)(2,1)}, u32[]{:S(2)}) copy-start(bf16[4,32,16,256]{3,2,1,0:T(8,128)(2,1)} %param.23) | copy-start | bytes 3145732
  7.2 386.0 %all-gather.7.cloned.1.call-start = ((), (), s32[]{:S(2)}) async-start(), calls=%async_computation.1 | async-start | bytes 1056768 | tf_op jit(solution)/shard_map/all_gather | solution.py:86
  77.8 8.1 copy-start.18
  78.0 7.9 copy-start.20
  80.8 11.4 %collective-permute-start = (bf16[4,1,16,256]{3,1,2,0:T(2,128)(2,1)}, bf16[4,1,16,256]{3,1,2,0:T(2,128)(2,1)}, u32[]{:S(2)}, u32[]{:S(2)}) collective-permute-start(bf16[4,1,16,256]{3,1,2,0:T(2,128)(2,1)} %get-tuple-element.38), channel_id=1, source_target_pairs={{0,8},{8,16},{16,24},{24,32},{32,40},{40,48},{48,56},{56,64},{64,7... | collective-permute-start | bytes 98312 | tf_op jit(solution)/shard_map/ppermute | solution.py:17
  82.9 9.3 collective-permute-start.1
  88.8 2.4 copy-start.8
  88.8 7.3 copy-start.6
  92.9 4.4 collective-permute-start.2
  94.7 7.1 collective-permute-start.3
  96.9 590.5 %all-gather.5.cloned.1.call-start = ((), (), s32[]{:S(2)}) async-start(), calls=%async_computation | async-start | bytes 1056768 | tf_op jit(solution)/shard_map/all_gather | solution.py:86
  117.7 74.1 %copy-start.23 = (f32[512]{0:T(512)S(1)}, f32[512]{0:T(512)}, u32[]{:S(2)}) copy-start(f32[512]{0:T(512)} %param.16) | copy-start | bytes 6148
  192.4 2.6 collective-permute-start.4
  193.7 3.1 collective-permute-start.5
  196.9 4.4 collective-permute-start.6
  199.4 6.2 collective-permute-start.7
  205.8 7.6 copy-start.5
  700.5 14.4 %copy-start.4 = (f32[4,32,8,512]{3,0,2,1:T(4,128)}, f32[4,32,8,512]{3,0,2,1:T(4,128)S(1)}, u32[]{:S(2)}) copy-start(f32[4,32,8,512]{3,0,2,1:T(4,128)S(1)} %subtract_multiply_fusion) | copy-start | bytes 6291460
  722.6 14.0 %collective-permute-start.8 = (bf16[4,1,4,512]{3,1,2,0:T(2,128)(2,1)S(1)}, bf16[4,1,4,512]{3,1,2,0:T(2,128)(2,1)S(1)}, u32[]{:S(2)}, u32[]{:S(2)}) collective-permute-start(bf16[4,1,4,512]{3,1,2,0:T(2,128)(2,1)S(1)} %get-tuple-element.44), channel_id=1, source_target_pairs={{0,8},{8,16},{16,24},{24,32},{32,40},{40,48},{48,56},{56,64},{64,7... | collective-permute-start | bytes 49160 | tf_op jit(solution)/shard_map/ppermute | solution.py:17
  724.7 22.6 %slice-start = ((s8[4718592]{0:T(1024)(128)(4,1)}), s8[4194304]{0:T(1024)(128)(4,1)S(1)}, s32[]{:S(2)}) async-start(s8[4718592]{0:T(1024)(128)(4,1)} %bitcast.106), calls=%async_computation.2 | async-start | bytes 8388608
  724.7 22.6 %slice-start.1 = ((s8[4718592]{0:T(1024)(128)(4,1)}), s8[524288]{0:T(1024)(128)(4,1)S(1)}, s32[]{:S(2)}) async-start(s8[4718592]{0:T(1024)(128)(4,1)} %bitcast.106), calls=%async_computation.3 | async-start | bytes 1048576
  724.7 11.9 %collective-permute-start.9 = (bf16[4,1,4,512]{3,1,2,0:T(2,128)(2,1)S(1)}, bf16[4,1,4,512]{3,1,2,0:T(2,128)(2,1)S(1)}, u32[]{:S(2)}, u32[]{:S(2)}) collective-permute-start(bf16[4,1,4,512]{3,1,2,0:T(2,128)(2,1)S(1)} %get-tuple-element.45), channel_id=1, source_target_pairs={{8,0},{16,8},{24,16},{32,24},{40,32},{48,40},{56,48},{64,56},{72,6... | collective-permute-start | bytes 49160 | tf_op jit(solution)/shard_map/ppermute | solution.py:20
  736.7 6.1 collective-permute-start.10
  740.5 6.6 collective-permute-start.11
  747.4 73.1 %copy-start.11 = (bf16[256,512]{1,0:T(8,128)(2,1)S(1)}, bf16[256,512]{1,0:T(8,128)(2,1)}, u32[]{:S(2)}) copy-start(bf16[256,512]{1,0:T(8,128)(2,1)} %param.15) | copy-start | bytes 786436
  825.5 6.0 copy-start.9
  825.5 6.0 copy-start.12
  828.6 7.9 collective-permute-start.12
  830.2 6.3 collective-permute-start.13
  836.6 6.5 collective-permute-start.14
  838.1 6.3 collective-permute-start.15
  (17 other events, 29.2 us)
Sparse Core Ops, SparseCore 0:
  97.1 296.1 all-gather.6
  394.9 292.4 all-gather.4
where the time goes:
time: 952 us; the launch traced here: 945 us
  waiting for transfers between devices  488 us (51%)
  blocking collectives  281 us (30%)
  local copies, waits for them, and re-layouts  47.7 us (5%)
  other arithmetic  44 us (5%)
  matrix products  41.6 us (4%)
  starting transfers between devices  28.2 us (3%)
  between operations  15.1 us (2%)
    all_gather x2, waiting for transfers between devices, coarse_whole(): lax.all_gather(tensor[None], ('wide', 'narrow'), axis=0, tiled=True)  470 us
    psum x2, blocking collectives, middle_total(): return lax.psum((partial_value[0], partial_value[1]), ('wide', 'narrow'))  141 us
    psum x2, blocking collectives, fine_total(): return lax.psum((partial_value[0], partial_value[1]), ('wide', 'narrow'))  140 us
    conv_general_dilated x6, matrix products, convolve(): lax.conv_general_dilated(padded, kernel, (1, 1), 'VALID', dimension_numbe...  37.7 us
  transfers between devices with their start and end apart: 18, of which 9 were waited for; matrix products, arithmetic and copies ran while one was open for 6% of the time, Pallas kernels for 0%

commit v1 on v0

v1 whole, which is shorter than its diff:
```python
import functools

import jax
import jax.numpy as jnp
import numpy as np
from jax import lax
from jax.experimental import pallas as pl
from jax.experimental.pallas import tpu as pltpu
from jax.sharding import PartitionSpec as P

MESH = pl.DeviceIdType.MESH
GROUPS = 32
epsilon = 1e-05
F32 = jnp.float32
BF16 = jnp.bfloat16

DIRS = ((0, 0), (-1, 0), (1, 0), (0, -1), (0, 1), (-1, -1), (-1, 1), (1, -1), (1, 1))

ABOVE, BELOW, LEFT, RIGHT, CORNER = 128, 144, 160, 192, 224


def mid_row(f, i, j):
    if 0 <= i < 8 and 0 <= j < 4:
        return 32 * f + 4 * i + j
    if i < 0 and 0 <= j < 4:
        return ABOVE + 4 * f + j
    if i > 7 and 0 <= j < 4:
        return BELOW + 4 * f + j
    if 0 <= i < 8:
        return (LEFT if j < 0 else RIGHT) + 8 * f + i
    return CORNER + 4 * (2 * (i > 7) + (j > 3)) + f


def coarse_row(f, i, side):
    down = -1 if i < 0 else (1 if i > 1 else 0)
    return 8 * DIRS.index((down, side)) + 2 * f + i % 2


def tables():
    pick = np.zeros((96, 512), np.float32)
    for i in range(32):
        for j in range(16):
            pick[4 * (i // 4) + j // 4, 16 * i + j] = 1
        pick[32 + i, 16 * i + 15] = 1
        pick[64 + i, 16 * i] = 1
    enlarge = np.zeros((912, 256), np.float32)
    taps = np.zeros((1152, 256), np.float32)
    ends = np.zeros((16, 256), np.float32)
    pack = np.zeros((112, 128), np.float32)
    pool = np.zeros((16, 128), np.float32)
    coarse_taps = np.zeros((144, 128), np.float32)
    spread = np.zeros((256, 128), np.float32)
    for f in range(4):
        for i in range(8):
            for j in range(16):
                enlarge[128 * f + 16 * i + j, mid_row(f, i, j // 4)] = 1
        for j in range(16):
            enlarge[512 + 16 * f + j, ABOVE + 4 * f + j // 4] = 1
            enlarge[576 + 16 * f + j, BELOW + 4 * f + j // 4] = 1
        for i in range(32):
            enlarge[640 + 32 * f + i, LEFT + 8 * f + i // 4] = 1
            enlarge[768 + 32 * f + i, RIGHT + 8 * f + i // 4] = 1
        for c in range(4):
            enlarge[896 + 4 * c + f, CORNER + 4 * c + f] = 1
            low, first = c < 2, c % 2 == 1
            ends[4 * c + f, 128 * first + 32 * f + 31 * low] = 1
            pack[96 + 4 * c + f, mid_row(f, 7 * low, 3 * (not first))] = 1
        for i in range(8):
            for j in range(4):
                here = 32 * f + 4 * i + j
                pool[2 * f + i // 4, here] = 1
                for t in range(9):
                    taps[128 * t + here, mid_row(f, i + t // 3 - 1, j + t % 3 - 1)] = 1
            pack[32 + 8 * f + i, mid_row(f, i, 3)] = 1
            pack[64 + 8 * f + i, mid_row(f, i, 0)] = 1
        for j in range(4):
            pack[4 * f + j, mid_row(f, 7, j)] = 1
            pack[16 + 4 * f + j, mid_row(f, 0, j)] = 1
        for i in range(2):
            for t in range(9):
                coarse_taps[16 * t + 2 * f + i, coarse_row(f, i + t // 3 - 1, t % 3 - 1)] = 1
        for i in range(-1, 9):
            for j in range(-1, 5):
                side = -1 if j < 0 else (1 if j > 3 else 0)
                spread[mid_row(f, i, j), coarse_row(f, i // 4 if i < 8 else 2, side)] = 1
    sides = np.zeros((512, 128), np.float32)
    for i in range(32):
        sides[16 * i, i] = 1
        sides[16 * i + 15, 64 + i] = 1
    wide_table = np.concatenate([pick, np.concatenate([enlarge, enlarge], axis=1)])
    middle_table = np.concatenate([taps, ends])
    narrow_table = np.concatenate([pack, pool, coarse_taps, spread, sides])
    return [jnp.asarray(t, BF16) for t in (wide_table, middle_table, narrow_table)]


def dot(a, b):
    return jnp.dot(a, b, preferred_element_type=F32)


def dot_t(a, b):
    return lax.dot_general(a, b, (((1,), (1,)), ((), ())), preferred_element_type=F32)


def group_lanes(t, size):
    lane = lax.broadcasted_iota(jnp.int32, t.shape, 1)
    step = 1
    while step < size:
        t = t + jnp.where(
            (lane & step) != 0, pltpu.roll(t, step, 1), pltpu.roll(t, 128 - step, 1)
        )
        step *= 2
    return t


def halves(t):
    high = t.astype(BF16)
    return high, (t - high.astype(F32)).astype(BF16)


def kernel(
    wide_count,
    narrow_count,
    x_in,
    gain_fine_in,
    kernel_fine_in,
    down_mid_in,
    gain_mid_in,
    kernel_mid_in,
    down_coarse_in,
    gain_coarse_in,
    kernel_coarse_in,
    up_coarse_in,
    up_mid_in,
    grad_in,
    wide_table_in,
    middle_table_in,
    narrow_table_in,
    out_ref,
    part_ref,
    tail_ref,
    xg,
    kernel_fine,
    flipped_fine,
    down_mid,
    kernel_mid,
    down_coarse,
    kernel_coarse,
    up_coarse,
    up_mid,
    gain_fine,
    gain_mid,
    gain_coarse,
    wide_table,
    middle_table,
    narrow_table,
    taps_buf,
    columns,
    fine_block,
    part,
    pooled,
    edge_rows,
    edge_sides,
    edge_ends,
    pool_grad,
    summed_grad,
    first,
    second,
    col_pack,
    cor_pack,
    row_in,
    col_in,
    cor_in,
    sum_pack,
    sum_in,
    sum_cor,
    cgrad_own,
    cgrad_in,
    mid_pack,
    mid_halo,
    mid_cor,
    coarse_own,
    coarse_halo,
    coarse_u,
    coarse_u_halo,
    u_pack,
    u_halo,
    u_cor,
    load_sem,
    out_sem,
    total_send,
    total_recv,
    halo_send,
    halo_recv,
):
    wide, narrow = lax.axis_index("wide"), lax.axis_index("narrow")

    def device(down, side):
        return (
            lax.rem(wide + down + wide_count, wide_count),
            lax.rem(narrow + side + narrow_count, narrow_count),
        )

    loads = {}
    pairs = (
        ("x", x_in, xg.at[0]),
        ("grad", grad_in, xg.at[1]),
        ("wide_table", wide_table_in, wide_table),
        ("middle_table", middle_table_in, middle_table),
        ("narrow_table", narrow_table_in, narrow_table),
        ("gain_fine", gain_fine_in, gain_fine),
        ("kernel_fine", kernel_fine_in, kernel_fine),
        ("up_mid", up_mid_in, up_mid),
        ("up_coarse", up_coarse_in, up_coarse),
        ("down_mid", down_mid_in, down_mid),
        ("gain_mid", gain_mid_in, gain_mid),
        ("kernel_coarse", kernel_coarse_in, kernel_coarse),
        ("kernel_mid", kernel_mid_in, kernel_mid),
        ("down_coarse", down_coarse_in, down_coarse),
        ("gain_coarse", gain_coarse_in, gain_coarse),
    )
    for number, (name, source, target) in enumerate(pairs):
        loads[name] = pltpu.make_async_copy(source, target, load_sem.at[number])
        loads[name].start()

    barrier = pltpu.get_barrier_semaphore()
    greeted = 0
    for down in range(wide_count):
        for side in range(-2, narrow_count - 2):
            near = (down <= 1 or down == wide_count - 1) and abs(side) <= 1
            if (down, side) != (0, 0) and (down == 0 or side == 0 or near):
                pl.semaphore_signal(
                    barrier, inc=1, device_id=device(down, side), device_id_type=MESH
                )
                greeted += 1

    def send(source, target, which, down, side):
        pltpu.make_async_remote_copy(
            src_ref=source,
            dst_ref=target,
            send_sem=halo_send.at[which],
            recv_sem=halo_recv.at[which],
            device_id=device(down, side),
            device_id_type=MESH,
        ).start()

    def arrived(buffer, which):
        pltpu.make_async_copy(buffer, buffer, halo_recv.at[which]).wait()

    def sent(buffer, which):
        pltpu.make_async_copy(buffer, buffer, halo_send.at[which]).wait()

    def total_begin(phase, one, two):
        blank = jnp.zeros((8, 128), F32)
        first[phase, wide] = blank
        for k in range(one.shape[1] // 128):
            first[phase, wide, k : k + 1, :] = one[:, 128 * k : 128 * k + 128]
            first[phase, wide, 4 + k : 5 + k, :] = two[:, 128 * k : 128 * k + 128]
        for step in range(1, wide_count):
            pltpu.make_async_remote_copy(
                src_ref=first.at[phase, wide],
                dst_ref=first.at[phase, wide],
                send_sem=total_send.at[2 * phase],
                recv_sem=total_recv.at[2 * phase],
                device_id=device(step, 0),
                device_id_type=MESH,
            ).start()

    def total_middle(phase):
        whole = first.at[phase, pl.ds(0, wide_count - 1)]
        pltpu.make_async_copy(whole, whole, total_recv.at[2 * phase]).wait()
        second[phase, narrow] = jnp.sum(first[phase], axis=0)
        for step in range(1, narrow_count):
            pltpu.make_async_remote_copy(
                src_ref=second.at[phase, narrow],
                dst_ref=second.at[phase, narrow],
                send_sem=total_send.at[2 * phase + 1],
                recv_sem=total_recv.at[2 * phase + 1],
                device_id=device(0, step),
                device_id_type=MESH,
            ).start()

    def total_end(phase, channels, cells):
        whole = second.at[phase, pl.ds(0, narrow_count - 1)]
        pltpu.make_async_copy(whole, whole, total_recv.at[2 * phase + 1]).wait()
        size = channels // GROUPS
        t = group_lanes(jnp.sum(second[phase], axis=0), size) * (1.0 / (size * cells))
        count = channels // 128
        return (
            jnp.concatenate([t[k : k + 1] for k in range(count)], axis=1),
            jnp.concatenate([t[4 + k : 5 + k] for k in range(count)], axis=1),
        )

    has_above, has_below = wide > 0, wide < wide_count - 1
    has_left, has_right = narrow > 0, narrow < narrow_count - 1
    has_corner = (
        jnp.logical_and(has_above, has_left),
        jnp.logical_and(has_above, has_right),
        jnp.logical_and(has_below, has_left),
        jnp.logical_and(has_below, has_right),
    )
    exists = (None, has_above, has_below, has_left, has_right) + has_corner

    def only(condition, value):
        return value * jnp.where(condition, 1.0, 0.0).astype(F32)

    def corners(read, change, masked):
        result = None
        for c in range(4):
            value = change(read(c).astype(F32))
            if masked:
                value = only(has_corner[c], value)
            quarter = lax.broadcasted_iota(jnp.int32, value.shape, 0) // 4
            result = value if result is None else jnp.where(quarter == c, value, result)
        return result

    def mid_extended(own, read_halo, read_cor, change, masked):
        pieces = [change(own)]
        halo = change(read_halo.astype(F32))
        for low, high, d in ((0, 16, 1), (16, 32, 2), (32, 64, 3), (64, 96, 4)):
            piece = halo[low:high]
            pieces.append(only(exists[d], piece) if masked else piece)
        pieces.append(corners(read_cor, change, masked))
        pieces.append(jnp.zeros((16, own.shape[1]), F32))
        return jnp.concatenate(pieces, axis=0)

    def send_mid(pack, halo, cor, which):
        send(pack.at[pl.ds(0, 16)], halo.at[pl.ds(0, 16)], which, 1, 0)
        send(pack.at[pl.ds(16, 16)], halo.at[pl.ds(16, 16)], which, -1, 0)
        send(pack.at[pl.ds(32, 32)], halo.at[pl.ds(32, 32)], which, 0, 1)
        send(pack.at[pl.ds(64, 32)], halo.at[pl.ds(64, 32)], which, 0, -1)
        for c in range(4):
            down, side = DIRS[5 + c]
            send(pack.at[pl.ds(96, 16)], cor.at[c], which + 1, -down, -side)

    def send_coarse(own, halo, which):
        for d in range(1, 9):
            down, side = DIRS[d]
            send(own, halo.at[d - 1], which, -down, -side)

    def coarse_extended(own, halo, change, masked):
        pieces = [change(own)]
        for d in range(1, 9):
            piece = change(halo(d - 1))
            pieces.append(only(exists[d], piece) if masked else piece)
        pieces.append(jnp.zeros((56, own.shape[1]), F32))
        return jnp.concatenate(pieces, axis=0)

    PICK = wide_table.at[pl.ds(0, 96)]
    ENLARGE = wide_table.at[pl.ds(96, 912)]
    TAPS = middle_table.at[pl.ds(0, 1152)]
    ENDS = middle_table.at[pl.ds(1152, 16)]
    PACK = narrow_table.at[pl.ds(0, 112)]
    POOL = narrow_table.at[pl.ds(112, 16)]
    COARSE_TAPS = narrow_table.at[pl.ds(128, 144)]
    SPREAD = narrow_table.at[pl.ds(272, 256)]
    SIDES = narrow_table.at[pl.ds(528, 512)]

    def frame(which, f):
        return xg[which, f].reshape(512, 256)

    loads["x"].wait()

    def add_frame(f, carry):
        value = frame(0, f).astype(F32)
        return (
            carry[0] + jnp.sum(value.reshape(64, 8, 256), axis=0),
            carry[1] + jnp.sum((value * value).reshape(64, 8, 256), axis=0),
        )

    blank = jnp.zeros((8, 256), F32)
    one, two = lax.fori_loop(0, 4, add_frame, (blank, blank))
    pl.semaphore_wait(barrier, greeted)
    total_begin(0, jnp.sum(one, axis=0, keepdims=True), jnp.sum(two, axis=0, keepdims=True))

    loads["grad"].wait()
    send(xg.at[:, :, 31], row_in.at[0], 0, 1, 0)
    send(xg.at[:, :, 0], row_in.at[1], 0, -1, 0)
    loads["wide_table"].wait()
    for which in range(2):
        for f in range(4):
            picked = dot(PICK[...], frame(which, f)).astype(BF16)
            col_pack[0, which, 32 * f : 32 * f + 32] = picked[32:64]
            col_pack[1, which, 32 * f : 32 * f + 32] = picked[64:96]
            if which == 1:
                pooled[32 * f : 32 * f + 32] = picked[0:32]
    send(col_pack.at[0], col_in.at[0], 1, 0, 1)
    send(col_pack.at[1], col_in.at[1], 1, 0, -1)
    loads["middle_table"].wait()
    for which in range(2):
        ends = jnp.concatenate([col_pack[0, which], col_pack[1, which]], axis=0)
        cor_pack[which] = dot(ENDS[...], ends).astype(BF16)
    for c in range(4):
        down, side = DIRS[5 + c]
        send(cor_pack, cor_in.at[c], 2, -down, -side)
    total_middle(0)

    loads["narrow_table"].wait()
    up_mid_grad = pooled[...]
    sum_pack[...] = dot(PACK[...], up_mid_grad).astype(BF16)
    send_mid(sum_pack, sum_in, sum_cor, 3)
    loads["up_mid"].wait()
    mid_sum_grad = dot_t(up_mid_grad, up_mid[...])
    high, low = halves(mid_sum_grad)
    up_coarse_grad = (dot(POOL[...], high) + dot(POOL[...], low)).astype(BF16)
    loads["up_coarse"].wait()
    cgrad_own[...] = dot_t(up_coarse_grad, up_coarse[...]).astype(BF16)
    send_coarse(cgrad_own, cgrad_in, 5)
    loads["gain_fine"].wait()
    loads["kernel_fine"].wait()
    for a in range(3):
        for b in range(3):
            flipped_fine[a, 256 * b : 256 * b + 256, :] = kernel_fine[
                2 - a, 256 * (2 - b) : 256 * (2 - b) + 256, :
            ].T

    fine_center, fine_square = total_end(0, 256, 2048 * wide_count * narrow_count)
    fine_inverse = lax.rsqrt(fine_square - fine_center * fine_center + epsilon)
    s_fine = gain_fine[...]

    def silu(value, center, inverse, scaling):
        normed = (value - center) * inverse * scaling
        return normed / (1.0 + jnp.exp(-normed))

    def fine_act(value):
        return silu(value, fine_center, fine_inverse, s_fine)

    arrived(row_in, 0)
    arrived(col_in, 1)
    arrived(cor_in, 2)

    def set_edges(above, below, left, right, ends):
        edge_rows[0] = only(has_above, above)
        edge_rows[1] = only(has_below, below)
        left = only(has_left, left).astype(BF16)
        right = only(has_right, right).astype(BF16)
        for f in range(4):
            edge_sides[f, 0:32] = left[32 * f : 32 * f + 32]
            edge_sides[f, 32:64] = right[32 * f : 32 * f + 32]
        edge_ends[...] = ends

    def place(f, own):
        column = lax.broadcasted_iota(jnp.int32, (512, 256), 0) % 16
        sides = edge_sides[f]
        low = jnp.where(
            column == 0, dot(SIDES[:, 0:64], sides), pltpu.roll(own, 1, 0)
        )
        columns[f, 16:528, 0:256] = low.astype(BF16)
        columns[f, 16:528, 256:512] = own.astype(BF16)
        high = jnp.where(
            column == 15, dot(SIDES[:, 32:96], sides), pltpu.roll(own, 511, 0)
        )
        columns[f, 16:528, 512:768] = high.astype(BF16)
        cell = lax.broadcasted_iota(jnp.int32, (16, 256), 0)
        for k in range(2):
            row = edge_rows[k, f]
            at = slice(528 * k, 528 * k + 16)
            west = edge_ends[pl.ds(8 * k + f, 1), :]
            east = edge_ends[pl.ds(8 * k + 4 + f, 1), :]
            columns[f, at, 0:256] = jnp.where(cell == 0, west, pltpu.roll(row, 1, 0)).astype(BF16)
            columns[f, at, 256:512] = row.astype(BF16)
            columns[f, at, 512:768] = jnp.where(cell == 15, east, pltpu.roll(row, 15, 0)).astype(BF16)

    def fine_convolve(f, weights):
        total = dot(columns[f, 0:512, :], weights[0])
        total += dot(columns[f, 16:528, :], weights[1])
        return total + dot(columns[f, 32:544, :], weights[2])

    set_edges(
        fine_act(row_in[0, 0].astype(F32)),
        fine_act(row_in[1, 0].astype(F32)),
        fine_act(col_in[0, 0].astype(F32)),
        fine_act(col_in[1, 0].astype(F32)),
        corners(lambda c: cor_in[c, 0], fine_act, True),
    )

    def fine_forward(f, carry):
        value = frame(0, f).astype(F32)
        place(f, fine_act(value))
        block = (value + fine_convolve(f, kernel_fine)).astype(BF16)
        fine_block[f] = block
        pooled[pl.ds(pl.multiple_of(32 * f, 32), 32), :] = (
            dot(PICK[0:32, :], block) * 0.0625
        ).astype(BF16)
        return carry

    lax.fori_loop(0, 4, fine_forward, 0)

    loads["down_mid"].wait()
    mid_in = dot(pooled[...], down_mid[...]).astype(BF16)
    mid_value = mid_in.astype(F32)

    def column_sums(value):
        return jnp.sum(value, axis=0, keepdims=True)

    total_begin(1, column_sums(mid_value), column_sums(mid_value * mid_value))
    mid_pack[...] = dot(PACK[...], mid_in).astype(BF16)
    send_mid(mid_pack, mid_halo, mid_cor, 6)
    total_middle(1)

    arrived(cgrad_in, 5)
    loads["kernel_coarse"].wait()

    def coarse_convolve(extended, weights):
        spread_out = dot(COARSE_TAPS[...], extended.astype(BF16)).astype(BF16)
        total = None
        for t in range(9):
            term = weights(t, spread_out[16 * t : 16 * t + 16])
            total = term if total is None else total + term
        return total

    def same(value):
        return value

    cgrad = cgrad_own[...].astype(F32)[0:8]
    coarse_act_grad = coarse_convolve(
        coarse_extended(cgrad, lambda d: cgrad_in[d].astype(F32)[0:8], same, True),
        lambda t, part_: dot_t(part_, kernel_coarse[8 - t]),
    )[0:8]

    loads["gain_mid"].wait()
    loads["kernel_mid"].wait()
    mid_center, mid_square = total_end(1, 512, 128 * wide_count * narrow_count)
    mid_inverse = lax.rsqrt(mid_square - mid_center * mid_center + epsilon)
    s_mid = gain_mid[...]

    def mid_act(value):
        return silu(value, mid_center, mid_inverse, s_mid)

    def mid_scaled(value):
        return (value - mid_center) * mid_inverse

    def mid_convolve(extended, weights):
        taps_buf[...] = dot(TAPS[...], extended.astype(BF16)).astype(BF16)
        total = None
        for t in range(9):
            term = weights(t, taps_buf[128 * t : 128 * t + 128, :])
            total = term if total is None else total + term
        return total

    arrived(mid_halo, 6)
    arrived(mid_cor, 7)
    mid_block = (
        mid_value
        + mid_convolve(
            mid_extended(mid_value, mid_halo[...], lambda c: mid_cor[c], mid_act, True),
            lambda t, part_: dot(part_, kernel_mid[t]),
        )
    ).astype(BF16)

    loads["down_coarse"].wait()
    mid_pooled = (dot(POOL[...], mid_block) * 0.0625).astype(BF16)
    coarse_in = dot(mid_pooled, down_coarse[...]).astype(BF16)
    coarse_own[...] = coarse_in
    coarse_value = coarse_in.astype(F32)[0:8]
    total_begin(2, column_sums(coarse_value), column_sums(coarse_value * coarse_value))
    send_coarse(coarse_own, coarse_halo, 8)
    total_middle(2)

    arrived(sum_in, 3)
    arrived(sum_cor, 4)
    sum_extended = mid_extended(
        up_mid_grad.astype(F32), sum_in[...], lambda c: sum_cor[c], same, True
    )
    summed_grad[...] = dot_t(sum_extended.astype(BF16), up_mid[...])

    loads["gain_coarse"].wait()
    coarse_center, coarse_square = total_end(2, 512, 8 * wide_count * narrow_count)
    coarse_inverse = lax.rsqrt(coarse_square - coarse_center * coarse_center + epsilon)
    s_coarse = gain_coarse[...]

    def coarse_scaled(value):
        return (value - coarse_center) * coarse_inverse

    def slope(scaled, scaling):
        normed = scaled * scaling
        logistic = 1.0 / (1.0 + jnp.exp(-normed))
        return logistic * (1.0 + normed * (1.0 - logistic)) * scaling

    scaled = coarse_scaled(coarse_value)
    normed_grad = coarse_act_grad * slope(scaled, s_coarse)
    total_begin(3, column_sums(normed_grad), column_sums(normed_grad * scaled))
    coarse_u[...] = cgrad + coarse_inverse * normed_grad
    send_coarse(coarse_u, coarse_u_halo, 9)
    total_middle(3)

    arrived(coarse_halo, 8)
    coarse_block = (
        coarse_in.astype(F32)
        + coarse_convolve(
            coarse_extended(
                coarse_value,
                lambda d: coarse_halo[d].astype(F32)[0:8],
                lambda v: silu(v, coarse_center, coarse_inverse, s_coarse),
                True,
            ),
            lambda t, part_: dot(part_, kernel_coarse[t]),
        )
    ).astype(BF16)
    coarse_up = dot(coarse_block, up_coarse[...]).astype(BF16)
    mid_sum = (mid_block.astype(F32) + dot(SPREAD[0:128, 0:16], coarse_up)).astype(BF16)
    mid_up = dot(mid_sum, up_mid[...]).astype(BF16)

    first_mean, second_mean = total_end(3, 512, 8 * wide_count * narrow_count)
    arrived(coarse_u_halo, 9)
    offset = coarse_inverse * first_mean
    factor = coarse_inverse * second_mean
    pieces = [coarse_u[...] - offset - scaled * factor]
    for d in range(8):
        piece = coarse_scaled(coarse_halo[d].astype(F32)[0:8])
        pieces.append(coarse_u_halo[d] - offset - piece * factor)
    pieces.append(jnp.zeros((56, 512), F32))
    coarse_in_grad = jnp.concatenate(pieces, axis=0).astype(BF16)

    mid_pool_grad = dot_t(dot(SPREAD[...], coarse_in_grad).astype(BF16), down_coarse[...])
    row = lax.broadcasted_iota(jnp.int32, (256, 512), 0)
    keep = jnp.where(row < ABOVE, 1.0, 0.0)
    bounds = ((ABOVE, 16, 1), (BELOW, 16, 2), (LEFT, 32, 3), (RIGHT, 32, 4)) + tuple(
        (CORNER + 4 * c, 4, 5 + c) for c in range(4)
    )
    for start, size, d in bounds:
        inside = jnp.logical_and(row >= start, row < start + size)
        keep = jnp.where(inside, jnp.where(exists[d], 1.0, 0.0).astype(F32), keep)
    mid_grad = (summed_grad[...] + 0.0625 * mid_pool_grad) * keep
    mid_act_grad = mid_convolve(mid_grad, lambda t, part_: dot_t(part_, kernel_mid[8 - t]))
    scaled = mid_scaled(mid_value)
    normed_grad = mid_act_grad * slope(scaled, s_mid)
    total_begin(4, column_sums(normed_grad), column_sums(normed_grad * scaled))
    mid_u = mid_grad[0:128].astype(BF16).astype(F32) + mid_inverse * normed_grad
    u_pack[...] = dot(PACK[...], mid_u.astype(BF16)).astype(BF16)
    send_mid(u_pack, u_halo, u_cor, 10)
    total_middle(4)

    mid_up = dot(ENLARGE[0:512, 0:128], mid_up).reshape(4, 8, 1, 16, 256)
    for f in range(4):
        block = fine_block[f].astype(F32).reshape(8, 4, 16, 256)
        fine_block[f] = (block + mid_up[f]).astype(BF16).reshape(512, 256)
    out_copy = pltpu.make_async_copy(fine_block, out_ref, out_sem.at[0])
    out_copy.start()

    first_mean, second_mean = total_end(4, 512, 128 * wide_count * narrow_count)
    arrived(u_halo, 10)
    arrived(u_cor, 11)
    offset = mid_inverse * first_mean
    factor = mid_inverse * second_mean
    mid_in_grad = mid_extended(
        mid_u, u_halo[...], lambda c: u_cor[c], lambda v: v - offset, False
    ) - factor * mid_extended(
        mid_value, mid_halo[...], lambda c: mid_cor[c], mid_scaled, False
    )

    high, low = halves(0.0625 * dot_t(mid_in_grad.astype(BF16), down_mid[...]))
    pool_grad[...] = dot(ENLARGE[...], jnp.concatenate([high, low], axis=0))

    def rounded(value):
        return value.astype(BF16).astype(F32)

    set_edges(
        rounded(row_in[0, 1].astype(F32) + pool_grad[512:576, :].reshape(4, 16, 256)),
        rounded(row_in[1, 1].astype(F32) + pool_grad[576:640, :].reshape(4, 16, 256)),
        rounded(col_in[0, 1].astype(F32) + pool_grad[640:768, :]),
        rounded(col_in[1, 1].astype(F32) + pool_grad[768:896, :]),
        corners(lambda c: cor_in[c, 1], lambda v: v + pool_grad[896:912, :], True),
    )

    def fine_backward(f, carry):
        added = pool_grad[pl.ds(pl.multiple_of(128 * f, 128), 128), :].reshape(8, 1, 16, 256)
        grad = xg[1, f].astype(F32).reshape(8, 4, 16, 256) + added
        grad = rounded(grad.reshape(512, 256))
        place(f, grad)
        act_grad = fine_convolve(f, flipped_fine)
        scaled = (frame(0, f).astype(F32) - fine_center) * fine_inverse
        normed_grad = act_grad * slope(scaled, s_fine)
        part[f] = grad + fine_inverse * normed_grad
        return (
            carry[0] + jnp.sum(normed_grad.reshape(64, 8, 256), axis=0),
            carry[1] + jnp.sum((normed_grad * scaled).reshape(64, 8, 256), axis=0),
        )

    one, two = lax.fori_loop(0, 4, fine_backward, (blank, blank))
    total_begin(5, jnp.sum(one, axis=0, keepdims=True), jnp.sum(two, axis=0, keepdims=True))
    part_copy = pltpu.make_async_copy(part, part_ref, out_sem.at[1])
    part_copy.start()
    total_middle(5)

    sent(row_in, 0)
    sent(col_in, 1)
    sent(cor_in, 2)
    sent(sum_in, 3)
    sent(sum_cor, 4)
    sent(cgrad_in, 5)
    sent(mid_halo, 6)
    sent(mid_cor, 7)
    sent(coarse_halo, 8)
    sent(coarse_u_halo, 9)
    sent(u_halo, 10)
    sent(u_cor, 11)
    for phase in range(6):
        whole = first.at[phase, pl.ds(0, wide_count - 1)]
        pltpu.make_async_copy(whole, whole, total_send.at[2 * phase]).wait()
    first_mean, second_mean = total_end(5, 256, 2048 * wide_count * narrow_count)
    for phase in range(6):
        whole = second.at[phase, pl.ds(0, narrow_count - 1)]
        pltpu.make_async_copy(whole, whole, total_send.at[2 * phase + 1]).wait()
    slant = -fine_inverse * fine_inverse * second_mean
    tail_ref[...] = jnp.zeros((8, 256), F32)
    tail_ref[0:1, :] = -fine_inverse * first_mean - fine_center * slant
    tail_ref[1:2, :] = slant
    out_copy.wait()
    part_copy.wait()


def shards(*arguments):
    (
        fine_input,
        gain_fine,
        kernel_fine,
        down_mid,
        gain_mid,
        kernel_mid,
        down_coarse,
        gain_coarse,
        kernel_coarse,
        up_coarse,
        up_mid,
        grad_out,
    ) = arguments
    wide_count, narrow_count = lax.axis_size("wide"), lax.axis_size("narrow")
    anywhere = pl.BlockSpec(memory_space=pl.ANY)
    vmem = pltpu.VMEM
    scratch = [
        vmem((2, 4, 32, 16, 256), BF16),
        vmem((3, 768, 256), BF16),
        vmem((3, 768, 256), BF16),
        vmem((256, 512), BF16),
        vmem((9, 512, 512), BF16),
        vmem((512, 512), BF16),
        vmem((9, 512, 512), BF16),
        vmem((512, 512), BF16),
        vmem((512, 256), BF16),
        vmem((1, 256), F32),
        vmem((1, 512), F32),
        vmem((1, 512), F32),
        vmem((1008, 512), BF16),
        vmem((1168, 256), BF16),
        vmem((1040, 128), BF16),
        vmem((1152, 512), BF16),
        vmem((4, 544, 768), BF16),
        vmem((4, 512, 256), BF16),
        vmem((4, 512, 256), F32),
        vmem((128, 256), BF16),
        vmem((2, 4, 16, 256), F32),
        vmem((4, 64, 256), BF16),
        vmem((16, 256), F32),
        vmem((912, 256), F32),
        vmem((256, 512), F32),
        vmem((6, wide_count, 8, 128), F32),
        vmem((6, narrow_count, 8, 128), F32),
        vmem((2, 2, 128, 256), BF16),
        vmem((2, 16, 256), BF16),
        vmem((2, 2, 4, 16, 256), BF16),
        vmem((2, 2, 128, 256), BF16),
        vmem((4, 2, 16, 256), BF16),
        vmem((112, 256), BF16),
        vmem((96, 256), BF16),
        vmem((4, 16, 256), BF16),
        vmem((16, 512), BF16),
        vmem((8, 16, 512), BF16),
        vmem((112, 512), BF16),
        vmem((96, 512), BF16),
        vmem((4, 16, 512), BF16),
        vmem((16, 512), BF16),
        vmem((8, 16, 512), BF16),
        vmem((8, 512), F32),
        vmem((8, 8, 512), F32),
        vmem((112, 512), BF16),
        vmem((96, 512), BF16),
        vmem((4, 16, 512), BF16),
        pltpu.SemaphoreType.DMA((15,)),
        pltpu.SemaphoreType.DMA((2,)),
        pltpu.SemaphoreType.DMA((12,)),
        pltpu.SemaphoreType.DMA((12,)),
        pltpu.SemaphoreType.DMA((12,)),
        pltpu.SemaphoreType.DMA((12,)),
    ]
    output, part, tail = pl.pallas_call(
        functools.partial(kernel, wide_count, narrow_count),
        out_shape=(
            jax.ShapeDtypeStruct((4, 512, 256), BF16),
            jax.ShapeDtypeStruct((4, 512, 256), F32),
            jax.ShapeDtypeStruct((8, 256), F32),
        ),
        in_specs=[anywhere] * 15,
        out_specs=(anywhere, anywhere, pl.BlockSpec(memory_space=pltpu.VMEM)),
        scratch_shapes=scratch,
        compiler_params=pltpu.CompilerParams(
            collective_id=0, has_side_effects=True, vmem_limit_bytes=56 * 2**20
        ),
        name="whole_net",
    )(
        fine_input,
        gain_fine.reshape(1, 256),
        kernel_fine.reshape(3, 768, 256),
        down_mid,
        gain_mid.reshape(1, 512),
        kernel_mid.reshape(9, 512, 512),
        down_coarse,
        gain_coarse.reshape(1, 512),
        kernel_coarse.reshape(9, 512, 512),
        up_coarse,
        up_mid,
        grad_out,
        *tables(),
    )
    grad = part.reshape(4, 32, 16, 256) + (tail[0] + fine_input.astype(F32) * tail[1])
    return output.reshape(4, 32, 16, 256), grad


def solution(mesh):
    tile = P(None, "wide", "narrow", None)
    return jax.shard_map(
        shards,
        mesh=mesh,
        in_specs=(tile,) + (P(),) * 10 + (tile,),
        out_specs=(tile, tile),
        check_vma=False,
    )
```

time: 952 us -> 85.8 us (0.09)
  waiting for transfers between devices: 488 us -> 0 us
  blocking collectives: 281 us -> 0 us
  Pallas kernels: 0 us -> 79.6 us
  local copies, waits for them, and re-layouts: 47.7 us -> 1.75 us
  matrix products: 41.6 us -> 0 us
  other arithmetic: 44 us -> 3.43 us
  starting transfers between devices: 28.2 us -> 0 us
  between operations: 15.1 us -> 0.65 us
    all_gather x2 -> x0, waiting for transfers between devices: 470 us -> none  [coarse_whole(): lax.all_gather(tensor[None], ('wide', 'narrow'), axis=0, tiled=True)]
    psum x4 -> x0, blocking collectives: 281 us -> none  [the longest x2 141 us: middle_total(): return lax.psum((partial_value[0], partial_value[1]), ('wide', 'narrow'))]
    pallas_call x0 -> x1, Pallas kernels: none -> 79.6 us  [shards(): pl.pallas_call(functools.partial(kernel, wide_count, narrow_count), out_s...]
    conv_general_dilated x6 -> x0, matrix products: 37.7 us -> none  [convolve(): lax.conv_general_dilated(padded, kernel, (1, 1), 'VALID', dimension_numbe...]
    ppermute x16 -> x0, starting transfers between devices: 28 us -> none  [the longest x8 16.8 us: with_halo(): lax.ppermute(lax.slice_in_dim(block, block.shape[dim] - width, None, axis...]
    reduce_sum x21 -> x0, other arithmetic: 18.9 us -> none  [the longest x4 8.16 us: group_sums(): per_channel = jnp.sum(values, axis=(0, 1, 2))]
    ppermute x16 -> x0, waiting for transfers between devices: 17.1 us -> none  [the longest x8 16.3 us: with_halo(): lax.ppermute(lax.slice_in_dim(block, 0, width, axis=dim), axis, backward)]
    reshape x16 -> x0, local copies, waits for them, and re-layouts: 15.2 us -> none  [the longest x12 3.63 us: group_sums(): return jnp.sum(per_channel.reshape(GROUPS, -1), axis=1)]
  transfers between devices with their start and end apart: 18 -> 0, of which waited for: 9 -> 0; matrix products, arithmetic and copies ran while one was open for 6% -> 0% of each run, Pallas kernels for 0% -> 0%
where the time goes in v1:
time: 85.8 us; the launch traced here: 85.4 us
  Pallas kernels  79.6 us (93%)
  other arithmetic  3.43 us (4%)
  local copies, waits for them, and re-layouts  1.75 us (2%)
    pallas_call x1, Pallas kernels, shards(): pl.pallas_call(functools.partial(kernel, wide_count, narrow_count), out_s...  79.6 us
    add x1, other arithmetic, shards(): part.reshape(4, 32, 16, 256) + (tail[0] + fine_input.astype(F32) * tail[1])  3.43 us

profile of v1, /device:TPU:0, one launch (start us, length us, event | category | flops | bytes accessed | tf_op | source)
XLA Modules:
  0.0 85.4 jit_solution(708712469505312016)
XLA Ops:
  0.6 0.0 copy-start
  0.6 79.6 %whole_net.1 = (bf16[4,512,256]{2,1,0:T(8,128)(2,1)}, f32[4,512,256]{2,1,0:T(8,128)}, f32[8,256]{1,0:T(8,128)}) custom-call(bf16[4,32,16,256]{3,2,1,0:T(8,128)(2,1)} %x_in.1, f32[1,256]{1,0:T(1,128)} %bitcast.19, bf16[3,768,256]{2,1,0:T(8,128)(2,1)} %bitcast.13, bf16[256,512]{1,0:T(8,128)(2,1)} %down_mid_in.1, f32[1,512]{1,0:T(1,128)} %bitcast.17, ...), custom_call_target="tpu_custom_call" | custom-call | tf_op jit(solution)/shard_map/whole_net/pallas_call | solution.py:785
  80.3 0.8 fusion
  81.0 0.0 copy-done
  81.0 0.0 copy-start.1
  81.0 3.4 %add_add_fusion = f32[4,32,16,256]{3,2,1,0:T(8,128)} fusion(f32[4,32,16,256]{3,2,1,0:T(8,128)} %bitcast.12, bf16[4,32,16,256]{3,2,1,0:T(8,128)(2,1)S(1)} %copy-done, f32[256]{0:T(256)S(1)} %bitcast.16, f32[256]{0:T(256)S(1)} %bitcast.15), kind=kLoop, calls=%fused_computation | loop fusion | flops 2097152 | bytes 5244928 | tf_op jit(solution)/shard_map/add | solution.py:814
  84.5 0.0 copy-done.1
  84.5 1.0 %copy.18 = bf16[4,32,16,256]{3,2,1,0:T(8,128)(2,1)} copy(bf16[4,32,16,256]{3,2,1,0:T(8,128)(2,1)S(1)} %bitcast.14) | data formatting | bytes 2097152
Async XLA Ops:
  0.6 80.4 %copy-start = (bf16[4,32,16,256]{3,2,1,0:T(8,128)(2,1)S(1)}, bf16[4,32,16,256]{3,2,1,0:T(8,128)(2,1)}, u32[]{:S(2)}) copy-start(bf16[4,32,16,256]{3,2,1,0:T(8,128)(2,1)} %x_in.1) | copy-start | bytes 3145732
  81.0 3.4 %copy-start.1 = (bf16[4,512,256]{2,1,0:T(8,128)(2,1)S(1)}, bf16[4,512,256]{2,1,0:T(8,128)(2,1)}, u32[]{:S(2)}) copy-start(bf16[4,512,256]{2,1,0:T(8,128)(2,1)} %get-tuple-element.5) | copy-start | bytes 3145732

commit v2 on v1

--- a/solution.py
+++ b/solution.py
@@ -137,7 +137,8 @@
     narrow_table_in,
     out_ref,
     part_ref,
-    tail_ref,
+    shift_ref,
+    slant_ref,
     xg,
     kernel_fine,
     flipped_fine,
@@ -154,10 +155,13 @@
     middle_table,
     narrow_table,
     taps_buf,
+    coarse_taps,
     columns,
     fine_block,
     part,
     pooled,
+    summed,
+    fine_slope,
     edge_rows,
     edge_sides,
     edge_ends,
@@ -220,7 +224,7 @@
     )
     for number, (name, source, target) in enumerate(pairs):
         loads[name] = pltpu.make_async_copy(source, target, load_sem.at[number])
-        loads[name].start()
+    loads["x"].start()
 
     barrier = pltpu.get_barrier_semaphore()
     greeted = 0
@@ -255,7 +259,8 @@
         for k in range(one.shape[1] // 128):
             first[phase, wide, k : k + 1, :] = one[:, 128 * k : 128 * k + 128]
             first[phase, wide, 4 + k : 5 + k, :] = two[:, 128 * k : 128 * k + 128]
-        for step in range(1, wide_count):
+        @pl.loop(1, wide_count)
+        def _(step):
             pltpu.make_async_remote_copy(
                 src_ref=first.at[phase, wide],
                 dst_ref=first.at[phase, wide],
@@ -269,7 +274,8 @@
         whole = first.at[phase, pl.ds(0, wide_count - 1)]
         pltpu.make_async_copy(whole, whole, total_recv.at[2 * phase]).wait()
         second[phase, narrow] = jnp.sum(first[phase], axis=0)
-        for step in range(1, narrow_count):
+        @pl.loop(1, narrow_count)
+        def _(step):
             pltpu.make_async_remote_copy(
                 src_ref=second.at[phase, narrow],
                 dst_ref=second.at[phase, narrow],
@@ -359,6 +365,9 @@
         return xg[which, f].reshape(512, 256)
 
     loads["x"].wait()
+    for name in loads:
+        if name != "x":
+            loads[name].start()
 
     def add_frame(f, carry):
         value = frame(0, f).astype(F32)
@@ -372,46 +381,33 @@
     pl.semaphore_wait(barrier, greeted)
     total_begin(0, jnp.sum(one, axis=0, keepdims=True), jnp.sum(two, axis=0, keepdims=True))
 
-    loads["grad"].wait()
-    send(xg.at[:, :, 31], row_in.at[0], 0, 1, 0)
-    send(xg.at[:, :, 0], row_in.at[1], 0, -1, 0)
-    loads["wide_table"].wait()
-    for which in range(2):
+    def rim(which):
+        sem = 13 * which
+        send(xg.at[which, :, 31], row_in.at[0, which], sem, 1, 0)
+        send(xg.at[which, :, 0], row_in.at[1, which], sem, -1, 0)
         for f in range(4):
             picked = dot(PICK[...], frame(which, f)).astype(BF16)
             col_pack[0, which, 32 * f : 32 * f + 32] = picked[32:64]
             col_pack[1, which, 32 * f : 32 * f + 32] = picked[64:96]
             if which == 1:
-                pooled[32 * f : 32 * f + 32] = picked[0:32]
-    send(col_pack.at[0], col_in.at[0], 1, 0, 1)
-    send(col_pack.at[1], col_in.at[1], 1, 0, -1)
-    loads["middle_table"].wait()
-    for which in range(2):
+                summed[32 * f : 32 * f + 32] = picked[0:32]
+        send(col_pack.at[0, which], col_in.at[0, which], sem + 1, 0, 1)
+        send(col_pack.at[1, which], col_in.at[1, which], sem + 1, 0, -1)
         ends = jnp.concatenate([col_pack[0, which], col_pack[1, which]], axis=0)
         cor_pack[which] = dot(ENDS[...], ends).astype(BF16)
-    for c in range(4):
-        down, side = DIRS[5 + c]
-        send(cor_pack, cor_in.at[c], 2, -down, -side)
+        for c in range(4):
+            down, side = DIRS[5 + c]
+            send(cor_pack.at[which], cor_in.at[which, c], sem + 2, -down, -side)
+
+    loads["wide_table"].wait()
+    loads["middle_table"].wait()
+    rim(0)
     total_middle(0)
-
+    loads["grad"].wait()
+    rim(1)
     loads["narrow_table"].wait()
-    up_mid_grad = pooled[...]
-    sum_pack[...] = dot(PACK[...], up_mid_grad).astype(BF16)
-    send_mid(sum_pack, sum_in, sum_cor, 3)
-    loads["up_mid"].wait()
-    mid_sum_grad = dot_t(up_mid_grad, up_mid[...])
-    high, low = halves(mid_sum_grad)
-    up_coarse_grad = (dot(POOL[...], high) + dot(POOL[...], low)).astype(BF16)
-    loads["up_coarse"].wait()
-    cgrad_own[...] = dot_t(up_coarse_grad, up_coarse[...]).astype(BF16)
-    send_coarse(cgrad_own, cgrad_in, 5)
     loads["gain_fine"].wait()
     loads["kernel_fine"].wait()
-    for a in range(3):
-        for b in range(3):
-            flipped_fine[a, 256 * b : 256 * b + 256, :] = kernel_fine[
-                2 - a, 256 * (2 - b) : 256 * (2 - b) + 256, :
-            ].T
 
     fine_center, fine_square = total_end(0, 256, 2048 * wide_count * narrow_count)
     fine_inverse = lax.rsqrt(fine_square - fine_center * fine_center + epsilon)
@@ -421,12 +417,17 @@
         normed = (value - center) * inverse * scaling
         return normed / (1.0 + jnp.exp(-normed))
 
+    def slope(scaled, scaling):
+        normed = scaled * scaling
+        logistic = 1.0 / (1.0 + jnp.exp(-normed))
+        return logistic * (1.0 + normed * (1.0 - logistic)) * scaling
+
     def fine_act(value):
         return silu(value, fine_center, fine_inverse, s_fine)
 
-    arrived(row_in, 0)
-    arrived(col_in, 1)
-    arrived(cor_in, 2)
+    arrived(row_in.at[:, 0], 0)
+    arrived(col_in.at[:, 0], 1)
+    arrived(cor_in.at[0], 2)
 
     def set_edges(above, below, left, right, ends):
         edge_rows[0] = only(has_above, above)
@@ -470,20 +471,21 @@
         fine_act(row_in[1, 0].astype(F32)),
         fine_act(col_in[0, 0].astype(F32)),
         fine_act(col_in[1, 0].astype(F32)),
-        corners(lambda c: cor_in[c, 0], fine_act, True),
+        corners(lambda c: cor_in[0, c], fine_act, True),
     )
 
-    def fine_forward(f, carry):
-        value = frame(0, f).astype(F32)
+    def fine_value(f):
+        return frame(0, f).astype(F32)
+
+    @pl.loop(0, 4)
+    def _(f):
+        value = fine_value(f)
         place(f, fine_act(value))
         block = (value + fine_convolve(f, kernel_fine)).astype(BF16)
         fine_block[f] = block
         pooled[pl.ds(pl.multiple_of(32 * f, 32), 32), :] = (
             dot(PICK[0:32, :], block) * 0.0625
         ).astype(BF16)
-        return carry
-
-    lax.fori_loop(0, 4, fine_forward, 0)
 
     loads["down_mid"].wait()
     mid_in = dot(pooled[...], down_mid[...]).astype(BF16)
@@ -495,27 +497,24 @@
     total_begin(1, column_sums(mid_value), column_sums(mid_value * mid_value))
     mid_pack[...] = dot(PACK[...], mid_in).astype(BF16)
     send_mid(mid_pack, mid_halo, mid_cor, 6)
+
+    up_mid_grad = summed[...]
+    sum_pack[...] = dot(PACK[...], up_mid_grad).astype(BF16)
+    send_mid(sum_pack, sum_in, sum_cor, 3)
+    loads["up_mid"].wait()
+    high, low = halves(dot_t(up_mid_grad, up_mid[...]))
+    up_coarse_grad = (dot(POOL[...], high) + dot(POOL[...], low)).astype(BF16)
+    loads["up_coarse"].wait()
+    cgrad_own[...] = dot_t(up_coarse_grad, up_coarse[...]).astype(BF16)
+    send_coarse(cgrad_own, cgrad_in, 5)
     total_middle(1)
 
-    arrived(cgrad_in, 5)
-    loads["kernel_coarse"].wait()
-
-    def coarse_convolve(extended, weights):
-        spread_out = dot(COARSE_TAPS[...], extended.astype(BF16)).astype(BF16)
-        total = None
-        for t in range(9):
-            term = weights(t, spread_out[16 * t : 16 * t + 16])
-            total = term if total is None else total + term
-        return total
-
-    def same(value):
-        return value
-
-    cgrad = cgrad_own[...].astype(F32)[0:8]
-    coarse_act_grad = coarse_convolve(
-        coarse_extended(cgrad, lambda d: cgrad_in[d].astype(F32)[0:8], same, True),
-        lambda t, part_: dot_t(part_, kernel_coarse[8 - t]),
-    )[0:8]
+    for a in range(3):
+        for b in range(3):
+            flipped_fine[a, 256 * b : 256 * b + 256, :] = kernel_fine[
+                2 - a, 256 * (2 - b) : 256 * (2 - b) + 256, :
+            ].T
+
 
     loads["gain_mid"].wait()
     loads["kernel_mid"].wait()
@@ -530,10 +529,10 @@
         return (value - mid_center) * mid_inverse
 
     def mid_convolve(extended, weights):
-        taps_buf[...] = dot(TAPS[...], extended.astype(BF16)).astype(BF16)
+        taps_buf[...] = dot(TAPS[...], extended.astype(BF16)).astype(BF16).reshape(9, 128, 512)
         total = None
         for t in range(9):
-            term = weights(t, taps_buf[128 * t : 128 * t + 128, :])
+            term = weights(t, taps_buf[t])
             total = term if total is None else total + term
         return total
 
@@ -556,6 +555,25 @@
     send_coarse(coarse_own, coarse_halo, 8)
     total_middle(2)
 
+    arrived(cgrad_in, 5)
+    loads["kernel_coarse"].wait()
+
+    def coarse_convolve(extended, weights):
+        spread_out = dot(COARSE_TAPS[...], extended.astype(BF16)).astype(BF16)
+        coarse_taps[...] = spread_out.reshape(9, 16, 512)
+        return lax.fori_loop(
+            0, 9, lambda t, total: total + weights(t, coarse_taps[t]), jnp.zeros((16, 512), F32)
+        )
+
+    def same(value):
+        return value
+
+    cgrad = cgrad_own[...].astype(F32)[0:8]
+    coarse_act_grad = coarse_convolve(
+        coarse_extended(cgrad, lambda d: cgrad_in[d].astype(F32)[0:8], same, True),
+        lambda t, part_: dot_t(part_, kernel_coarse[8 - t]),
+    )[0:8]
+
     arrived(sum_in, 3)
     arrived(sum_cor, 4)
     sum_extended = mid_extended(
@@ -570,11 +588,6 @@
 
     def coarse_scaled(value):
         return (value - coarse_center) * coarse_inverse
-
-    def slope(scaled, scaling):
-        normed = scaled * scaling
-        logistic = 1.0 / (1.0 + jnp.exp(-normed))
-        return logistic * (1.0 + normed * (1.0 - logistic)) * scaling
 
     scaled = coarse_scaled(coarse_value)
     normed_grad = coarse_act_grad * slope(scaled, s_coarse)
@@ -637,6 +650,17 @@
     out_copy = pltpu.make_async_copy(fine_block, out_ref, out_sem.at[0])
     out_copy.start()
 
+    def fine_scaled(f):
+        return (fine_value(f) - fine_center) * fine_inverse
+
+    @pl.loop(0, 4)
+    def _(f):
+        fine_slope[f] = slope(fine_scaled(f), s_fine)
+
+    arrived(row_in.at[:, 1], 13)
+    arrived(col_in.at[:, 1], 14)
+    arrived(cor_in.at[1], 15)
+
     first_mean, second_mean = total_end(4, 512, 128 * wide_count * narrow_count)
     arrived(u_halo, 10)
     arrived(u_cor, 11)
@@ -659,7 +683,7 @@
         rounded(row_in[1, 1].astype(F32) + pool_grad[576:640, :].reshape(4, 16, 256)),
         rounded(col_in[0, 1].astype(F32) + pool_grad[640:768, :]),
         rounded(col_in[1, 1].astype(F32) + pool_grad[768:896, :]),
-        corners(lambda c: cor_in[c, 1], lambda v: v + pool_grad[896:912, :], True),
+        corners(lambda c: cor_in[1, c], lambda v: v + pool_grad[896:912, :], True),
     )
 
     def fine_backward(f, carry):
@@ -667,13 +691,11 @@
         grad = xg[1, f].astype(F32).reshape(8, 4, 16, 256) + added
         grad = rounded(grad.reshape(512, 256))
         place(f, grad)
-        act_grad = fine_convolve(f, flipped_fine)
-        scaled = (frame(0, f).astype(F32) - fine_center) * fine_inverse
-        normed_grad = act_grad * slope(scaled, s_fine)
-        part[f] = grad + fine_inverse * normed_grad
+        normed_grad = fine_convolve(f, flipped_fine) * fine_slope[f]
+        part[f] = (grad + fine_inverse * normed_grad).astype(BF16)
         return (
             carry[0] + jnp.sum(normed_grad.reshape(64, 8, 256), axis=0),
-            carry[1] + jnp.sum((normed_grad * scaled).reshape(64, 8, 256), axis=0),
+            carry[1] + jnp.sum((normed_grad * fine_scaled(f)).reshape(64, 8, 256), axis=0),
         )
 
     one, two = lax.fori_loop(0, 4, fine_backward, (blank, blank))
@@ -682,9 +704,10 @@
     part_copy.start()
     total_middle(5)
 
-    sent(row_in, 0)
-    sent(col_in, 1)
-    sent(cor_in, 2)
+    for which in range(2):
+        sent(row_in.at[:, which], 13 * which)
+        sent(col_in.at[:, which], 13 * which + 1)
+        sent(cor_in.at[which], 13 * which + 2)
     sent(sum_in, 3)
     sent(sum_cor, 4)
     sent(cgrad_in, 5)
@@ -702,11 +725,15 @@
         whole = second.at[phase, pl.ds(0, narrow_count - 1)]
         pltpu.make_async_copy(whole, whole, total_send.at[2 * phase + 1]).wait()
     slant = -fine_inverse * fine_inverse * second_mean
-    tail_ref[...] = jnp.zeros((8, 256), F32)
-    tail_ref[0:1, :] = -fine_inverse * first_mean - fine_center * slant
-    tail_ref[1:2, :] = slant
+    shift_ref[...] = -fine_inverse * first_mean - fine_center * slant
+    slant_ref[...] = slant
     out_copy.wait()
     part_copy.wait()
+
+
+def finish(output_in, part, value, shift, slant, output, grad):
+    output[...] = output_in[...]
+    grad[0] = part[0].astype(F32) + (shift[...] + value[0].astype(F32) * slant[...])
 
 
 def shards(*arguments):
@@ -743,11 +770,14 @@
         vmem((1008, 512), BF16),
         vmem((1168, 256), BF16),
         vmem((1040, 128), BF16),
-        vmem((1152, 512), BF16),
+        vmem((9, 128, 512), BF16),
+        vmem((9, 16, 512), BF16),
         vmem((4, 544, 768), BF16),
         vmem((4, 512, 256), BF16),
+        vmem((4, 512, 256), BF16),
+        vmem((128, 256), BF16),
+        vmem((128, 256), BF16),
         vmem((4, 512, 256), F32),
-        vmem((128, 256), BF16),
         vmem((2, 4, 16, 256), F32),
         vmem((4, 64, 256), BF16),
         vmem((16, 256), F32),
@@ -759,7 +789,7 @@
         vmem((2, 16, 256), BF16),
         vmem((2, 2, 4, 16, 256), BF16),
         vmem((2, 2, 128, 256), BF16),
-        vmem((4, 2, 16, 256), BF16),
+        vmem((2, 4, 16, 256), BF16),
         vmem((112, 256), BF16),
         vmem((96, 256), BF16),
         vmem((4, 16, 256), BF16),
@@ -779,18 +809,19 @@
         pltpu.SemaphoreType.DMA((2,)),
         pltpu.SemaphoreType.DMA((12,)),
         pltpu.SemaphoreType.DMA((12,)),
-        pltpu.SemaphoreType.DMA((12,)),
-        pltpu.SemaphoreType.DMA((12,)),
+        pltpu.SemaphoreType.DMA((16,)),
+        pltpu.SemaphoreType.DMA((16,)),
     ]
-    output, part, tail = pl.pallas_call(
+    output, part, shift, slant = pl.pallas_call(
         functools.partial(kernel, wide_count, narrow_count),
         out_shape=(
             jax.ShapeDtypeStruct((4, 512, 256), BF16),
-            jax.ShapeDtypeStruct((4, 512, 256), F32),
-            jax.ShapeDtypeStruct((8, 256), F32),
+            jax.ShapeDtypeStruct((4, 512, 256), BF16),
+            jax.ShapeDtypeStruct((1, 256), F32),
+            jax.ShapeDtypeStruct((1, 256), F32),
         ),
         in_specs=[anywhere] * 15,
-        out_specs=(anywhere, anywhere, pl.BlockSpec(memory_space=pltpu.VMEM)),
+        out_specs=(anywhere, anywhere) + (pl.BlockSpec(memory_space=pltpu.VMEM),) * 2,
         scratch_shapes=scratch,
         compiler_params=pltpu.CompilerParams(
             collective_id=0, has_side_effects=True, vmem_limit_bytes=56 * 2**20
@@ -811,8 +842,20 @@
         grad_out,
         *tables(),
     )
-    grad = part.reshape(4, 32, 16, 256) + (tail[0] + fine_input.astype(F32) * tail[1])
-    return output.reshape(4, 32, 16, 256), grad
+    cells = pl.BlockSpec((1, 512, 256), lambda f: (f, 0, 0))
+    vector = pl.BlockSpec((1, 256), lambda f: (0, 0))
+    output, grad = pl.pallas_call(
+        finish,
+        grid=(4,),
+        out_shape=(
+            jax.ShapeDtypeStruct((4, 512, 256), BF16),
+            jax.ShapeDtypeStruct((4, 512, 256), F32),
+        ),
+        in_specs=[cells, cells, cells, vector, vector],
+        out_specs=(cells, cells),
+        name="finish",
+    )(output, part, fine_input.reshape(4, 512, 256), shift, slant)
+    return output.reshape(4, 32, 16, 256), grad.reshape(4, 32, 16, 256)
 
 
 def solution(mesh):

time: 85.8 us -> 83.9 us (0.978)
  other arithmetic: 3.43 us -> 0 us
  Pallas kernels: 79.6 us -> 82.9 us
  local copies, waits for them, and re-layouts: 1.75 us -> 0 us
    pallas_call x0 -> x1, Pallas kernels: none -> 4.09 us  [shards(): pl.pallas_call(finish, grid=(4,), out_shape=(jax.ShapeDtypeStruct((4, 512...]
    add x1 -> x0, other arithmetic: 3.43 us -> none  [shards(): part.reshape(4, 32, 16, 256) + (tail[0] + fine_input.astype(F32) * tail[1])]
    unnamed x5 -> x0, local copies, waits for them, and re-layouts: 0.98 us -> none
where the time goes in v2:
time: 83.9 us; the launch traced here: 83.5 us
  Pallas kernels  82.9 us (99%)
    pallas_call x1, Pallas kernels, shards(): pl.pallas_call(functools.partial(kernel, wide_count, narrow_count), out_s...  78.8 us
    pallas_call x1, Pallas kernels, shards(): pl.pallas_call(finish, grid=(4,), out_shape=(jax.ShapeDtypeStruct((4, 512...  4.09 us

profile of v2, /device:TPU:0, one launch (start us, length us, event | category | flops | bytes accessed | tf_op | source)
XLA Modules:
  0.0 83.5 jit_solution(13629423153902869253)
XLA Ops:
  0.6 78.8 %whole_net.1 = (bf16[4,512,256]{2,1,0:T(8,128)(2,1)}, bf16[4,512,256]{2,1,0:T(8,128)(2,1)}, f32[1,256]{1,0:T(1,128)}, f32[1,256]{1,0:T(1,128)}) custom-call(bf16[4,32,16,256]{3,2,1,0:T(8,128)(2,1)} %x_in.1, f32[1,256]{1,0:T(1,128)} %bitcast.15, bf16[3,768,256]{2,1,0:T(8,128)(2,1)} %bitcast.12, bf16[256,512]{1,0:T(8,128)(2,1)} %down_mid_in.1, ...), custom_call_target="tpu_custom_call" | custom-call | tf_op jit(solution)/shard_map/whole_net/pallas_call | solution.py:815
  79.4 4.1 %finish.1 = (bf16[4,512,256]{2,1,0:T(8,128)(2,1)}, f32[4,512,256]{2,1,0:T(8,128)}) custom-call(bf16[4,512,256]{2,1,0:T(8,128)(2,1)} %get-tuple-element.8.output_in, bf16[4,512,256]{2,1,0:T(8,128)(2,1)} %get-tuple-element.9.part, bf16[4,512,256]{2,1,0:T(8,128)(2,1)} %bitcast.11, f32[1,256]{1,0:T(1,128)} %get-tuple-element.10.shift, ...), custom_call_target="tpu_custom_call" | custom-call | tf_op jit(solution)/shard_map/finish/pallas_call | solution.py:847

commit v3 on v2

--- a/solution.py
+++ b/solution.py
@@ -43,7 +43,7 @@
             pick[4 * (i // 4) + j // 4, 16 * i + j] = 1
         pick[32 + i, 16 * i + 15] = 1
         pick[64 + i, 16 * i] = 1
-    enlarge = np.zeros((912, 256), np.float32)
+    enlarge = np.zeros((512, 256), np.float32)
     taps = np.zeros((1152, 256), np.float32)
     ends = np.zeros((16, 256), np.float32)
     pack = np.zeros((112, 128), np.float32)
@@ -54,14 +54,7 @@
         for i in range(8):
             for j in range(16):
                 enlarge[128 * f + 16 * i + j, mid_row(f, i, j // 4)] = 1
-        for j in range(16):
-            enlarge[512 + 16 * f + j, ABOVE + 4 * f + j // 4] = 1
-            enlarge[576 + 16 * f + j, BELOW + 4 * f + j // 4] = 1
-        for i in range(32):
-            enlarge[640 + 32 * f + i, LEFT + 8 * f + i // 4] = 1
-            enlarge[768 + 32 * f + i, RIGHT + 8 * f + i // 4] = 1
         for c in range(4):
-            enlarge[896 + 4 * c + f, CORNER + 4 * c + f] = 1
             low, first = c < 2, c % 2 == 1
             ends[4 * c + f, 128 * first + 32 * f + 31 * low] = 1
             pack[96 + 4 * c + f, mid_row(f, 7 * low, 3 * (not first))] = 1
@@ -83,14 +76,41 @@
             for j in range(-1, 5):
                 side = -1 if j < 0 else (1 if j > 3 else 0)
                 spread[mid_row(f, i, j), coarse_row(f, i // 4 if i < 8 else 2, side)] = 1
+    windows = np.zeros((288, 640), np.float32)
+    for t in range(9):
+        for i in range(32):
+            for j in range(16):
+                p, q = i + 1 - t // 3, j + 1 - t % 3
+                row = 32 * t + 4 * (i // 4) + j // 4
+                if 0 <= p < 32 and 0 <= q < 16:
+                    at = 16 * p + q
+                elif 0 <= q < 16:
+                    at = (512 if p < 0 else 528) + q
+                elif 0 <= p < 32:
+                    at = (544 if q < 0 else 576) + p
+                else:
+                    at = 608 + 2 * (p > 31) + (q > 15)
+                windows[row, at] = 1
+    stretch = np.zeros((640, 768), np.float32)
+    for f in range(4):
+        for i in range(10):
+            for j in range(16):
+                for b in range(3):
+                    at = 256 * b + mid_row(f, i - 1, (j + b - 1) // 4)
+                    stretch[160 * f + 16 * i + j, at] = 1
+    by_frame = np.zeros((128, 128), np.float32)
+    for f in range(4):
+        for c in range(4):
+            by_frame[32 * f + c, 4 * c + f] = 1
     sides = np.zeros((512, 128), np.float32)
     for i in range(32):
         sides[16 * i, i] = 1
         sides[16 * i + 15, 64 + i] = 1
     wide_table = np.concatenate([pick, np.concatenate([enlarge, enlarge], axis=1)])
     middle_table = np.concatenate([taps, ends])
-    narrow_table = np.concatenate([pack, pool, coarse_taps, spread, sides])
-    return [jnp.asarray(t, BF16) for t in (wide_table, middle_table, narrow_table)]
+    narrow_table = np.concatenate([pack, pool, coarse_taps, spread, sides, by_frame])
+    result = (wide_table, middle_table, narrow_table, windows, stretch)
+    return [jnp.asarray(t, BF16) for t in result]
 
 
 def dot(a, b):
@@ -99,6 +119,10 @@
 
 def dot_t(a, b):
     return lax.dot_general(a, b, (((1,), (1,)), ((), ())), preferred_element_type=F32)
+
+
+def dot_first(a, b):
+    return lax.dot_general(a, b, (((0,), (0,)), ((), ())), preferred_element_type=F32)
 
 
 def group_lanes(t, size):
@@ -135,13 +159,12 @@
     wide_table_in,
     middle_table_in,
     narrow_table_in,
+    windows_in,
+    stretch_in,
     out_ref,
-    part_ref,
-    shift_ref,
-    slant_ref,
+    grad_ref,
     xg,
     kernel_fine,
-    flipped_fine,
     down_mid,
     kernel_mid,
     down_coarse,
@@ -154,21 +177,33 @@
     wide_table,
     middle_table,
     narrow_table,
+    windows,
+    stretch,
     taps_buf,
     coarse_taps,
     columns,
     fine_block,
-    part,
+    grad_buf,
+    conv_grad,
     pooled,
     summed,
     fine_slope,
     edge_rows,
     edge_sides,
     edge_ends,
-    pool_grad,
     summed_grad,
     first,
     second,
+    first_joint,
+    second_joint,
+    first_matrix,
+    second_matrix,
+    window_sums,
+    slope_rows,
+    slope_sides,
+    slope_ends,
+    matrix_sum,
+    stretched,
     col_pack,
     cor_pack,
     row_in,
@@ -198,10 +233,16 @@
 ):
     wide, narrow = lax.axis_index("wide"), lax.axis_index("narrow")
 
+    def around(index, step, count):
+        moved = index + step
+        if isinstance(step, int) and step < 0:
+            return jnp.where(moved < 0, moved + count, moved)
+        return jnp.where(moved >= count, moved - count, moved)
+
     def device(down, side):
         return (
-            lax.rem(wide + down + wide_count, wide_count),
-            lax.rem(narrow + side + narrow_count, narrow_count),
+            wide if isinstance(down, int) and down == 0 else around(wide, down, wide_count),
+            narrow if isinstance(side, int) and side == 0 else around(narrow, side, narrow_count),
         )
 
     loads = {}
@@ -221,6 +262,8 @@
         ("kernel_mid", kernel_mid_in, kernel_mid),
         ("down_coarse", down_coarse_in, down_coarse),
         ("gain_coarse", gain_coarse_in, gain_coarse),
+        ("windows", windows_in, windows),
+        ("stretch", stretch_in, stretch),
     )
     for number, (name, source, target) in enumerate(pairs):
         loads[name] = pltpu.make_async_copy(source, target, load_sem.at[number])
@@ -253,48 +296,64 @@
     def sent(buffer, which):
         pltpu.make_async_copy(buffer, buffer, halo_send.at[which]).wait()
 
-    def total_begin(phase, one, two):
-        blank = jnp.zeros((8, 128), F32)
-        first[phase, wide] = blank
-        for k in range(one.shape[1] // 128):
-            first[phase, wide, k : k + 1, :] = one[:, 128 * k : 128 * k + 128]
-            first[phase, wide, 4 + k : 5 + k, :] = two[:, 128 * k : 128 * k + 128]
+    firsts = tuple(first.at[p] for p in range(4)) + (first_joint, first_matrix)
+    seconds = tuple(second.at[p] for p in range(4)) + (second_joint, second_matrix)
+
+    def total_send_wide(phase):
+        mine = firsts[phase].at[wide]
+
         @pl.loop(1, wide_count)
         def _(step):
             pltpu.make_async_remote_copy(
-                src_ref=first.at[phase, wide],
-                dst_ref=first.at[phase, wide],
+                src_ref=mine,
+                dst_ref=mine,
                 send_sem=total_send.at[2 * phase],
                 recv_sem=total_recv.at[2 * phase],
                 device_id=device(step, 0),
                 device_id_type=MESH,
             ).start()
 
+    def total_fill(phase, start, values):
+        for n, value in enumerate(values):
+            for k in range(value.shape[1] // 128):
+                at = start + 4 * n + k
+                firsts[phase][wide, at : at + 1, :] = value[:, 128 * k : 128 * k + 128]
+
+    def total_begin(phase, one, two):
+        if one.shape[1] < 512:
+            firsts[phase][wide] = jnp.zeros((8, 128), F32)
+        total_fill(phase, 0, (one, two))
+        total_send_wide(phase)
+
     def total_middle(phase):
-        whole = first.at[phase, pl.ds(0, wide_count - 1)]
+        whole = firsts[phase].at[pl.ds(0, wide_count - 1)]
         pltpu.make_async_copy(whole, whole, total_recv.at[2 * phase]).wait()
-        second[phase, narrow] = jnp.sum(first[phase], axis=0)
+        seconds[phase][narrow] = jnp.sum(firsts[phase][...], axis=0)
+        mine = seconds[phase].at[narrow]
+
         @pl.loop(1, narrow_count)
         def _(step):
             pltpu.make_async_remote_copy(
-                src_ref=second.at[phase, narrow],
-                dst_ref=second.at[phase, narrow],
+                src_ref=mine,
+                dst_ref=mine,
                 send_sem=total_send.at[2 * phase + 1],
                 recv_sem=total_recv.at[2 * phase + 1],
                 device_id=device(0, step),
                 device_id_type=MESH,
             ).start()
 
+    def total_sum(phase):
+        whole = seconds[phase].at[pl.ds(0, narrow_count - 1)]
+        pltpu.make_async_copy(whole, whole, total_recv.at[2 * phase + 1]).wait()
+        return jnp.sum(seconds[phase][...], axis=0)
+
+    def row_of(t, start, channels):
+        return jnp.concatenate([t[start + k : start + k + 1] for k in range(channels // 128)], axis=1)
+
     def total_end(phase, channels, cells):
-        whole = second.at[phase, pl.ds(0, narrow_count - 1)]
-        pltpu.make_async_copy(whole, whole, total_recv.at[2 * phase + 1]).wait()
         size = channels // GROUPS
-        t = group_lanes(jnp.sum(second[phase], axis=0), size) * (1.0 / (size * cells))
-        count = channels // 128
-        return (
-            jnp.concatenate([t[k : k + 1] for k in range(count)], axis=1),
-            jnp.concatenate([t[4 + k : 5 + k] for k in range(count)], axis=1),
-        )
+        t = group_lanes(total_sum(phase), size) * (1.0 / (size * cells))
+        return row_of(t, 0, channels), row_of(t, 4, channels)
 
     has_above, has_below = wide > 0, wide < wide_count - 1
     has_left, has_right = narrow > 0, narrow < narrow_count - 1
@@ -315,8 +374,8 @@
             value = change(read(c).astype(F32))
             if masked:
                 value = only(has_corner[c], value)
-            quarter = lax.broadcasted_iota(jnp.int32, value.shape, 0) // 4
-            result = value if result is None else jnp.where(quarter == c, value, result)
+            cell = lax.broadcasted_iota(jnp.int32, value.shape, 0)
+            result = value if result is None else jnp.where(cell >= 4 * c, value, result)
         return result
 
     def mid_extended(own, read_halo, read_cor, change, masked):
@@ -352,7 +411,7 @@
         return jnp.concatenate(pieces, axis=0)
 
     PICK = wide_table.at[pl.ds(0, 96)]
-    ENLARGE = wide_table.at[pl.ds(96, 912)]
+    ENLARGE = wide_table.at[pl.ds(96, 512)]
     TAPS = middle_table.at[pl.ds(0, 1152)]
     ENDS = middle_table.at[pl.ds(1152, 16)]
     PACK = narrow_table.at[pl.ds(0, 112)]
@@ -360,6 +419,7 @@
     COARSE_TAPS = narrow_table.at[pl.ds(128, 144)]
     SPREAD = narrow_table.at[pl.ds(272, 256)]
     SIDES = narrow_table.at[pl.ds(528, 512)]
+    BY_FRAME = narrow_table.at[pl.ds(1040, 128)]
 
     def frame(which, f):
         return xg[which, f].reshape(512, 256)
@@ -413,17 +473,22 @@
     fine_inverse = lax.rsqrt(fine_square - fine_center * fine_center + epsilon)
     s_fine = gain_fine[...]
 
-    def silu(value, center, inverse, scaling):
-        normed = (value - center) * inverse * scaling
-        return normed / (1.0 + jnp.exp(-normed))
+    def silu(center, inverse, scaling):
+        gain = 0.5 * inverse * scaling
+        shift = -center * gain
+
+        def change(value):
+            half = value * gain + shift
+            return half * jnp.tanh(half) + half
+
+        return change
 
     def slope(scaled, scaling):
-        normed = scaled * scaling
-        logistic = 1.0 / (1.0 + jnp.exp(-normed))
-        return logistic * (1.0 + normed * (1.0 - logistic)) * scaling
-
-    def fine_act(value):
-        return silu(value, fine_center, fine_inverse, s_fine)
+        half = scaled * (0.5 * scaling)
+        bend = jnp.tanh(half)
+        return (0.5 * scaling) * (1.0 + bend) * (1.0 + half * (1.0 - bend))
+
+    fine_act = silu(fine_center, fine_inverse, s_fine)
 
     arrived(row_in.at[:, 0], 0)
     arrived(col_in.at[:, 0], 1)
@@ -440,7 +505,7 @@
         edge_ends[...] = ends
 
     def place(f, own):
-        column = lax.broadcasted_iota(jnp.int32, (512, 256), 0) % 16
+        column = lax.broadcasted_iota(jnp.int32, (512, 256), 0) & 15
         sides = edge_sides[f]
         low = jnp.where(
             column == 0, dot(SIDES[:, 0:64], sides), pltpu.roll(own, 1, 0)
@@ -461,10 +526,24 @@
             columns[f, at, 256:512] = row.astype(BF16)
             columns[f, at, 512:768] = jnp.where(cell == 15, east, pltpu.roll(row, 15, 0)).astype(BF16)
 
-    def fine_convolve(f, weights):
-        total = dot(columns[f, 0:512, :], weights[0])
-        total += dot(columns[f, 16:528, :], weights[1])
-        return total + dot(columns[f, 32:544, :], weights[2])
+    def fine_convolve(f):
+        total = dot(columns[f, 0:512, :], kernel_fine[0:3].reshape(768, 256))
+        total += dot(columns[f, 16:528, :], kernel_fine[3:6].reshape(768, 256))
+        return total + dot(columns[f, 32:544, :], kernel_fine[6:9].reshape(768, 256))
+
+    def fine_convolve_back(f):
+        total = None
+        for a in range(3):
+            for b in range(3):
+                term = dot_t(
+                    columns[f, 16 * a : 16 * a + 512, 256 * b : 256 * b + 256],
+                    kernel_fine[8 - 3 * a - b],
+                )
+                total = term if total is None else total + term
+        return total
+
+    def fine_scaled(value):
+        return (value - fine_center) * fine_inverse
 
     set_edges(
         fine_act(row_in[0, 0].astype(F32)),
@@ -481,12 +560,15 @@
     def _(f):
         value = fine_value(f)
         place(f, fine_act(value))
-        block = (value + fine_convolve(f, kernel_fine)).astype(BF16)
+        block = (value + fine_convolve(f)).astype(BF16)
         fine_block[f] = block
         pooled[pl.ds(pl.multiple_of(32 * f, 32), 32), :] = (
             dot(PICK[0:32, :], block) * 0.0625
         ).astype(BF16)
 
+    def same(value):
+        return value
+
     loads["down_mid"].wait()
     mid_in = dot(pooled[...], down_mid[...]).astype(BF16)
     mid_value = mid_in.astype(F32)
@@ -497,6 +579,27 @@
     total_begin(1, column_sums(mid_value), column_sums(mid_value * mid_value))
     mid_pack[...] = dot(PACK[...], mid_in).astype(BF16)
     send_mid(mid_pack, mid_halo, mid_cor, 6)
+
+    @pl.loop(0, 4)
+    def _(f):
+        fine_slope[f] = slope(fine_scaled(fine_value(f)), s_fine)
+
+    def pair_of(value, condition):
+        scaled = fine_scaled(value.astype(F32))
+        bent = slope(scaled, s_fine)
+        if condition is not None:
+            bent = only(condition, bent)
+        return bent.astype(BF16), (bent * scaled).astype(BF16)
+
+    for k in range(2):
+        for n, value in enumerate(pair_of(row_in[k, 0], exists[1 + k])):
+            slope_rows[n, k] = value
+        for n, value in enumerate(pair_of(col_in[k, 0], exists[3 + k])):
+            slope_sides[n, k] = value.reshape(4, 32, 256)
+    bent = corners(lambda c: cor_in[0, c], lambda v: slope(fine_scaled(v), s_fine), True)
+    scaled = corners(lambda c: cor_in[0, c], fine_scaled, False)
+    for n, value in enumerate((bent, bent * scaled)):
+        slope_ends[n] = dot(BY_FRAME[:, 0:16], value.astype(BF16)).astype(BF16).reshape(4, 32, 256)
 
     up_mid_grad = summed[...]
     sum_pack[...] = dot(PACK[...], up_mid_grad).astype(BF16)
@@ -509,21 +612,13 @@
     send_coarse(cgrad_own, cgrad_in, 5)
     total_middle(1)
 
-    for a in range(3):
-        for b in range(3):
-            flipped_fine[a, 256 * b : 256 * b + 256, :] = kernel_fine[
-                2 - a, 256 * (2 - b) : 256 * (2 - b) + 256, :
-            ].T
-
-
     loads["gain_mid"].wait()
     loads["kernel_mid"].wait()
     mid_center, mid_square = total_end(1, 512, 128 * wide_count * narrow_count)
     mid_inverse = lax.rsqrt(mid_square - mid_center * mid_center + epsilon)
     s_mid = gain_mid[...]
 
-    def mid_act(value):
-        return silu(value, mid_center, mid_inverse, s_mid)
+    mid_act = silu(mid_center, mid_inverse, s_mid)
 
     def mid_scaled(value):
         return (value - mid_center) * mid_inverse
@@ -553,6 +648,30 @@
     coarse_value = coarse_in.astype(F32)[0:8]
     total_begin(2, column_sums(coarse_value), column_sums(coarse_value * coarse_value))
     send_coarse(coarse_own, coarse_halo, 8)
+
+    arrived(row_in.at[:, 1], 13)
+    arrived(col_in.at[:, 1], 14)
+    arrived(cor_in.at[1], 15)
+    set_edges(
+        row_in[0, 1].astype(F32),
+        row_in[1, 1].astype(F32),
+        col_in[0, 1].astype(F32),
+        col_in[1, 1].astype(F32),
+        corners(lambda c: cor_in[1, c], same, True),
+    )
+
+    def convolve_grad(f, carry):
+        place(f, frame(1, f).astype(F32))
+        result = fine_convolve_back(f)
+        conv_grad[f] = result
+        weighted = result * fine_slope[f]
+        scaled = fine_scaled(fine_value(f))
+        return (
+            carry[0] + jnp.sum(weighted.reshape(64, 8, 256), axis=0),
+            carry[1] + jnp.sum((weighted * scaled).reshape(64, 8, 256), axis=0),
+        )
+
+    grad_sums = lax.fori_loop(0, 2, convolve_grad, (blank, blank))
     total_middle(2)
 
     arrived(cgrad_in, 5)
@@ -565,9 +684,6 @@
             0, 9, lambda t, total: total + weights(t, coarse_taps[t]), jnp.zeros((16, 512), F32)
         )
 
-    def same(value):
-        return value
-
     cgrad = cgrad_own[...].astype(F32)[0:8]
     coarse_act_grad = coarse_convolve(
         coarse_extended(cgrad, lambda d: cgrad_in[d].astype(F32)[0:8], same, True),
@@ -594,26 +710,63 @@
     total_begin(3, column_sums(normed_grad), column_sums(normed_grad * scaled))
     coarse_u[...] = cgrad + coarse_inverse * normed_grad
     send_coarse(coarse_u, coarse_u_halo, 9)
+    grad_sums = lax.fori_loop(2, 4, convolve_grad, grad_sums)
+
+    loads["windows"].wait()
+
+    @pl.loop(0, 4)
+    def _(f):
+        for n in range(2):
+            bent = fine_slope[f]
+            if n == 1:
+                bent = bent * fine_scaled(fine_value(f))
+            field = jnp.concatenate(
+                [
+                    bent.astype(BF16),
+                    slope_rows[n, 0, f],
+                    slope_rows[n, 1, f],
+                    slope_sides[n, 0, f],
+                    slope_sides[n, 1, f],
+                    slope_ends[n, f],
+                ],
+                axis=0,
+            )
+            window_sums[n, :, f] = dot(windows[...], field).astype(BF16).reshape(9, 32, 256)
+
     total_middle(3)
 
+    mid_mix = jnp.concatenate(
+        [mid_scaled(mid_value).astype(BF16), jnp.ones((128, 128), BF16)], axis=1
+    )
+    matrix_sum[...] = jnp.zeros((4, 256, 512), F32)
+
+    @pl.loop(0, 9)
+    def _(t):
+        through = 0.0625 * dot(kernel_fine[8 - t], down_mid[...])
+        for n in range(2):
+            mixed = dot_first(window_sums[n, t].reshape(128, 256), mid_mix)
+            plain = jnp.concatenate([mixed[:, 512:640]] * 4, axis=1)
+            matrix_sum[2 * n] += through * plain
+            matrix_sum[2 * n + 1] += through * mixed[:, 0:512]
+
+    def iota(shape, axis):
+        return lax.broadcasted_iota(jnp.int32, shape, axis)
+
+    def one_hot(condition):
+        return jnp.where(condition, 1.0, 0.0).astype(BF16)
+
+    by_group = one_hot((iota((32, 256), 1) >> 3) == iota((32, 256), 0))
+    matrix = jnp.zeros((32, 128), F32)
+    for n in range(4):
+        high, low = halves(matrix_sum[n] * mid_inverse)
+        high, low = halves(dot(by_group, high) + dot(by_group, low))
+        to_lane = one_hot(iota((512, 128), 1) == 32 * n + (iota((512, 128), 0) >> 4))
+        matrix += dot(high, to_lane) + dot(low, to_lane)
+    first_matrix[wide] = matrix
+    total_send_wide(5)
+
+    first_mean, second_mean = total_end(3, 512, 8 * wide_count * narrow_count)
     arrived(coarse_halo, 8)
-    coarse_block = (
-        coarse_in.astype(F32)
-        + coarse_convolve(
-            coarse_extended(
-                coarse_value,
-                lambda d: coarse_halo[d].astype(F32)[0:8],
-                lambda v: silu(v, coarse_center, coarse_inverse, s_coarse),
-                True,
-            ),
-            lambda t, part_: dot(part_, kernel_coarse[t]),
-        )
-    ).astype(BF16)
-    coarse_up = dot(coarse_block, up_coarse[...]).astype(BF16)
-    mid_sum = (mid_block.astype(F32) + dot(SPREAD[0:128, 0:16], coarse_up)).astype(BF16)
-    mid_up = dot(mid_sum, up_mid[...]).astype(BF16)
-
-    first_mean, second_mean = total_end(3, 512, 8 * wide_count * narrow_count)
     arrived(coarse_u_halo, 9)
     offset = coarse_inverse * first_mean
     factor = coarse_inverse * second_mean
@@ -625,7 +778,7 @@
     coarse_in_grad = jnp.concatenate(pieces, axis=0).astype(BF16)
 
     mid_pool_grad = dot_t(dot(SPREAD[...], coarse_in_grad).astype(BF16), down_coarse[...])
-    row = lax.broadcasted_iota(jnp.int32, (256, 512), 0)
+    row = lax.broadcasted_iota(jnp.int32, (256, 128), 0)
     keep = jnp.where(row < ABOVE, 1.0, 0.0)
     bounds = ((ABOVE, 16, 1), (BELOW, 16, 2), (LEFT, 32, 3), (RIGHT, 32, 4)) + tuple(
         (CORNER + 4 * c, 4, 5 + c) for c in range(4)
@@ -633,35 +786,53 @@
     for start, size, d in bounds:
         inside = jnp.logical_and(row >= start, row < start + size)
         keep = jnp.where(inside, jnp.where(exists[d], 1.0, 0.0).astype(F32), keep)
-    mid_grad = (summed_grad[...] + 0.0625 * mid_pool_grad) * keep
+    mid_grad = (summed_grad[...] + 0.0625 * mid_pool_grad) * jnp.concatenate([keep] * 4, axis=1)
     mid_act_grad = mid_convolve(mid_grad, lambda t, part_: dot_t(part_, kernel_mid[8 - t]))
     scaled = mid_scaled(mid_value)
     normed_grad = mid_act_grad * slope(scaled, s_mid)
-    total_begin(4, column_sums(normed_grad), column_sums(normed_grad * scaled))
     mid_u = mid_grad[0:128].astype(BF16).astype(F32) + mid_inverse * normed_grad
     u_pack[...] = dot(PACK[...], mid_u.astype(BF16)).astype(BF16)
     send_mid(u_pack, u_halo, u_cor, 10)
+    pulled = (0.0625 * dot_t(mid_u.astype(BF16), down_mid[...])).astype(BF16)
+    fine_sums = [jnp.sum(value, axis=0, keepdims=True) for value in grad_sums]
+    for t in range(9):
+        term = dot_t(pulled, kernel_fine[8 - t])
+        for n in range(2):
+            fine_sums[n] += column_sums(window_sums[n, t].reshape(128, 256).astype(F32) * term)
+    first_joint[wide, 8:16, :] = jnp.zeros((8, 128), F32)
+    total_fill(4, 0, (column_sums(normed_grad), column_sums(normed_grad * scaled)))
+    total_fill(4, 8, fine_sums)
+    total_send_wide(4)
+    total_middle(5)
+
+    coarse_block = (
+        coarse_in.astype(F32)
+        + coarse_convolve(
+            coarse_extended(
+                coarse_value,
+                lambda d: coarse_halo[d].astype(F32)[0:8],
+                silu(coarse_center, coarse_inverse, s_coarse),
+                True,
+            ),
+            lambda t, part_: dot(part_, kernel_coarse[t]),
+        )
+    ).astype(BF16)
+    coarse_up = dot(coarse_block, up_coarse[...]).astype(BF16)
+    mid_sum = (mid_block.astype(F32) + dot(SPREAD[0:128, 0:16], coarse_up)).astype(BF16)
+    mid_up = dot(mid_sum, up_mid[...]).astype(BF16)
     total_middle(4)
 
-    mid_up = dot(ENLARGE[0:512, 0:128], mid_up).reshape(4, 8, 1, 16, 256)
+    mid_up = dot(ENLARGE[:, 0:128], mid_up).reshape(4, 8, 1, 16, 256)
     for f in range(4):
         block = fine_block[f].astype(F32).reshape(8, 4, 16, 256)
         fine_block[f] = (block + mid_up[f]).astype(BF16).reshape(512, 256)
     out_copy = pltpu.make_async_copy(fine_block, out_ref, out_sem.at[0])
     out_copy.start()
-
-    def fine_scaled(f):
-        return (fine_value(f) - fine_center) * fine_inverse
-
-    @pl.loop(0, 4)
-    def _(f):
-        fine_slope[f] = slope(fine_scaled(f), s_fine)
-
-    arrived(row_in.at[:, 1], 13)
-    arrived(col_in.at[:, 1], 14)
-    arrived(cor_in.at[1], 15)
-
-    first_mean, second_mean = total_end(4, 512, 128 * wide_count * narrow_count)
+    matrix = total_sum(5)
+
+    joint = total_sum(4)
+    t = group_lanes(joint[0:8], 16) * (1.0 / (16 * 128 * wide_count * narrow_count))
+    first_mean, second_mean = row_of(t, 0, 512), row_of(t, 4, 512)
     arrived(u_halo, 10)
     arrived(u_cor, 11)
     offset = mid_inverse * first_mean
@@ -672,37 +843,54 @@
         mid_value, mid_halo[...], lambda c: mid_cor[c], mid_scaled, False
     )
 
-    high, low = halves(0.0625 * dot_t(mid_in_grad.astype(BF16), down_mid[...]))
-    pool_grad[...] = dot(ENLARGE[...], jnp.concatenate([high, low], axis=0))
-
-    def rounded(value):
-        return value.astype(BF16).astype(F32)
-
-    set_edges(
-        rounded(row_in[0, 1].astype(F32) + pool_grad[512:576, :].reshape(4, 16, 256)),
-        rounded(row_in[1, 1].astype(F32) + pool_grad[576:640, :].reshape(4, 16, 256)),
-        rounded(col_in[0, 1].astype(F32) + pool_grad[640:768, :]),
-        rounded(col_in[1, 1].astype(F32) + pool_grad[768:896, :]),
-        corners(lambda c: cor_in[1, c], lambda v: v + pool_grad[896:912, :], True),
-    )
-
-    def fine_backward(f, carry):
-        added = pool_grad[pl.ds(pl.multiple_of(128 * f, 128), 128), :].reshape(8, 1, 16, 256)
-        grad = xg[1, f].astype(F32).reshape(8, 4, 16, 256) + added
-        grad = rounded(grad.reshape(512, 256))
-        place(f, grad)
-        normed_grad = fine_convolve(f, flipped_fine) * fine_slope[f]
-        part[f] = (grad + fine_inverse * normed_grad).astype(BF16)
-        return (
-            carry[0] + jnp.sum(normed_grad.reshape(64, 8, 256), axis=0),
-            carry[1] + jnp.sum((normed_grad * fine_scaled(f)).reshape(64, 8, 256), axis=0),
+    pool_grad = 0.0625 * dot_t(mid_in_grad.astype(BF16), down_mid[...])
+    pool_grad = pool_grad * jnp.concatenate([keep] * 2, axis=1)
+    high, low = halves(pool_grad)
+    added = dot(ENLARGE[...], jnp.concatenate([high[0:256], low[0:256]], axis=0))
+    loads["stretch"].wait()
+    for a in range(3):
+        fields = [dot_t(high, kernel_fine[8 - 3 * a - b]).astype(BF16) for b in range(3)]
+        stretched[a] = dot(stretch[...], jnp.concatenate(fields, axis=0)).reshape(4, 10, 16, 256)
+
+    means = jnp.zeros((8, 128), F32)
+    for n, mean in enumerate((first_mean, second_mean)):
+        lane, row = iota((512, 128), 1), iota((512, 128), 0)
+        inside = jnp.logical_and((lane & 31) == (row >> 4), ((lane >> 5) & 1) == n)
+        to_lane = jnp.where(inside, 0.0625, 0.0).astype(BF16)
+        high, low = halves(jnp.broadcast_to(mean, (8, 512)))
+        means += dot(high, to_lane) + dot(low, to_lane)
+    matrix_high, matrix_low = halves(matrix)
+    spread_groups = one_hot((iota((256, 32), 0) >> 3) == iota((256, 32), 1))
+    t = group_lanes(joint[8:16], 8)
+    fine_means = []
+    for n in range(2):
+        half = jnp.where((iota((8, 128), 1) >> 6) == n, means, 0.0)
+        high, low = halves(half)
+        change = dot_t(high, matrix_high) + dot_t(low, matrix_high) + dot_t(high, matrix_low)
+        high, low = halves(change)
+        change = dot_t(high, spread_groups) + dot_t(low, spread_groups)
+        fine_means.append(
+            (row_of(t, 4 * n, 256) - change[0:1]) * (1.0 / (8 * 2048 * wide_count * narrow_count))
         )
-
-    one, two = lax.fori_loop(0, 4, fine_backward, (blank, blank))
-    total_begin(5, jnp.sum(one, axis=0, keepdims=True), jnp.sum(two, axis=0, keepdims=True))
-    part_copy = pltpu.make_async_copy(part, part_ref, out_sem.at[1])
-    part_copy.start()
-    total_middle(5)
+    slant = -fine_inverse * fine_inverse * fine_means[1]
+    shift = -fine_inverse * fine_means[0] - fine_center * slant
+
+    added = added.reshape(4, 8, 1, 16, 256)
+    grad_copies = []
+    for f in range(4):
+        above, here, below = stretched[0, f], stretched[1, f], stretched[2, f]
+        centre = here[1:9] + above[1:9] + below[1:9]
+        top = here[1:9] + above[0:8] + below[1:9]
+        bottom = here[1:9] + above[1:9] + below[2:10]
+        back = jnp.stack([top, centre, centre, bottom], axis=1).reshape(512, 256)
+        normed_grad = (conv_grad[f] + back) * fine_slope[f]
+        grad = xg[1, f].astype(F32).reshape(8, 4, 16, 256) + added[f]
+        grad = grad.reshape(512, 256).astype(BF16).astype(F32)
+        grad_buf[f] = grad + fine_inverse * normed_grad + (shift + fine_value(f) * slant)
+        grad_copies.append(
+            pltpu.make_async_copy(grad_buf.at[f], grad_ref.at[f], out_sem.at[1 + f])
+        )
+        grad_copies[f].start()
 
     for which in range(2):
         sent(row_in.at[:, which], 13 * which)
@@ -718,22 +906,13 @@
     sent(u_halo, 10)
     sent(u_cor, 11)
     for phase in range(6):
-        whole = first.at[phase, pl.ds(0, wide_count - 1)]
+        whole = firsts[phase].at[pl.ds(0, wide_count - 1)]
         pltpu.make_async_copy(whole, whole, total_send.at[2 * phase]).wait()
-    first_mean, second_mean = total_end(5, 256, 2048 * wide_count * narrow_count)
-    for phase in range(6):
-        whole = second.at[phase, pl.ds(0, narrow_count - 1)]
+        whole = seconds[phase].at[pl.ds(0, narrow_count - 1)]
         pltpu.make_async_copy(whole, whole, total_send.at[2 * phase + 1]).wait()
-    slant = -fine_inverse * fine_inverse * second_mean
-    shift_ref[...] = -fine_inverse * first_mean - fine_center * slant
-    slant_ref[...] = slant
     out_copy.wait()
-    part_copy.wait()
-
-
-def finish(output_in, part, value, shift, slant, output, grad):
-    output[...] = output_in[...]
-    grad[0] = part[0].astype(F32) + (shift[...] + value[0].astype(F32) * slant[...])
+    for copy in grad_copies:
+        copy.wait()
 
 
 def shards(*arguments):
@@ -756,8 +935,7 @@
     vmem = pltpu.VMEM
     scratch = [
         vmem((2, 4, 32, 16, 256), BF16),
-        vmem((3, 768, 256), BF16),
-        vmem((3, 768, 256), BF16),
+        vmem((9, 256, 256), BF16),
         vmem((256, 512), BF16),
         vmem((9, 512, 512), BF16),
         vmem((512, 512), BF16),
@@ -767,24 +945,36 @@
         vmem((1, 256), F32),
         vmem((1, 512), F32),
         vmem((1, 512), F32),
-        vmem((1008, 512), BF16),
+        vmem((608, 512), BF16),
         vmem((1168, 256), BF16),
-        vmem((1040, 128), BF16),
+        vmem((1168, 128), BF16),
+        vmem((288, 640), BF16),
+        vmem((640, 768), BF16),
         vmem((9, 128, 512), BF16),
         vmem((9, 16, 512), BF16),
         vmem((4, 544, 768), BF16),
         vmem((4, 512, 256), BF16),
-        vmem((4, 512, 256), BF16),
+        vmem((4, 512, 256), F32),
+        vmem((4, 512, 256), F32),
         vmem((128, 256), BF16),
         vmem((128, 256), BF16),
         vmem((4, 512, 256), F32),
         vmem((2, 4, 16, 256), F32),
         vmem((4, 64, 256), BF16),
         vmem((16, 256), F32),
-        vmem((912, 256), F32),
         vmem((256, 512), F32),
-        vmem((6, wide_count, 8, 128), F32),
-        vmem((6, narrow_count, 8, 128), F32),
+        vmem((4, wide_count, 8, 128), F32),
+        vmem((4, narrow_count, 8, 128), F32),
+        vmem((wide_count, 16, 128), F32),
+        vmem((narrow_count, 16, 128), F32),
+        vmem((wide_count, 32, 128), F32),
+        vmem((narrow_count, 32, 128), F32),
+        vmem((2, 9, 4, 32, 256), BF16),
+        vmem((2, 2, 4, 16, 256), BF16),
+        vmem((2, 2, 4, 32, 256), BF16),
+        vmem((2, 4, 32, 256), BF16),
+        vmem((4, 256, 512), F32),
+        vmem((3, 4, 10, 16, 256), F32),
         vmem((2, 2, 128, 256), BF16),
         vmem((2, 16, 256), BF16),
         vmem((2, 2, 4, 16, 256), BF16),
@@ -805,23 +995,21 @@
         vmem((112, 512), BF16),
         vmem((96, 512), BF16),
         vmem((4, 16, 512), BF16),
-        pltpu.SemaphoreType.DMA((15,)),
-        pltpu.SemaphoreType.DMA((2,)),
+        pltpu.SemaphoreType.DMA((17,)),
+        pltpu.SemaphoreType.DMA((5,)),
         pltpu.SemaphoreType.DMA((12,)),
         pltpu.SemaphoreType.DMA((12,)),
         pltpu.SemaphoreType.DMA((16,)),
         pltpu.SemaphoreType.DMA((16,)),
     ]
-    output, part, shift, slant = pl.pallas_call(
+    output, grad = pl.pallas_call(
         functools.partial(kernel, wide_count, narrow_count),
         out_shape=(
             jax.ShapeDtypeStruct((4, 512, 256), BF16),
-            jax.ShapeDtypeStruct((4, 512, 256), BF16),
-            jax.ShapeDtypeStruct((1, 256), F32),
-            jax.ShapeDtypeStruct((1, 256), F32),
+            jax.ShapeDtypeStruct((4, 512, 256), F32),
         ),
-        in_specs=[anywhere] * 15,
-        out_specs=(anywhere, anywhere) + (pl.BlockSpec(memory_space=pltpu.VMEM),) * 2,
+        in_specs=[anywhere] * 17,
+        out_specs=(anywhere, anywhere),
         scratch_shapes=scratch,
         compiler_params=pltpu.CompilerParams(
             collective_id=0, has_side_effects=True, vmem_limit_bytes=56 * 2**20
@@ -830,7 +1018,7 @@
     )(
         fine_input,
         gain_fine.reshape(1, 256),
-        kernel_fine.reshape(3, 768, 256),
+        kernel_fine.reshape(9, 256, 256),
         down_mid,
         gain_mid.reshape(1, 512),
         kernel_mid.reshape(9, 512, 512),
@@ -842,19 +1030,6 @@
         grad_out,
         *tables(),
     )
-    cells = pl.BlockSpec((1, 512, 256), lambda f: (f, 0, 0))
-    vector = pl.BlockSpec((1, 256), lambda f: (0, 0))
-    output, grad = pl.pallas_call(
-        finish,
-        grid=(4,),
-        out_shape=(
-            jax.ShapeDtypeStruct((4, 512, 256), BF16),
-            jax.ShapeDtypeStruct((4, 512, 256), F32),
-        ),
-        in_specs=[cells, cells, cells, vector, vector],
-        out_specs=(cells, cells),
-        name="finish",
-    )(output, part, fine_input.reshape(4, 512, 256), shift, slant)
     return output.reshape(4, 32, 16, 256), grad.reshape(4, 32, 16, 256)
 
 

time: 83.9 us -> 75.3 us (0.90)
  Pallas kernels: 82.9 us -> 70.4 us
  local copies, waits for them, and re-layouts: 0 us -> 3.73 us
    pallas_call x1, Pallas kernels: 78.8 us -> 70.4 us  [shards(): pl.pallas_call(functools.partial(kernel, wide_count, narrow_count), out_s...]
    pallas_call x1 -> x0, Pallas kernels: 4.09 us -> none  [shards(): pl.pallas_call(finish, grid=(4,), out_shape=(jax.ShapeDtypeStruct((4, 512...]
    unnamed x0 -> x4, local copies, waits for them, and re-layouts: none -> 3.73 us
where the time goes in v3:
time: 75.3 us; the launch traced here: 74.8 us
  Pallas kernels  70.4 us (93%)
  local copies, waits for them, and re-layouts  3.73 us (5%)
    pallas_call x1, Pallas kernels, shards(): pl.pallas_call(functools.partial(kernel, wide_count, narrow_count), out_s...  70.4 us
    unnamed x4, local copies, waits for them, and re-layouts  3.73 us

profile of v3, /device:TPU:0, one launch (start us, length us, event | category | flops | bytes accessed | tf_op | source)
XLA Modules:
  0.0 74.8 jit_solution(4010115706969694453)
XLA Ops:
  0.6 70.4 %whole_net.1 = (bf16[4,512,256]{2,1,0:T(8,128)(2,1)}, f32[4,512,256]{2,1,0:T(8,128)}) custom-call(bf16[4,32,16,256]{3,2,1,0:T(8,128)(2,1)} %x_in.1, f32[1,256]{1,0:T(1,128)} %bitcast.15, bf16[9,256,256]{2,1,0:T(8,128)(2,1)} %bitcast.11, bf16[256,512]{1,0:T(8,128)(2,1)} %down_mid_in.1, f32[1,512]{1,0:T(1,128)} %bitcast.13, bf16[9,512,512]{2,1,0:T(8,128)(2,1)} %bitcast.8, ...), custom_call_target="tpu_custom_call" | custom-call | tf_op jit(solution)/shard_map/whole_net/pallas_call | solution.py:1005
  71.1 0.0 copy-start
  71.1 2.4 %copy.21 = bf16[4,32,16,256]{3,2,1,0:T(8,128)(2,1)} copy(bf16[4,32,16,256]{3,2,1,0:T(8,128)(2,1)} %bitcast.12) | data formatting | bytes 2097152
  73.5 0.0 copy-done
  73.5 1.3 %copy.22 = f32[4,32,16,256]{3,2,1,0:T(8,128)} copy(f32[4,32,16,256]{3,2,1,0:T(8,128)S(1)} %bitcast.10) | data formatting | bytes 4194304
Async XLA Ops:
  71.1 2.4 %copy-start = (f32[4,512,256]{2,1,0:T(8,128)S(1)}, f32[4,512,256]{2,1,0:T(8,128)}, u32[]{:S(2)}) copy-start(f32[4,512,256]{2,1,0:T(8,128)} %get-tuple-element.5) | copy-start | bytes 6291460

commit v4 on v3

--- a/solution.py
+++ b/solution.py
@@ -185,7 +185,7 @@
     fine_block,
     grad_buf,
     conv_grad,
-    pooled,
+    pooled_x,
     summed,
     fine_slope,
     edge_rows,
@@ -199,9 +199,9 @@
     first_matrix,
     second_matrix,
     window_sums,
-    slope_rows,
-    slope_sides,
-    slope_ends,
+    rim_rows,
+    rim_sides,
+    rim_ends,
     matrix_sum,
     stretched,
     col_pack,
@@ -253,6 +253,7 @@
         ("middle_table", middle_table_in, middle_table),
         ("narrow_table", narrow_table_in, narrow_table),
         ("gain_fine", gain_fine_in, gain_fine),
+        ("windows", windows_in, windows),
         ("kernel_fine", kernel_fine_in, kernel_fine),
         ("up_mid", up_mid_in, up_mid),
         ("up_coarse", up_coarse_in, up_coarse),
@@ -262,7 +263,6 @@
         ("kernel_mid", kernel_mid_in, kernel_mid),
         ("down_coarse", down_coarse_in, down_coarse),
         ("gain_coarse", gain_coarse_in, gain_coarse),
-        ("windows", windows_in, windows),
         ("stretch", stretch_in, stretch),
     )
     for number, (name, source, target) in enumerate(pairs):
@@ -446,7 +446,10 @@
         send(xg.at[which, :, 31], row_in.at[0, which], sem, 1, 0)
         send(xg.at[which, :, 0], row_in.at[1, which], sem, -1, 0)
         for f in range(4):
-            picked = dot(PICK[...], frame(which, f)).astype(BF16)
+            picked = dot(PICK[...], frame(which, f))
+            if which == 0:
+                pooled_x[32 * f : 32 * f + 32] = picked[0:32]
+            picked = picked.astype(BF16)
             col_pack[0, which, 32 * f : 32 * f + 32] = picked[32:64]
             col_pack[1, which, 32 * f : 32 * f + 32] = picked[64:96]
             if which == 1:
@@ -545,32 +548,61 @@
     def fine_scaled(value):
         return (value - fine_center) * fine_inverse
 
-    set_edges(
-        fine_act(row_in[0, 0].astype(F32)),
-        fine_act(row_in[1, 0].astype(F32)),
-        fine_act(col_in[0, 0].astype(F32)),
-        fine_act(col_in[1, 0].astype(F32)),
-        corners(lambda c: cor_in[0, c], fine_act, True),
-    )
-
     def fine_value(f):
         return frame(0, f).astype(F32)
 
+    def set_fields(n, change):
+        for k in range(2):
+            rim_rows[n, k] = only(exists[1 + k], change(row_in[k, 0].astype(F32))).astype(BF16)
+            sides = only(exists[3 + k], change(col_in[k, 0].astype(F32))).astype(BF16)
+            rim_sides[n, k] = sides.reshape(4, 32, 256)
+        ends = corners(lambda c: cor_in[0, c], change, True)
+        ends = dot(BY_FRAME[:, 0:16], ends.astype(BF16)).astype(BF16)
+        rim_ends[n] = ends.reshape(4, 32, 256)
+
+    def window(n, f, own):
+        field = jnp.concatenate(
+            [
+                own.astype(BF16),
+                rim_rows[n, 0, f],
+                rim_rows[n, 1, f],
+                rim_sides[n, 0, f],
+                rim_sides[n, 1, f],
+                rim_ends[n, f],
+            ],
+            axis=0,
+        )
+        return dot(windows[...], field)
+
+    set_fields(0, fine_act)
+    loads["windows"].wait()
+
     @pl.loop(0, 4)
     def _(f):
+        sums = window(0, f, fine_act(fine_value(f)))
+        high, low = halves(sums)
+        window_sums[0, :, f] = high.reshape(9, 32, 256)
+        window_sums[1, :, f] = low.reshape(9, 32, 256)
+
+    pooled = pooled_x[...]
+    for t in range(9):
+        both = jnp.concatenate(
+            [window_sums[0, t].reshape(128, 256), window_sums[1, t].reshape(128, 256)], axis=0
+        )
+        both = dot(both, kernel_fine[8 - t])
+        pooled += both[0:128] + both[128:256]
+    pooled = (pooled * 0.0625).astype(BF16)
+
+    def fine_forward(f):
         value = fine_value(f)
         place(f, fine_act(value))
-        block = (value + fine_convolve(f)).astype(BF16)
-        fine_block[f] = block
-        pooled[pl.ds(pl.multiple_of(32 * f, 32), 32), :] = (
-            dot(PICK[0:32, :], block) * 0.0625
-        ).astype(BF16)
+        fine_block[f] = (value + fine_convolve(f)).astype(BF16)
 
     def same(value):
         return value
 
     loads["down_mid"].wait()
-    mid_in = dot(pooled[...], down_mid[...]).astype(BF16)
+    mid_in = dot(pooled, down_mid[...]).astype(BF16)
     mid_value = mid_in.astype(F32)
 
     def column_sums(value):
@@ -584,22 +616,10 @@
     def _(f):
         fine_slope[f] = slope(fine_scaled(fine_value(f)), s_fine)
 
-    def pair_of(value, condition):
-        scaled = fine_scaled(value.astype(F32))
-        bent = slope(scaled, s_fine)
-        if condition is not None:
-            bent = only(condition, bent)
-        return bent.astype(BF16), (bent * scaled).astype(BF16)
-
-    for k in range(2):
-        for n, value in enumerate(pair_of(row_in[k, 0], exists[1 + k])):
-            slope_rows[n, k] = value
-        for n, value in enumerate(pair_of(col_in[k, 0], exists[3 + k])):
-            slope_sides[n, k] = value.reshape(4, 32, 256)
-    bent = corners(lambda c: cor_in[0, c], lambda v: slope(fine_scaled(v), s_fine), True)
-    scaled = corners(lambda c: cor_in[0, c], fine_scaled, False)
-    for n, value in enumerate((bent, bent * scaled)):
-        slope_ends[n] = dot(BY_FRAME[:, 0:16], value.astype(BF16)).astype(BF16).reshape(4, 32, 256)
+    set_fields(0, lambda v: slope(fine_scaled(v), s_fine))
+    set_fields(1, lambda v: slope(fine_scaled(v), s_fine) * fine_scaled(v))
+
+    total_middle(1)
 
     up_mid_grad = summed[...]
     sum_pack[...] = dot(PACK[...], up_mid_grad).astype(BF16)
@@ -610,7 +630,13 @@
     loads["up_coarse"].wait()
     cgrad_own[...] = dot_t(up_coarse_grad, up_coarse[...]).astype(BF16)
     send_coarse(cgrad_own, cgrad_in, 5)
-    total_middle(1)
+
+    @pl.loop(0, 4)
+    def _(f):
+        bent = fine_slope[f]
+        window_sums[0, :, f] = window(0, f, bent).astype(BF16).reshape(9, 32, 256)
+        bent = bent * fine_scaled(fine_value(f))
+        window_sums[1, :, f] = window(1, f, bent).astype(BF16).reshape(9, 32, 256)
 
     loads["gain_mid"].wait()
     loads["kernel_mid"].wait()
@@ -711,27 +737,6 @@
     coarse_u[...] = cgrad + coarse_inverse * normed_grad
     send_coarse(coarse_u, coarse_u_halo, 9)
     grad_sums = lax.fori_loop(2, 4, convolve_grad, grad_sums)
-
-    loads["windows"].wait()
-
-    @pl.loop(0, 4)
-    def _(f):
-        for n in range(2):
-            bent = fine_slope[f]
-            if n == 1:
-                bent = bent * fine_scaled(fine_value(f))
-            field = jnp.concatenate(
-                [
-                    bent.astype(BF16),
-                    slope_rows[n, 0, f],
-                    slope_rows[n, 1, f],
-                    slope_sides[n, 0, f],
-                    slope_sides[n, 1, f],
-                    slope_ends[n, f],
-                ],
-                axis=0,
-            )
-            window_sums[n, :, f] = dot(windows[...], field).astype(BF16).reshape(9, 32, 256)
 
     total_middle(3)
 
@@ -805,6 +810,18 @@
     total_send_wide(4)
     total_middle(5)
 
+    set_edges(
+        fine_act(row_in[0, 0].astype(F32)),
+        fine_act(row_in[1, 0].astype(F32)),
+        fine_act(col_in[0, 0].astype(F32)),
+        fine_act(col_in[1, 0].astype(F32)),
+        corners(lambda c: cor_in[0, c], fine_act, True),
+    )
+
+    @pl.loop(0, 2)
+    def _(f):
+        fine_forward(f)
+
     coarse_block = (
         coarse_in.astype(F32)
         + coarse_convolve(
@@ -821,6 +838,10 @@
     mid_sum = (mid_block.astype(F32) + dot(SPREAD[0:128, 0:16], coarse_up)).astype(BF16)
     mid_up = dot(mid_sum, up_mid[...]).astype(BF16)
     total_middle(4)
+
+    @pl.loop(2, 4)
+    def _(f):
+        fine_forward(f)
 
     mid_up = dot(ENLARGE[:, 0:128], mid_up).reshape(4, 8, 1, 16, 256)
     for f in range(4):
@@ -956,7 +977,7 @@
         vmem((4, 512, 256), BF16),
         vmem((4, 512, 256), F32),
         vmem((4, 512, 256), F32),
-        vmem((128, 256), BF16),
+        vmem((128, 256), F32),
         vmem((128, 256), BF16),
         vmem((4, 512, 256), F32),
         vmem((2, 4, 16, 256), F32),

time: 75.3 us -> 75.1 us (level)
  no operation moved by 1% of the time
where the time goes in v4:
time: 75.1 us; the launch traced here: 74.6 us
  Pallas kernels  70.2 us (93%)
  local copies, waits for them, and re-layouts  3.73 us (5%)
    pallas_call x1, Pallas kernels, shards(): pl.pallas_call(functools.partial(kernel, wide_count, narrow_count), out_s...  70.2 us
    unnamed x4, local copies, waits for them, and re-layouts  3.73 us

profile of v4, /device:TPU:0, one launch (start us, length us, event | category | flops | bytes accessed | tf_op | source)
XLA Modules:
  0.0 74.6 jit_solution(12082082287374320990)
XLA Ops:
  0.6 70.2 %whole_net.1 = (bf16[4,512,256]{2,1,0:T(8,128)(2,1)}, f32[4,512,256]{2,1,0:T(8,128)}) custom-call(bf16[4,32,16,256]{3,2,1,0:T(8,128)(2,1)} %x_in.1, f32[1,256]{1,0:T(1,128)} %bitcast.15, bf16[9,256,256]{2,1,0:T(8,128)(2,1)} %bitcast.11, bf16[256,512]{1,0:T(8,128)(2,1)} %down_mid_in.1, f32[1,512]{1,0:T(1,128)} %bitcast.13, bf16[9,512,512]{2,1,0:T(8,128)(2,1)} %bitcast.8, ...), custom_call_target="tpu_custom_call" | custom-call | tf_op jit(solution)/shard_map/whole_net/pallas_call | solution.py:1026
  70.9 0.0 copy-start
  70.9 2.4 %copy.21 = bf16[4,32,16,256]{3,2,1,0:T(8,128)(2,1)} copy(bf16[4,32,16,256]{3,2,1,0:T(8,128)(2,1)} %bitcast.12) | data formatting | bytes 2097152
  73.3 0.0 copy-done
  73.3 1.3 %copy.22 = f32[4,32,16,256]{3,2,1,0:T(8,128)} copy(f32[4,32,16,256]{3,2,1,0:T(8,128)S(1)} %bitcast.10) | data formatting | bytes 4194304
Async XLA Ops:
  70.9 2.4 %copy-start = (f32[4,512,256]{2,1,0:T(8,128)S(1)}, f32[4,512,256]{2,1,0:T(8,128)}, u32[]{:S(2)}) copy-start(f32[4,512,256]{2,1,0:T(8,128)} %get-tuple-element.5) | copy-start | bytes 6291460

commit v5 on v4

--- a/solution.py
+++ b/solution.py
@@ -179,8 +179,6 @@
     narrow_table,
     windows,
     stretch,
-    taps_buf,
-    coarse_taps,
     columns,
     fine_block,
     grad_buf,
@@ -194,8 +192,7 @@
     summed_grad,
     first,
     second,
-    first_joint,
-    second_joint,
+    rows,
     first_matrix,
     second_matrix,
     window_sums,
@@ -203,6 +200,7 @@
     rim_sides,
     rim_ends,
     matrix_sum,
+    through,
     stretched,
     col_pack,
     cor_pack,
@@ -296,8 +294,8 @@
     def sent(buffer, which):
         pltpu.make_async_copy(buffer, buffer, halo_send.at[which]).wait()
 
-    firsts = tuple(first.at[p] for p in range(4)) + (first_joint, first_matrix)
-    seconds = tuple(second.at[p] for p in range(4)) + (second_joint, second_matrix)
+    firsts = tuple(first.at[p] for p in range(6)) + (first_matrix,)
+    seconds = tuple(second.at[p] for p in range(6)) + (second_matrix,)
 
     def total_send_wide(phase):
         mine = firsts[phase].at[wide]
@@ -313,22 +311,27 @@
                 device_id_type=MESH,
             ).start()
 
-    def total_fill(phase, start, values):
-        for n, value in enumerate(values):
-            for k in range(value.shape[1] // 128):
-                at = start + 4 * n + k
-                firsts[phase][wide, at : at + 1, :] = value[:, 128 * k : 128 * k + 128]
+    def diagonal(shape=(8, 128)):
+        lane = lax.broadcasted_iota(jnp.int32, shape, 1) & 7
+        return lane == lax.broadcasted_iota(jnp.int32, shape, 0)
 
     def total_begin(phase, one, two):
-        if one.shape[1] < 512:
-            firsts[phase][wide] = jnp.zeros((8, 128), F32)
-        total_fill(phase, 0, (one, two))
+        channels = one.shape[1]
+        if channels < 512:
+            rows[...] = jnp.zeros((8, 128), F32)
+        for n, value in enumerate((one, two)):
+            for k in range(channels // 128):
+                rows[4 * n + k : 4 * n + k + 1, :] = value[:, 128 * k : 128 * k + 128]
+        grouped = group_lanes(rows[...], channels // GROUPS)
+        grouped = jnp.where(diagonal(), grouped, 0.0)
+        firsts[phase][wide] = jnp.sum(grouped, axis=0, keepdims=True)
         total_send_wide(phase)
 
     def total_middle(phase):
         whole = firsts[phase].at[pl.ds(0, wide_count - 1)]
         pltpu.make_async_copy(whole, whole, total_recv.at[2 * phase]).wait()
-        seconds[phase][narrow] = jnp.sum(firsts[phase][...], axis=0)
+        summed_up = jnp.sum(firsts[phase][...].astype(F32), axis=0)
+        seconds[phase][narrow] = summed_up.astype(seconds[phase].dtype)
         mine = seconds[phase].at[narrow]
 
         @pl.loop(1, narrow_count)
@@ -345,15 +348,18 @@
     def total_sum(phase):
         whole = seconds[phase].at[pl.ds(0, narrow_count - 1)]
         pltpu.make_async_copy(whole, whole, total_recv.at[2 * phase + 1]).wait()
-        return jnp.sum(seconds[phase][...], axis=0)
+        return jnp.sum(seconds[phase][...].astype(F32), axis=0)
 
     def row_of(t, start, channels):
         return jnp.concatenate([t[start + k : start + k + 1] for k in range(channels // 128)], axis=1)
 
+    def total_groups(phase, channels, scale):
+        packed = jnp.broadcast_to(total_sum(phase), (8, 128))
+        t = group_lanes(jnp.where(diagonal(), packed, 0.0), 8) * scale
+        return row_of(t, 0, channels), row_of(t, 4, channels)
+
     def total_end(phase, channels, cells):
-        size = channels // GROUPS
-        t = group_lanes(total_sum(phase), size) * (1.0 / (size * cells))
-        return row_of(t, 0, channels), row_of(t, 4, channels)
+        return total_groups(phase, channels, 1.0 / (channels // GROUPS * cells))
 
     has_above, has_below = wide > 0, wide < wide_count - 1
     has_left, has_right = narrow > 0, narrow < narrow_count - 1
@@ -469,8 +475,24 @@
     loads["grad"].wait()
     rim(1)
     loads["narrow_table"].wait()
+
+    up_mid_grad = summed[...]
+    sum_pack[...] = dot(PACK[...], up_mid_grad).astype(BF16)
+    send_mid(sum_pack, sum_in, sum_cor, 3)
+    loads["up_mid"].wait()
+    high, low = halves(dot_t(up_mid_grad, up_mid[...]))
+    up_coarse_grad = (dot(POOL[...], high) + dot(POOL[...], low)).astype(BF16)
+    loads["up_coarse"].wait()
+    cgrad_own[...] = dot_t(up_coarse_grad, up_coarse[...]).astype(BF16)
+    send_coarse(cgrad_own, cgrad_in, 5)
+
     loads["gain_fine"].wait()
     loads["kernel_fine"].wait()
+    loads["down_mid"].wait()
+
+    @pl.loop(0, 9)
+    def _(t):
+        through[t] = (0.0625 * dot(kernel_fine[8 - t], down_mid[...])).astype(BF16)
 
     fine_center, fine_square = total_end(0, 256, 2048 * wide_count * narrow_count)
     fine_inverse = lax.rsqrt(fine_square - fine_center * fine_center + epsilon)
@@ -497,19 +519,19 @@
     arrived(col_in.at[:, 0], 1)
     arrived(cor_in.at[0], 2)
 
-    def set_edges(above, below, left, right, ends):
-        edge_rows[0] = only(has_above, above)
-        edge_rows[1] = only(has_below, below)
+    def set_edges(kind, above, below, left, right, ends):
+        edge_rows[kind, 0] = only(has_above, above)
+        edge_rows[kind, 1] = only(has_below, below)
         left = only(has_left, left).astype(BF16)
         right = only(has_right, right).astype(BF16)
         for f in range(4):
-            edge_sides[f, 0:32] = left[32 * f : 32 * f + 32]
-            edge_sides[f, 32:64] = right[32 * f : 32 * f + 32]
-        edge_ends[...] = ends
-
-    def place(f, own):
+            edge_sides[kind, f, 0:32] = left[32 * f : 32 * f + 32]
+            edge_sides[kind, f, 32:64] = right[32 * f : 32 * f + 32]
+        edge_ends[kind] = ends
+
+    def place(kind, f, own):
         column = lax.broadcasted_iota(jnp.int32, (512, 256), 0) & 15
-        sides = edge_sides[f]
+        sides = edge_sides[kind, f]
         low = jnp.where(
             column == 0, dot(SIDES[:, 0:64], sides), pltpu.roll(own, 1, 0)
         )
@@ -521,29 +543,25 @@
         columns[f, 16:528, 512:768] = high.astype(BF16)
         cell = lax.broadcasted_iota(jnp.int32, (16, 256), 0)
         for k in range(2):
-            row = edge_rows[k, f]
+            row = edge_rows[kind, k, f]
             at = slice(528 * k, 528 * k + 16)
-            west = edge_ends[pl.ds(8 * k + f, 1), :]
-            east = edge_ends[pl.ds(8 * k + 4 + f, 1), :]
+            west = edge_ends[kind, pl.ds(8 * k + f, 1), :]
+            east = edge_ends[kind, pl.ds(8 * k + 4 + f, 1), :]
             columns[f, at, 0:256] = jnp.where(cell == 0, west, pltpu.roll(row, 1, 0)).astype(BF16)
             columns[f, at, 256:512] = row.astype(BF16)
             columns[f, at, 512:768] = jnp.where(cell == 15, east, pltpu.roll(row, 15, 0)).astype(BF16)
 
+    def side_by_side(pieces):
+        return jnp.concatenate(list(pieces), axis=1)
+
+    def fine_taps(f):
+        return side_by_side(columns[f, 16 * a : 16 * a + 512, :] for a in range(3))
+
     def fine_convolve(f):
-        total = dot(columns[f, 0:512, :], kernel_fine[0:3].reshape(768, 256))
-        total += dot(columns[f, 16:528, :], kernel_fine[3:6].reshape(768, 256))
-        return total + dot(columns[f, 32:544, :], kernel_fine[6:9].reshape(768, 256))
+        return dot(fine_taps(f), kernel_fine[...].reshape(2304, 256))
 
     def fine_convolve_back(f):
-        total = None
-        for a in range(3):
-            for b in range(3):
-                term = dot_t(
-                    columns[f, 16 * a : 16 * a + 512, 256 * b : 256 * b + 256],
-                    kernel_fine[8 - 3 * a - b],
-                )
-                total = term if total is None else total + term
-        return total
+        return dot_t(fine_taps(f), side_by_side(kernel_fine[8 - t] for t in range(9)))
 
     def fine_scaled(value):
         return (value - fine_center) * fine_inverse
@@ -584,24 +602,22 @@
         window_sums[0, :, f] = high.reshape(9, 32, 256)
         window_sums[1, :, f] = low.reshape(9, 32, 256)
 
-    pooled = pooled_x[...]
-    for t in range(9):
-        both = jnp.concatenate(
-            [window_sums[0, t].reshape(128, 256), window_sums[1, t].reshape(128, 256)], axis=0
-        )
-        both = dot(both, kernel_fine[8 - t])
-        pooled += both[0:128] + both[128:256]
+    both = side_by_side(
+        jnp.concatenate([window_sums[n, 8 - t].reshape(128, 256) for n in range(2)], axis=0)
+        for t in range(9)
+    )
+    both = dot(both, kernel_fine[...].reshape(2304, 256))
+    pooled = pooled_x[...] + both[0:128] + both[128:256]
     pooled = (pooled * 0.0625).astype(BF16)
 
     def fine_forward(f):
         value = fine_value(f)
-        place(f, fine_act(value))
+        place(0, f, fine_act(value))
         fine_block[f] = (value + fine_convolve(f)).astype(BF16)
 
     def same(value):
         return value
 
-    loads["down_mid"].wait()
     mid_in = dot(pooled, down_mid[...]).astype(BF16)
     mid_value = mid_in.astype(F32)
 
@@ -619,17 +635,17 @@
     set_fields(0, lambda v: slope(fine_scaled(v), s_fine))
     set_fields(1, lambda v: slope(fine_scaled(v), s_fine) * fine_scaled(v))
 
+    set_edges(
+        0,
+        fine_act(row_in[0, 0].astype(F32)),
+        fine_act(row_in[1, 0].astype(F32)),
+        fine_act(col_in[0, 0].astype(F32)),
+        fine_act(col_in[1, 0].astype(F32)),
+        corners(lambda c: cor_in[0, c], fine_act, True),
+    )
+    fine_forward(0)
     total_middle(1)
-
-    up_mid_grad = summed[...]
-    sum_pack[...] = dot(PACK[...], up_mid_grad).astype(BF16)
-    send_mid(sum_pack, sum_in, sum_cor, 3)
-    loads["up_mid"].wait()
-    high, low = halves(dot_t(up_mid_grad, up_mid[...]))
-    up_coarse_grad = (dot(POOL[...], high) + dot(POOL[...], low)).astype(BF16)
-    loads["up_coarse"].wait()
-    cgrad_own[...] = dot_t(up_coarse_grad, up_coarse[...]).astype(BF16)
-    send_coarse(cgrad_own, cgrad_in, 5)
+    fine_forward(1)
 
     @pl.loop(0, 4)
     def _(f):
@@ -649,13 +665,9 @@
     def mid_scaled(value):
         return (value - mid_center) * mid_inverse
 
-    def mid_convolve(extended, weights):
-        taps_buf[...] = dot(TAPS[...], extended.astype(BF16)).astype(BF16).reshape(9, 128, 512)
-        total = None
-        for t in range(9):
-            term = weights(t, taps_buf[t])
-            total = term if total is None else total + term
-        return total
+    def mid_convolve(extended, product, weights):
+        taps = dot(TAPS[...], extended.astype(BF16)).astype(BF16)
+        return product(side_by_side(taps[128 * t : 128 * t + 128] for t in range(9)), weights)
 
     arrived(mid_halo, 6)
     arrived(mid_cor, 7)
@@ -663,7 +675,8 @@
         mid_value
         + mid_convolve(
             mid_extended(mid_value, mid_halo[...], lambda c: mid_cor[c], mid_act, True),
-            lambda t, part_: dot(part_, kernel_mid[t]),
+            dot,
+            kernel_mid[...].reshape(4608, 512),
         )
     ).astype(BF16)
 
@@ -679,6 +692,7 @@
     arrived(col_in.at[:, 1], 14)
     arrived(cor_in.at[1], 15)
     set_edges(
+        1,
         row_in[0, 1].astype(F32),
         row_in[1, 1].astype(F32),
         col_in[0, 1].astype(F32),
@@ -687,7 +701,7 @@
     )
 
     def convolve_grad(f, carry):
-        place(f, frame(1, f).astype(F32))
+        place(1, f, frame(1, f).astype(F32))
         result = fine_convolve_back(f)
         conv_grad[f] = result
         weighted = result * fine_slope[f]
@@ -703,17 +717,15 @@
     arrived(cgrad_in, 5)
     loads["kernel_coarse"].wait()
 
-    def coarse_convolve(extended, weights):
-        spread_out = dot(COARSE_TAPS[...], extended.astype(BF16)).astype(BF16)
-        coarse_taps[...] = spread_out.reshape(9, 16, 512)
-        return lax.fori_loop(
-            0, 9, lambda t, total: total + weights(t, coarse_taps[t]), jnp.zeros((16, 512), F32)
-        )
+    def coarse_convolve(extended, product, weights):
+        taps = dot(COARSE_TAPS[...], extended.astype(BF16)).astype(BF16)
+        return product(side_by_side(taps[16 * t : 16 * t + 16] for t in range(9)), weights)
 
     cgrad = cgrad_own[...].astype(F32)[0:8]
     coarse_act_grad = coarse_convolve(
         coarse_extended(cgrad, lambda d: cgrad_in[d].astype(F32)[0:8], same, True),
-        lambda t, part_: dot_t(part_, kernel_coarse[8 - t]),
+        dot_t,
+        side_by_side(kernel_coarse[8 - t] for t in range(9)),
     )[0:8]
 
     arrived(sum_in, 3)
@@ -747,12 +759,12 @@
 
     @pl.loop(0, 9)
     def _(t):
-        through = 0.0625 * dot(kernel_fine[8 - t], down_mid[...])
+        weight = through[t].astype(F32)
         for n in range(2):
             mixed = dot_first(window_sums[n, t].reshape(128, 256), mid_mix)
             plain = jnp.concatenate([mixed[:, 512:640]] * 4, axis=1)
-            matrix_sum[2 * n] += through * plain
-            matrix_sum[2 * n + 1] += through * mixed[:, 0:512]
+            matrix_sum[2 * n] += weight * plain
+            matrix_sum[2 * n + 1] += weight * mixed[:, 0:512]
 
     def iota(shape, axis):
         return lax.broadcasted_iota(jnp.int32, shape, axis)
@@ -767,8 +779,8 @@
         high, low = halves(dot(by_group, high) + dot(by_group, low))
         to_lane = one_hot(iota((512, 128), 1) == 32 * n + (iota((512, 128), 0) >> 4))
         matrix += dot(high, to_lane) + dot(low, to_lane)
-    first_matrix[wide] = matrix
-    total_send_wide(5)
+    first_matrix[wide] = matrix.astype(BF16)
+    total_send_wide(6)
 
     first_mean, second_mean = total_end(3, 512, 8 * wide_count * narrow_count)
     arrived(coarse_halo, 8)
@@ -792,9 +804,12 @@
         inside = jnp.logical_and(row >= start, row < start + size)
         keep = jnp.where(inside, jnp.where(exists[d], 1.0, 0.0).astype(F32), keep)
     mid_grad = (summed_grad[...] + 0.0625 * mid_pool_grad) * jnp.concatenate([keep] * 4, axis=1)
-    mid_act_grad = mid_convolve(mid_grad, lambda t, part_: dot_t(part_, kernel_mid[8 - t]))
+    mid_act_grad = mid_convolve(
+        mid_grad, dot_t, side_by_side(kernel_mid[8 - t] for t in range(9))
+    )
     scaled = mid_scaled(mid_value)
     normed_grad = mid_act_grad * slope(scaled, s_mid)
+    total_begin(4, column_sums(normed_grad), column_sums(normed_grad * scaled))
     mid_u = mid_grad[0:128].astype(BF16).astype(F32) + mid_inverse * normed_grad
     u_pack[...] = dot(PACK[...], mid_u.astype(BF16)).astype(BF16)
     send_mid(u_pack, u_halo, u_cor, 10)
@@ -804,24 +819,10 @@
         term = dot_t(pulled, kernel_fine[8 - t])
         for n in range(2):
             fine_sums[n] += column_sums(window_sums[n, t].reshape(128, 256).astype(F32) * term)
-    first_joint[wide, 8:16, :] = jnp.zeros((8, 128), F32)
-    total_fill(4, 0, (column_sums(normed_grad), column_sums(normed_grad * scaled)))
-    total_fill(4, 8, fine_sums)
-    total_send_wide(4)
-    total_middle(5)
-
-    set_edges(
-        fine_act(row_in[0, 0].astype(F32)),
-        fine_act(row_in[1, 0].astype(F32)),
-        fine_act(col_in[0, 0].astype(F32)),
-        fine_act(col_in[1, 0].astype(F32)),
-        corners(lambda c: cor_in[0, c], fine_act, True),
-    )
-
-    @pl.loop(0, 2)
-    def _(f):
-        fine_forward(f)
-
+    total_begin(5, *fine_sums)
+    total_middle(6)
+
+    fine_forward(2)
     coarse_block = (
         coarse_in.astype(F32)
         + coarse_convolve(
@@ -831,29 +832,24 @@
                 silu(coarse_center, coarse_inverse, s_coarse),
                 True,
             ),
-            lambda t, part_: dot(part_, kernel_coarse[t]),
+            dot,
+            kernel_coarse[...].reshape(4608, 512),
         )
     ).astype(BF16)
     coarse_up = dot(coarse_block, up_coarse[...]).astype(BF16)
     mid_sum = (mid_block.astype(F32) + dot(SPREAD[0:128, 0:16], coarse_up)).astype(BF16)
     mid_up = dot(mid_sum, up_mid[...]).astype(BF16)
     total_middle(4)
-
-    @pl.loop(2, 4)
-    def _(f):
-        fine_forward(f)
-
+    total_middle(5)
+
+    fine_forward(3)
     mid_up = dot(ENLARGE[:, 0:128], mid_up).reshape(4, 8, 1, 16, 256)
     for f in range(4):
         block = fine_block[f].astype(F32).reshape(8, 4, 16, 256)
         fine_block[f] = (block + mid_up[f]).astype(BF16).reshape(512, 256)
     out_copy = pltpu.make_async_copy(fine_block, out_ref, out_sem.at[0])
     out_copy.start()
-    matrix = total_sum(5)
-
-    joint = total_sum(4)
-    t = group_lanes(joint[0:8], 16) * (1.0 / (16 * 128 * wide_count * narrow_count))
-    first_mean, second_mean = row_of(t, 0, 512), row_of(t, 4, 512)
+    first_mean, second_mean = total_end(4, 512, 128 * wide_count * narrow_count)
     arrived(u_halo, 10)
     arrived(u_cor, 11)
     offset = mid_inverse * first_mean
@@ -880,9 +876,9 @@
         to_lane = jnp.where(inside, 0.0625, 0.0).astype(BF16)
         high, low = halves(jnp.broadcast_to(mean, (8, 512)))
         means += dot(high, to_lane) + dot(low, to_lane)
-    matrix_high, matrix_low = halves(matrix)
+    matrix_high, matrix_low = halves(total_sum(6))
+    fine_totals = total_groups(5, 256, 1.0)
     spread_groups = one_hot((iota((256, 32), 0) >> 3) == iota((256, 32), 1))
-    t = group_lanes(joint[8:16], 8)
     fine_means = []
     for n in range(2):
         half = jnp.where((iota((8, 128), 1) >> 6) == n, means, 0.0)
@@ -891,7 +887,7 @@
         high, low = halves(change)
         change = dot_t(high, spread_groups) + dot_t(low, spread_groups)
         fine_means.append(
-            (row_of(t, 4 * n, 256) - change[0:1]) * (1.0 / (8 * 2048 * wide_count * narrow_count))
+            (fine_totals[n] - change[0:1]) * (1.0 / (8 * 2048 * wide_count * narrow_count))
         )
     slant = -fine_inverse * fine_inverse * fine_means[1]
     shift = -fine_inverse * fine_means[0] - fine_center * slant
@@ -926,7 +922,7 @@
     sent(coarse_u_halo, 9)
     sent(u_halo, 10)
     sent(u_cor, 11)
-    for phase in range(6):
+    for phase in range(7):
         whole = firsts[phase].at[pl.ds(0, wide_count - 1)]
         pltpu.make_async_copy(whole, whole, total_send.at[2 * phase]).wait()
         whole = seconds[phase].at[pl.ds(0, narrow_count - 1)]
@@ -971,8 +967,6 @@
         vmem((1168, 128), BF16),
         vmem((288, 640), BF16),
         vmem((640, 768), BF16),
-        vmem((9, 128, 512), BF16),
-        vmem((9, 16, 512), BF16),
         vmem((4, 544, 768), BF16),
         vmem((4, 512, 256), BF16),
         vmem((4, 512, 256), F32),
@@ -980,21 +974,21 @@
         vmem((128, 256), F32),
         vmem((128, 256), BF16),
         vmem((4, 512, 256), F32),
-        vmem((2, 4, 16, 256), F32),
-        vmem((4, 64, 256), BF16),
-        vmem((16, 256), F32),
+        vmem((2, 2, 4, 16, 256), F32),
+        vmem((2, 4, 64, 256), BF16),
+        vmem((2, 16, 256), F32),
         vmem((256, 512), F32),
-        vmem((4, wide_count, 8, 128), F32),
-        vmem((4, narrow_count, 8, 128), F32),
-        vmem((wide_count, 16, 128), F32),
-        vmem((narrow_count, 16, 128), F32),
-        vmem((wide_count, 32, 128), F32),
-        vmem((narrow_count, 32, 128), F32),
+        vmem((6, wide_count, 1, 128), F32),
+        vmem((6, narrow_count, 1, 128), F32),
+        vmem((8, 128), F32),
+        vmem((wide_count, 32, 128), BF16),
+        vmem((narrow_count, 32, 128), BF16),
         vmem((2, 9, 4, 32, 256), BF16),
         vmem((2, 2, 4, 16, 256), BF16),
         vmem((2, 2, 4, 32, 256), BF16),
         vmem((2, 4, 32, 256), BF16),
         vmem((4, 256, 512), F32),
+        vmem((9, 256, 512), BF16),
         vmem((3, 4, 10, 16, 256), F32),
         vmem((2, 2, 128, 256), BF16),
         vmem((2, 16, 256), BF16),
@@ -1018,8 +1012,8 @@
         vmem((4, 16, 512), BF16),
         pltpu.SemaphoreType.DMA((17,)),
         pltpu.SemaphoreType.DMA((5,)),
-        pltpu.SemaphoreType.DMA((12,)),
-        pltpu.SemaphoreType.DMA((12,)),
+        pltpu.SemaphoreType.DMA((14,)),
+        pltpu.SemaphoreType.DMA((14,)),
         pltpu.SemaphoreType.DMA((16,)),
         pltpu.SemaphoreType.DMA((16,)),
     ]

time: 75.1 us -> 71.2 us (0.948)
  Pallas kernels: 70.2 us -> 66.7 us
    pallas_call x1, Pallas kernels: 70.2 us -> 66.7 us  [shards(): pl.pallas_call(functools.partial(kernel, wide_count, narrow_count), out_s...]
where the time goes in v5:
time: 71.2 us; the launch traced here: 71.1 us
  Pallas kernels  66.7 us (94%)
  local copies, waits for them, and re-layouts  3.73 us (5%)
    pallas_call x1, Pallas kernels, shards(): pl.pallas_call(functools.partial(kernel, wide_count, narrow_count), out_s...  66.7 us
    unnamed x4, local copies, waits for them, and re-layouts  3.73 us

profile of v5, /device:TPU:0, one launch (start us, length us, event | category | flops | bytes accessed | tf_op | source)
XLA Modules:
  0.0 71.1 jit_solution(16367447183807764308)
XLA Ops:
  0.6 66.7 %whole_net.1 = (bf16[4,512,256]{2,1,0:T(8,128)(2,1)}, f32[4,512,256]{2,1,0:T(8,128)}) custom-call(bf16[4,32,16,256]{3,2,1,0:T(8,128)(2,1)} %x_in.1, f32[1,256]{1,0:T(1,128)} %bitcast.15, bf16[9,256,256]{2,1,0:T(8,128)(2,1)} %bitcast.11, bf16[256,512]{1,0:T(8,128)(2,1)} %down_mid_in.1, f32[1,512]{1,0:T(1,128)} %bitcast.13, bf16[9,512,512]{2,1,0:T(8,128)(2,1)} %bitcast.8, ...), custom_call_target="tpu_custom_call" | custom-call | tf_op jit(solution)/shard_map/whole_net/pallas_call | solution.py:1020
  67.3 0.0 copy-start
  67.4 2.4 %copy.21 = bf16[4,32,16,256]{3,2,1,0:T(8,128)(2,1)} copy(bf16[4,32,16,256]{3,2,1,0:T(8,128)(2,1)} %bitcast.12) | data formatting | bytes 2097152
  69.8 0.0 copy-done
  69.8 1.3 %copy.22 = f32[4,32,16,256]{3,2,1,0:T(8,128)} copy(f32[4,32,16,256]{3,2,1,0:T(8,128)S(1)} %bitcast.10) | data formatting | bytes 4194304
Async XLA Ops:
  67.3 2.4 %copy-start = (f32[4,512,256]{2,1,0:T(8,128)S(1)}, f32[4,512,256]{2,1,0:T(8,128)}, u32[]{:S(2)}) copy-start(f32[4,512,256]{2,1,0:T(8,128)} %get-tuple-element.5) | copy-start | bytes 6291460

commit v6 on v5

--- a/solution.py
+++ b/solution.py
@@ -245,7 +245,10 @@
 
     loads = {}
     pairs = (
-        ("x", x_in, xg.at[0]),
+        ("x0", x_in.at[0], xg.at[0, 0]),
+        ("x1", x_in.at[1], xg.at[0, 1]),
+        ("x2", x_in.at[2], xg.at[0, 2]),
+        ("x3", x_in.at[3], xg.at[0, 3]),
         ("grad", grad_in, xg.at[1]),
         ("wide_table", wide_table_in, wide_table),
         ("middle_table", middle_table_in, middle_table),
@@ -265,7 +268,12 @@
     )
     for number, (name, source, target) in enumerate(pairs):
         loads[name] = pltpu.make_async_copy(source, target, load_sem.at[number])
-    loads["x"].start()
+
+    def begin_loads(*names):
+        for name in names:
+            loads[name].start()
+
+    begin_loads("x0", "x1", "x2", "x3", "wide_table", "middle_table")
 
     barrier = pltpu.get_barrier_semaphore()
     greeted = 0
@@ -430,22 +438,18 @@
     def frame(which, f):
         return xg[which, f].reshape(512, 256)
 
-    loads["x"].wait()
-    for name in loads:
-        if name != "x":
-            loads[name].start()
-
-    def add_frame(f, carry):
+    blank = jnp.zeros((8, 256), F32)
+    one, two = blank, blank
+    for f in range(4):
+        loads["x%d" % f].wait()
         value = frame(0, f).astype(F32)
-        return (
-            carry[0] + jnp.sum(value.reshape(64, 8, 256), axis=0),
-            carry[1] + jnp.sum((value * value).reshape(64, 8, 256), axis=0),
-        )
-
-    blank = jnp.zeros((8, 256), F32)
-    one, two = lax.fori_loop(0, 4, add_frame, (blank, blank))
+        one += jnp.sum(value.reshape(64, 8, 256), axis=0)
+        two += jnp.sum((value * value).reshape(64, 8, 256), axis=0)
     pl.semaphore_wait(barrier, greeted)
     total_begin(0, jnp.sum(one, axis=0, keepdims=True), jnp.sum(two, axis=0, keepdims=True))
+
+    begin_loads("grad", "narrow_table", "gain_fine", "windows", "kernel_fine")
+    begin_loads("up_mid", "up_coarse", "down_mid", "gain_mid")
 
     def rim(which):
         sem = 13 * which
@@ -472,6 +476,7 @@
     loads["middle_table"].wait()
     rim(0)
     total_middle(0)
+    begin_loads("kernel_mid")
     loads["grad"].wait()
     rim(1)
     loads["narrow_table"].wait()
@@ -627,6 +632,7 @@
     total_begin(1, column_sums(mid_value), column_sums(mid_value * mid_value))
     mid_pack[...] = dot(PACK[...], mid_in).astype(BF16)
     send_mid(mid_pack, mid_halo, mid_cor, 6)
+    begin_loads("down_coarse", "gain_coarse", "kernel_coarse", "stretch")
 
     @pl.loop(0, 4)
     def _(f):
@@ -1010,7 +1016,7 @@
         vmem((112, 512), BF16),
         vmem((96, 512), BF16),
         vmem((4, 16, 512), BF16),
-        pltpu.SemaphoreType.DMA((17,)),
+        pltpu.SemaphoreType.DMA((20,)),
         pltpu.SemaphoreType.DMA((5,)),
         pltpu.SemaphoreType.DMA((14,)),
         pltpu.SemaphoreType.DMA((14,)),

time: 71.2 us -> 71.2 us (level)
  no operation moved by 1% of the time
where the time goes in v6:
time: 71.2 us; the launch traced here: 71.1 us
  Pallas kernels  66.7 us (94%)
  local copies, waits for them, and re-layouts  3.73 us (5%)
    pallas_call x1, Pallas kernels, shards(): pl.pallas_call(functools.partial(kernel, wide_count, narrow_count), out_s...  66.7 us
    unnamed x4, local copies, waits for them, and re-layouts  3.73 us

profile of v6, /device:TPU:0, one launch (start us, length us, event | category | flops | bytes accessed | tf_op | source)
XLA Modules:
  0.0 71.1 jit_solution(2822456900596773054)
XLA Ops:
  0.6 66.7 %whole_net.1 = (bf16[4,512,256]{2,1,0:T(8,128)(2,1)}, f32[4,512,256]{2,1,0:T(8,128)}) custom-call(bf16[4,32,16,256]{3,2,1,0:T(8,128)(2,1)} %x_in.1, f32[1,256]{1,0:T(1,128)} %bitcast.15, bf16[9,256,256]{2,1,0:T(8,128)(2,1)} %bitcast.11, bf16[256,512]{1,0:T(8,128)(2,1)} %down_mid_in.1, f32[1,512]{1,0:T(1,128)} %bitcast.13, bf16[9,512,512]{2,1,0:T(8,128)(2,1)} %bitcast.8, ...), custom_call_target="tpu_custom_call" | custom-call | tf_op jit(solution)/shard_map/whole_net/pallas_call | solution.py:1026
  67.4 0.0 copy-start
  67.4 2.4 %copy.21 = bf16[4,32,16,256]{3,2,1,0:T(8,128)(2,1)} copy(bf16[4,32,16,256]{3,2,1,0:T(8,128)(2,1)} %bitcast.12) | data formatting | bytes 2097152
  69.8 0.0 copy-done
  69.8 1.3 %copy.22 = f32[4,32,16,256]{3,2,1,0:T(8,128)} copy(f32[4,32,16,256]{3,2,1,0:T(8,128)S(1)} %bitcast.10) | data formatting | bytes 4194304
Async XLA Ops:
  67.4 2.4 %copy-start = (f32[4,512,256]{2,1,0:T(8,128)S(1)}, f32[4,512,256]{2,1,0:T(8,128)}, u32[]{:S(2)}) copy-start(f32[4,512,256]{2,1,0:T(8,128)} %get-tuple-element.5) | copy-start | bytes 6291460

commit v7 on v6

--- a/solution.py
+++ b/solution.py
@@ -201,6 +201,7 @@
     rim_ends,
     matrix_sum,
     through,
+    mixed,
     stretched,
     col_pack,
     cor_pack,
@@ -451,10 +452,11 @@
     begin_loads("grad", "narrow_table", "gain_fine", "windows", "kernel_fine")
     begin_loads("up_mid", "up_coarse", "down_mid", "gain_mid")
 
-    def rim(which):
-        sem = 13 * which
-        send(xg.at[which, :, 31], row_in.at[0, which], sem, 1, 0)
-        send(xg.at[which, :, 0], row_in.at[1, which], sem, -1, 0)
+    def rim_rows_out(which):
+        send(xg.at[which, :, 31], row_in.at[0, which], 13 * which, 1, 0)
+        send(xg.at[which, :, 0], row_in.at[1, which], 13 * which, -1, 0)
+
+    def rim_pick(which):
         for f in range(4):
             picked = dot(PICK[...], frame(which, f))
             if which == 0:
@@ -464,21 +466,31 @@
             col_pack[1, which, 32 * f : 32 * f + 32] = picked[64:96]
             if which == 1:
                 summed[32 * f : 32 * f + 32] = picked[0:32]
-        send(col_pack.at[0, which], col_in.at[0, which], sem + 1, 0, 1)
-        send(col_pack.at[1, which], col_in.at[1, which], sem + 1, 0, -1)
+
+    def rim_sides_out(which):
+        send(col_pack.at[0, which], col_in.at[0, which], 13 * which + 1, 0, 1)
+        send(col_pack.at[1, which], col_in.at[1, which], 13 * which + 1, 0, -1)
+
+    def rim_ends_out(which):
         ends = jnp.concatenate([col_pack[0, which], col_pack[1, which]], axis=0)
         cor_pack[which] = dot(ENDS[...], ends).astype(BF16)
         for c in range(4):
             down, side = DIRS[5 + c]
-            send(cor_pack.at[which], cor_in.at[which, c], sem + 2, -down, -side)
+            send(cor_pack.at[which], cor_in.at[which, c], 13 * which + 2, -down, -side)
 
     loads["wide_table"].wait()
     loads["middle_table"].wait()
-    rim(0)
+    rim_rows_out(0)
+    rim_pick(0)
+    rim_sides_out(0)
+    rim_ends_out(0)
+    loads["grad"].wait()
+    rim_pick(1)
     total_middle(0)
     begin_loads("kernel_mid")
-    loads["grad"].wait()
-    rim(1)
+    rim_rows_out(1)
+    rim_sides_out(1)
+    rim_ends_out(1)
     loads["narrow_table"].wait()
 
     up_mid_grad = summed[...]
@@ -495,10 +507,6 @@
     loads["kernel_fine"].wait()
     loads["down_mid"].wait()
 
-    @pl.loop(0, 9)
-    def _(t):
-        through[t] = (0.0625 * dot(kernel_fine[8 - t], down_mid[...])).astype(BF16)
-
     fine_center, fine_square = total_end(0, 256, 2048 * wide_count * narrow_count)
     fine_inverse = lax.rsqrt(fine_square - fine_center * fine_center + epsilon)
     s_fine = gain_fine[...]
@@ -527,25 +535,24 @@
     def set_edges(kind, above, below, left, right, ends):
         edge_rows[kind, 0] = only(has_above, above)
         edge_rows[kind, 1] = only(has_below, below)
-        left = only(has_left, left).astype(BF16)
-        right = only(has_right, right).astype(BF16)
+        left = only(has_left, left)
+        right = only(has_right, right)
         for f in range(4):
             edge_sides[kind, f, 0:32] = left[32 * f : 32 * f + 32]
             edge_sides[kind, f, 32:64] = right[32 * f : 32 * f + 32]
         edge_ends[kind] = ends
 
     def place(kind, f, own):
-        column = lax.broadcasted_iota(jnp.int32, (512, 256), 0) & 15
-        sides = edge_sides[kind, f]
-        low = jnp.where(
-            column == 0, dot(SIDES[:, 0:64], sides), pltpu.roll(own, 1, 0)
+        column = lax.broadcasted_iota(jnp.int32, (32, 16, 256), 1)
+        west, east = (
+            jnp.broadcast_to(edge_sides[kind, f, 32 * k : 32 * k + 32].reshape(32, 1, 256), (32, 16, 256))
+            for k in range(2)
         )
-        columns[f, 16:528, 0:256] = low.astype(BF16)
+        low = jnp.where(column == 0, west, pltpu.roll(own, 1, 0).reshape(32, 16, 256))
+        columns[f, 16:528, 0:256] = low.reshape(512, 256).astype(BF16)
         columns[f, 16:528, 256:512] = own.astype(BF16)
-        high = jnp.where(
-            column == 15, dot(SIDES[:, 32:96], sides), pltpu.roll(own, 511, 0)
-        )
-        columns[f, 16:528, 512:768] = high.astype(BF16)
+        high = jnp.where(column == 15, east, pltpu.roll(own, 511, 0).reshape(32, 16, 256))
+        columns[f, 16:528, 512:768] = high.reshape(512, 256).astype(BF16)
         cell = lax.broadcasted_iota(jnp.int32, (16, 256), 0)
         for k in range(2):
             row = edge_rows[kind, k, f]
@@ -560,10 +567,13 @@
         return jnp.concatenate(list(pieces), axis=1)
 
     def fine_taps(f):
-        return side_by_side(columns[f, 16 * a : 16 * a + 512, :] for a in range(3))
+        return side_by_side(
+            columns[f : f + 2, 16 * a : 16 * a + 512, :].reshape(1024, 768) for a in range(3)
+        )
 
     def fine_convolve(f):
-        return dot(fine_taps(f), kernel_fine[...].reshape(2304, 256))
+        taps = side_by_side(columns[f, 16 * a : 16 * a + 512, :] for a in range(3))
+        return dot(taps, kernel_fine[...].reshape(2304, 256))
 
     def fine_convolve_back(f):
         return dot_t(fine_taps(f), side_by_side(kernel_fine[8 - t] for t in range(9)))
@@ -706,18 +716,19 @@
         corners(lambda c: cor_in[1, c], same, True),
     )
 
-    def convolve_grad(f, carry):
-        place(1, f, frame(1, f).astype(F32))
-        result = fine_convolve_back(f)
-        conv_grad[f] = result
-        weighted = result * fine_slope[f]
-        scaled = fine_scaled(fine_value(f))
-        return (
-            carry[0] + jnp.sum(weighted.reshape(64, 8, 256), axis=0),
-            carry[1] + jnp.sum((weighted * scaled).reshape(64, 8, 256), axis=0),
-        )
-
-    grad_sums = lax.fori_loop(0, 2, convolve_grad, (blank, blank))
+    def convolve_grad(f):
+        for k in range(2):
+            place(1, f + k, frame(1, f + k).astype(F32))
+        result = fine_convolve_back(f).reshape(2, 512, 256)
+        for k in range(2):
+            conv_grad[f + k] = result[k]
+            weighted = result[k] * fine_slope[f + k]
+            scaled = fine_scaled(fine_value(f + k))
+            grad_sums[0] += jnp.sum(weighted.reshape(64, 8, 256), axis=0)
+            grad_sums[1] += jnp.sum((weighted * scaled).reshape(64, 8, 256), axis=0)
+
+    grad_sums = [blank, blank]
+    convolve_grad(0)
     total_middle(2)
 
     arrived(cgrad_in, 5)
@@ -734,6 +745,10 @@
         side_by_side(kernel_coarse[8 - t] for t in range(9)),
     )[0:8]
 
+    @pl.loop(0, 9)
+    def _(t):
+        through[t] = (0.0625 * dot(kernel_fine[8 - t], down_mid[...])).astype(BF16)
+
     arrived(sum_in, 3)
     arrived(sum_cor, 4)
     sum_extended = mid_extended(
@@ -754,23 +769,29 @@
     total_begin(3, column_sums(normed_grad), column_sums(normed_grad * scaled))
     coarse_u[...] = cgrad + coarse_inverse * normed_grad
     send_coarse(coarse_u, coarse_u_halo, 9)
-    grad_sums = lax.fori_loop(2, 4, convolve_grad, grad_sums)
+    convolve_grad(2)
 
     total_middle(3)
 
     mid_mix = jnp.concatenate(
         [mid_scaled(mid_value).astype(BF16), jnp.ones((128, 128), BF16)], axis=1
     )
-    matrix_sum[...] = jnp.zeros((4, 256, 512), F32)
-
-    @pl.loop(0, 9)
-    def _(t):
-        weight = through[t].astype(F32)
-        for n in range(2):
-            mixed = dot_first(window_sums[n, t].reshape(128, 256), mid_mix)
-            plain = jnp.concatenate([mixed[:, 512:640]] * 4, axis=1)
-            matrix_sum[2 * n] += weight * plain
-            matrix_sum[2 * n + 1] += weight * mixed[:, 0:512]
+    for n in range(2):
+        sums = side_by_side(window_sums[n, t].reshape(128, 256) for t in range(9))
+        mixed[n] = dot_first(sums, mid_mix).astype(BF16).reshape(9, 256, 640)
+
+    @pl.loop(0, 16)
+    def _(part):
+        here = pl.ds(pl.multiple_of(16 * part, 16), 16)
+        totals = [jnp.zeros((16, 512), F32) for _ in range(4)]
+        for t in range(9):
+            weight = through[t, here, :].astype(F32)
+            for n in range(2):
+                value = mixed[n, t, here, :].astype(F32)
+                totals[2 * n] += weight * side_by_side([value[:, 512:640]] * 4)
+                totals[2 * n + 1] += weight * value[:, 0:512]
+        for n in range(4):
+            matrix_sum[n, here, :] = totals[n]
 
     def iota(shape, axis):
         return lax.broadcasted_iota(jnp.int32, shape, axis)
@@ -828,7 +849,6 @@
     total_begin(5, *fine_sums)
     total_middle(6)
 
-    fine_forward(2)
     coarse_block = (
         coarse_in.astype(F32)
         + coarse_convolve(
@@ -848,6 +868,7 @@
     total_middle(4)
     total_middle(5)
 
+    fine_forward(2)
     fine_forward(3)
     mid_up = dot(ENLARGE[:, 0:128], mid_up).reshape(4, 8, 1, 16, 256)
     for f in range(4):
@@ -981,7 +1002,7 @@
         vmem((128, 256), BF16),
         vmem((4, 512, 256), F32),
         vmem((2, 2, 4, 16, 256), F32),
-        vmem((2, 4, 64, 256), BF16),
+        vmem((2, 4, 64, 256), F32),
         vmem((2, 16, 256), F32),
         vmem((256, 512), F32),
         vmem((6, wide_count, 1, 128), F32),
@@ -995,6 +1016,7 @@
         vmem((2, 4, 32, 256), BF16),
         vmem((4, 256, 512), F32),
         vmem((9, 256, 512), BF16),
+        vmem((2, 9, 256, 640), BF16),
         vmem((3, 4, 10, 16, 256), F32),
         vmem((2, 2, 128, 256), BF16),
         vmem((2, 16, 256), BF16),

time: 71.2 us -> 71.8 us (level)
  no operation moved by 1% of the time
where the time goes in v7:
time: 71.8 us; the launch traced here: 71.5 us
  Pallas kernels  67.2 us (94%)
  local copies, waits for them, and re-layouts  3.73 us (5%)
    pallas_call x1, Pallas kernels, shards(): pl.pallas_call(functools.partial(kernel, wide_count, narrow_count), out_s...  67.2 us
    unnamed x4, local copies, waits for them, and re-layouts  3.73 us

profile of v7, /device:TPU:0, one launch (start us, length us, event | category | flops | bytes accessed | tf_op | source)
XLA Modules:
  0.0 71.5 jit_solution(7656505267615982128)
XLA Ops:
  0.6 67.2 %whole_net.1 = (bf16[4,512,256]{2,1,0:T(8,128)(2,1)}, f32[4,512,256]{2,1,0:T(8,128)}) custom-call(bf16[4,32,16,256]{3,2,1,0:T(8,128)(2,1)} %x_in.1, f32[1,256]{1,0:T(1,128)} %bitcast.15, bf16[9,256,256]{2,1,0:T(8,128)(2,1)} %bitcast.11, bf16[256,512]{1,0:T(8,128)(2,1)} %down_mid_in.1, f32[1,512]{1,0:T(1,128)} %bitcast.13, bf16[9,512,512]{2,1,0:T(8,128)(2,1)} %bitcast.8, ...), custom_call_target="tpu_custom_call" | custom-call | tf_op jit(solution)/shard_map/whole_net/pallas_call | solution.py:1048
  67.8 0.0 copy-start
  67.8 2.4 %copy.21 = bf16[4,32,16,256]{3,2,1,0:T(8,128)(2,1)} copy(bf16[4,32,16,256]{3,2,1,0:T(8,128)(2,1)} %bitcast.12) | data formatting | bytes 2097152
  70.2 0.0 copy-done
  70.2 1.3 %copy.22 = f32[4,32,16,256]{3,2,1,0:T(8,128)} copy(f32[4,32,16,256]{3,2,1,0:T(8,128)S(1)} %bitcast.10) | data formatting | bytes 4194304
Async XLA Ops:
  67.8 2.4 %copy-start = (f32[4,512,256]{2,1,0:T(8,128)S(1)}, f32[4,512,256]{2,1,0:T(8,128)}, u32[]{:S(2)}) copy-start(f32[4,512,256]{2,1,0:T(8,128)} %get-tuple-element.5) | copy-start | bytes 6291460

commit v8 on v6

--- a/solution.py
+++ b/solution.py
@@ -308,8 +308,7 @@
     def total_send_wide(phase):
         mine = firsts[phase].at[wide]
 
-        @pl.loop(1, wide_count)
-        def _(step):
+        for step in sorted(range(1, wide_count), key=lambda k: -min(k & 7, 8 - (k & 7))):
             pltpu.make_async_remote_copy(
                 src_ref=mine,
                 dst_ref=mine,
@@ -342,8 +341,7 @@
         seconds[phase][narrow] = summed_up.astype(seconds[phase].dtype)
         mine = seconds[phase].at[narrow]
 
-        @pl.loop(1, narrow_count)
-        def _(step):
+        for step in sorted(range(1, narrow_count), key=lambda k: -min(k & 3, 4 - (k & 3))):
             pltpu.make_async_remote_copy(
                 src_ref=mine,
                 dst_ref=mine,
@@ -451,10 +449,11 @@
     begin_loads("grad", "narrow_table", "gain_fine", "windows", "kernel_fine")
     begin_loads("up_mid", "up_coarse", "down_mid", "gain_mid")
 
-    def rim(which):
-        sem = 13 * which
-        send(xg.at[which, :, 31], row_in.at[0, which], sem, 1, 0)
-        send(xg.at[which, :, 0], row_in.at[1, which], sem, -1, 0)
+    def rim_rows_out(which):
+        send(xg.at[which, :, 31], row_in.at[0, which], 13 * which, 1, 0)
+        send(xg.at[which, :, 0], row_in.at[1, which], 13 * which, -1, 0)
+
+    def rim_pick(which):
         for f in range(4):
             picked = dot(PICK[...], frame(which, f))
             if which == 0:
@@ -464,21 +463,31 @@
             col_pack[1, which, 32 * f : 32 * f + 32] = picked[64:96]
             if which == 1:
                 summed[32 * f : 32 * f + 32] = picked[0:32]
-        send(col_pack.at[0, which], col_in.at[0, which], sem + 1, 0, 1)
-        send(col_pack.at[1, which], col_in.at[1, which], sem + 1, 0, -1)
+
+    def rim_sides_out(which):
+        send(col_pack.at[0, which], col_in.at[0, which], 13 * which + 1, 0, 1)
+        send(col_pack.at[1, which], col_in.at[1, which], 13 * which + 1, 0, -1)
+
+    def rim_ends_out(which):
         ends = jnp.concatenate([col_pack[0, which], col_pack[1, which]], axis=0)
         cor_pack[which] = dot(ENDS[...], ends).astype(BF16)
         for c in range(4):
             down, side = DIRS[5 + c]
-            send(cor_pack.at[which], cor_in.at[which, c], sem + 2, -down, -side)
+            send(cor_pack.at[which], cor_in.at[which, c], 13 * which + 2, -down, -side)
 
     loads["wide_table"].wait()
     loads["middle_table"].wait()
-    rim(0)
+    rim_rows_out(0)
+    rim_pick(0)
+    rim_sides_out(0)
+    rim_ends_out(0)
+    loads["grad"].wait()
+    rim_pick(1)
     total_middle(0)
     begin_loads("kernel_mid")
-    loads["grad"].wait()
-    rim(1)
+    rim_rows_out(1)
+    rim_sides_out(1)
+    rim_ends_out(1)
     loads["narrow_table"].wait()
 
     up_mid_grad = summed[...]
@@ -495,10 +504,6 @@
     loads["kernel_fine"].wait()
     loads["down_mid"].wait()
 
-    @pl.loop(0, 9)
-    def _(t):
-        through[t] = (0.0625 * dot(kernel_fine[8 - t], down_mid[...])).astype(BF16)
-
     fine_center, fine_square = total_end(0, 256, 2048 * wide_count * narrow_count)
     fine_inverse = lax.rsqrt(fine_square - fine_center * fine_center + epsilon)
     s_fine = gain_fine[...]
@@ -527,25 +532,24 @@
     def set_edges(kind, above, below, left, right, ends):
         edge_rows[kind, 0] = only(has_above, above)
         edge_rows[kind, 1] = only(has_below, below)
-        left = only(has_left, left).astype(BF16)
-        right = only(has_right, right).astype(BF16)
+        left = only(has_left, left)
+        right = only(has_right, right)
         for f in range(4):
             edge_sides[kind, f, 0:32] = left[32 * f : 32 * f + 32]
             edge_sides[kind, f, 32:64] = right[32 * f : 32 * f + 32]
         edge_ends[kind] = ends
 
     def place(kind, f, own):
-        column = lax.broadcasted_iota(jnp.int32, (512, 256), 0) & 15
-        sides = edge_sides[kind, f]
-        low = jnp.where(
-            column == 0, dot(SIDES[:, 0:64], sides), pltpu.roll(own, 1, 0)
+        column = lax.broadcasted_iota(jnp.int32, (32, 16, 256), 1)
+        west, east = (
+            jnp.broadcast_to(edge_sides[kind, f, 32 * k : 32 * k + 32].reshape(32, 1, 256), (32, 16, 256))
+            for k in range(2)
         )
-        columns[f, 16:528, 0:256] = low.astype(BF16)
+        low = jnp.where(column == 0, west, pltpu.roll(own, 1, 0).reshape(32, 16, 256))
+        columns[f, 16:528, 0:256] = low.reshape(512, 256).astype(BF16)
         columns[f, 16:528, 256:512] = own.astype(BF16)
-        high = jnp.where(
-            column == 15, dot(SIDES[:, 32:96], sides), pltpu.roll(own, 511, 0)
-        )
-        columns[f, 16:528, 512:768] = high.astype(BF16)
+        high = jnp.where(column == 15, east, pltpu.roll(own, 511, 0).reshape(32, 16, 256))
+        columns[f, 16:528, 512:768] = high.reshape(512, 256).astype(BF16)
         cell = lax.broadcasted_iota(jnp.int32, (16, 256), 0)
         for k in range(2):
             row = edge_rows[kind, k, f]
@@ -733,6 +737,10 @@
         dot_t,
         side_by_side(kernel_coarse[8 - t] for t in range(9)),
     )[0:8]
+
+    @pl.loop(0, 9)
+    def _(t):
+        through[t] = (0.0625 * dot(kernel_fine[8 - t], down_mid[...])).astype(BF16)
 
     arrived(sum_in, 3)
     arrived(sum_cor, 4)
@@ -981,7 +989,7 @@
         vmem((128, 256), BF16),
         vmem((4, 512, 256), F32),
         vmem((2, 2, 4, 16, 256), F32),
-        vmem((2, 4, 64, 256), BF16),
+        vmem((2, 4, 64, 256), F32),
         vmem((2, 16, 256), F32),
         vmem((256, 512), F32),
         vmem((6, wide_count, 1, 128), F32),

time: 71.2 us -> 70.6 us (level)
  no operation moved by 1% of the time
where the time goes in v8:
time: 70.6 us; the launch traced here: 70.4 us
  Pallas kernels  66 us (93%)
  local copies, waits for them, and re-layouts  3.73 us (5%)
    pallas_call x1, Pallas kernels, shards(): pl.pallas_call(functools.partial(kernel, wide_count, narrow_count), out_s...  66 us
    unnamed x4, local copies, waits for them, and re-layouts  3.73 us

profile of v8, /device:TPU:0, one launch (start us, length us, event | category | flops | bytes accessed | tf_op | source)
XLA Modules:
  0.0 70.4 jit_solution(5189760893591879588)
XLA Ops:
  0.6 66.0 %whole_net.1 = (bf16[4,512,256]{2,1,0:T(8,128)(2,1)}, f32[4,512,256]{2,1,0:T(8,128)}) custom-call(bf16[4,32,16,256]{3,2,1,0:T(8,128)(2,1)} %x_in.1, f32[1,256]{1,0:T(1,128)} %bitcast.15, bf16[9,256,256]{2,1,0:T(8,128)(2,1)} %bitcast.11, bf16[256,512]{1,0:T(8,128)(2,1)} %down_mid_in.1, f32[1,512]{1,0:T(1,128)} %bitcast.13, bf16[9,512,512]{2,1,0:T(8,128)(2,1)} %bitcast.8, ...), custom_call_target="tpu_custom_call" | custom-call | tf_op jit(solution)/shard_map/whole_net/pallas_call | solution.py:1034
  66.7 0.0 copy-start
  66.7 2.4 %copy.21 = bf16[4,32,16,256]{3,2,1,0:T(8,128)(2,1)} copy(bf16[4,32,16,256]{3,2,1,0:T(8,128)(2,1)} %bitcast.12) | data formatting | bytes 2097152
  69.1 0.0 copy-done
  69.1 1.3 %copy.22 = f32[4,32,16,256]{3,2,1,0:T(8,128)} copy(f32[4,32,16,256]{3,2,1,0:T(8,128)S(1)} %bitcast.10) | data formatting | bytes 4194304
Async XLA Ops:
  66.7 2.4 %copy-start = (f32[4,512,256]{2,1,0:T(8,128)S(1)}, f32[4,512,256]{2,1,0:T(8,128)}, u32[]{:S(2)}) copy-start(f32[4,512,256]{2,1,0:T(8,128)} %get-tuple-element.5) | copy-start | bytes 6291460

commit v9 on v8

--- a/solution.py
+++ b/solution.py
@@ -201,6 +201,7 @@
     rim_ends,
     matrix_sum,
     through,
+    mixed,
     stretched,
     col_pack,
     cor_pack,
@@ -769,16 +770,22 @@
     mid_mix = jnp.concatenate(
         [mid_scaled(mid_value).astype(BF16), jnp.ones((128, 128), BF16)], axis=1
     )
-    matrix_sum[...] = jnp.zeros((4, 256, 512), F32)
-
-    @pl.loop(0, 9)
-    def _(t):
-        weight = through[t].astype(F32)
-        for n in range(2):
-            mixed = dot_first(window_sums[n, t].reshape(128, 256), mid_mix)
-            plain = jnp.concatenate([mixed[:, 512:640]] * 4, axis=1)
-            matrix_sum[2 * n] += weight * plain
-            matrix_sum[2 * n + 1] += weight * mixed[:, 0:512]
+    for n in range(2):
+        sums = side_by_side(window_sums[n, t].reshape(128, 256) for t in range(9))
+        mixed[n] = dot_first(sums, mid_mix).astype(BF16).reshape(9, 256, 640)
+
+    @pl.loop(0, 16)
+    def _(part):
+        here = pl.ds(pl.multiple_of(16 * part, 16), 16)
+        totals = [jnp.zeros((16, 512), F32) for _ in range(4)]
+        for t in range(9):
+            weight = through[t, here, :].astype(F32)
+            for n in range(2):
+                value = mixed[n, t, here, :].astype(F32)
+                totals[2 * n] += weight * side_by_side([value[:, 512:640]] * 4)
+                totals[2 * n + 1] += weight * value[:, 0:512]
+        for n in range(4):
+            matrix_sum[n, here, :] = totals[n]
 
     def iota(shape, axis):
         return lax.broadcasted_iota(jnp.int32, shape, axis)
@@ -836,7 +843,6 @@
     total_begin(5, *fine_sums)
     total_middle(6)
 
-    fine_forward(2)
     coarse_block = (
         coarse_in.astype(F32)
         + coarse_convolve(
@@ -856,6 +862,7 @@
     total_middle(4)
     total_middle(5)
 
+    fine_forward(2)
     fine_forward(3)
     mid_up = dot(ENLARGE[:, 0:128], mid_up).reshape(4, 8, 1, 16, 256)
     for f in range(4):
@@ -1003,6 +1010,7 @@
         vmem((2, 4, 32, 256), BF16),
         vmem((4, 256, 512), F32),
         vmem((9, 256, 512), BF16),
+        vmem((2, 9, 256, 640), BF16),
         vmem((3, 4, 10, 16, 256), F32),
         vmem((2, 2, 128, 256), BF16),
         vmem((2, 16, 256), BF16),

time: 70.6 us -> 70 us (level)
  no operation moved by 1% of the time
where the time goes in v9:
time: 70 us; the launch traced here: 69.9 us
  Pallas kernels  65.5 us (94%)
  local copies, waits for them, and re-layouts  3.73 us (5%)
    pallas_call x1, Pallas kernels, shards(): pl.pallas_call(functools.partial(kernel, wide_count, narrow_count), out_s...  65.5 us
    unnamed x4, local copies, waits for them, and re-layouts  3.73 us

profile of v9, /device:TPU:0, one launch (start us, length us, event | category | flops | bytes accessed | tf_op | source)
XLA Modules:
  0.0 69.9 jit_solution(6413793438136005595)
XLA Ops:
  0.6 65.5 %whole_net.1 = (bf16[4,512,256]{2,1,0:T(8,128)(2,1)}, f32[4,512,256]{2,1,0:T(8,128)}) custom-call(bf16[4,32,16,256]{3,2,1,0:T(8,128)(2,1)} %x_in.1, f32[1,256]{1,0:T(1,128)} %bitcast.15, bf16[9,256,256]{2,1,0:T(8,128)(2,1)} %bitcast.11, bf16[256,512]{1,0:T(8,128)(2,1)} %down_mid_in.1, f32[1,512]{1,0:T(1,128)} %bitcast.13, bf16[9,512,512]{2,1,0:T(8,128)(2,1)} %bitcast.8, ...), custom_call_target="tpu_custom_call" | custom-call | tf_op jit(solution)/shard_map/whole_net/pallas_call | solution.py:1042
  66.1 0.0 copy-start
  66.1 2.4 %copy.21 = bf16[4,32,16,256]{3,2,1,0:T(8,128)(2,1)} copy(bf16[4,32,16,256]{3,2,1,0:T(8,128)(2,1)} %bitcast.12) | data formatting | bytes 2097152
  68.5 0.0 copy-done
  68.5 1.3 %copy.22 = f32[4,32,16,256]{3,2,1,0:T(8,128)} copy(f32[4,32,16,256]{3,2,1,0:T(8,128)S(1)} %bitcast.10) | data formatting | bytes 4194304
Async XLA Ops:
  66.1 2.4 %copy-start = (f32[4,512,256]{2,1,0:T(8,128)S(1)}, f32[4,512,256]{2,1,0:T(8,128)}, u32[]{:S(2)}) copy-start(f32[4,512,256]{2,1,0:T(8,128)} %get-tuple-element.5) | copy-start | bytes 6291460

commit v10 on v9

--- a/solution.py
+++ b/solution.py
@@ -803,6 +803,16 @@
     first_matrix[wide] = matrix.astype(BF16)
     total_send_wide(6)
 
+    row = lax.broadcasted_iota(jnp.int32, (256, 128), 0)
+    keep = jnp.where(row < ABOVE, 1.0, 0.0)
+    bounds = ((ABOVE, 16, 1), (BELOW, 16, 2), (LEFT, 32, 3), (RIGHT, 32, 4)) + tuple(
+        (CORNER + 4 * c, 4, 5 + c) for c in range(4)
+    )
+    for start, size, d in bounds:
+        inside = jnp.logical_and(row >= start, row < start + size)
+        keep = jnp.where(inside, jnp.where(exists[d], 1.0, 0.0).astype(F32), keep)
+    mid_scaled_own = mid_scaled(mid_value)
+    mid_bend = slope(mid_scaled_own, s_mid)
     first_mean, second_mean = total_end(3, 512, 8 * wide_count * narrow_count)
     arrived(coarse_halo, 8)
     arrived(coarse_u_halo, 9)
@@ -816,28 +826,21 @@
     coarse_in_grad = jnp.concatenate(pieces, axis=0).astype(BF16)
 
     mid_pool_grad = dot_t(dot(SPREAD[...], coarse_in_grad).astype(BF16), down_coarse[...])
-    row = lax.broadcasted_iota(jnp.int32, (256, 128), 0)
-    keep = jnp.where(row < ABOVE, 1.0, 0.0)
-    bounds = ((ABOVE, 16, 1), (BELOW, 16, 2), (LEFT, 32, 3), (RIGHT, 32, 4)) + tuple(
-        (CORNER + 4 * c, 4, 5 + c) for c in range(4)
-    )
-    for start, size, d in bounds:
-        inside = jnp.logical_and(row >= start, row < start + size)
-        keep = jnp.where(inside, jnp.where(exists[d], 1.0, 0.0).astype(F32), keep)
     mid_grad = (summed_grad[...] + 0.0625 * mid_pool_grad) * jnp.concatenate([keep] * 4, axis=1)
     mid_act_grad = mid_convolve(
         mid_grad, dot_t, side_by_side(kernel_mid[8 - t] for t in range(9))
     )
-    scaled = mid_scaled(mid_value)
-    normed_grad = mid_act_grad * slope(scaled, s_mid)
+    scaled = mid_scaled_own
+    normed_grad = mid_act_grad * mid_bend
     total_begin(4, column_sums(normed_grad), column_sums(normed_grad * scaled))
     mid_u = mid_grad[0:128].astype(BF16).astype(F32) + mid_inverse * normed_grad
     u_pack[...] = dot(PACK[...], mid_u.astype(BF16)).astype(BF16)
     send_mid(u_pack, u_halo, u_cor, 10)
     pulled = (0.0625 * dot_t(mid_u.astype(BF16), down_mid[...])).astype(BF16)
     fine_sums = [jnp.sum(value, axis=0, keepdims=True) for value in grad_sums]
+    terms = dot_t(pulled, kernel_fine[...].reshape(2304, 256))
     for t in range(9):
-        term = dot_t(pulled, kernel_fine[8 - t])
+        term = terms[:, 256 * (8 - t) : 256 * (9 - t)]
         for n in range(2):
             fine_sums[n] += column_sums(window_sums[n, t].reshape(128, 256).astype(F32) * term)
     total_begin(5, *fine_sums)
@@ -870,6 +873,14 @@
         fine_block[f] = (block + mid_up[f]).astype(BF16).reshape(512, 256)
     out_copy = pltpu.make_async_copy(fine_block, out_ref, out_sem.at[0])
     out_copy.start()
+    scaled_around = mid_extended(
+        mid_value, mid_halo[...], lambda c: mid_cor[c], mid_scaled, False
+    )
+    to_lanes = []
+    for n in range(2):
+        lane, row = iota((512, 128), 1), iota((512, 128), 0)
+        inside = jnp.logical_and((lane & 31) == (row >> 4), ((lane >> 5) & 1) == n)
+        to_lanes.append(jnp.where(inside, 0.0625, 0.0).astype(BF16))
     first_mean, second_mean = total_end(4, 512, 128 * wide_count * narrow_count)
     arrived(u_halo, 10)
     arrived(u_cor, 11)
@@ -877,24 +888,21 @@
     factor = mid_inverse * second_mean
     mid_in_grad = mid_extended(
         mid_u, u_halo[...], lambda c: u_cor[c], lambda v: v - offset, False
-    ) - factor * mid_extended(
-        mid_value, mid_halo[...], lambda c: mid_cor[c], mid_scaled, False
-    )
+    ) - factor * scaled_around
 
     pool_grad = 0.0625 * dot_t(mid_in_grad.astype(BF16), down_mid[...])
     pool_grad = pool_grad * jnp.concatenate([keep] * 2, axis=1)
     high, low = halves(pool_grad)
     added = dot(ENLARGE[...], jnp.concatenate([high[0:256], low[0:256]], axis=0))
     loads["stretch"].wait()
+    all_fields = dot_t(high, kernel_fine[...].reshape(2304, 256)).astype(BF16)
     for a in range(3):
-        fields = [dot_t(high, kernel_fine[8 - 3 * a - b]).astype(BF16) for b in range(3)]
+        fields = [all_fields[:, 256 * k : 256 * k + 256] for k in range(8 - 3 * a, 5 - 3 * a, -1)]
         stretched[a] = dot(stretch[...], jnp.concatenate(fields, axis=0)).reshape(4, 10, 16, 256)
 
     means = jnp.zeros((8, 128), F32)
     for n, mean in enumerate((first_mean, second_mean)):
-        lane, row = iota((512, 128), 1), iota((512, 128), 0)
-        inside = jnp.logical_and((lane & 31) == (row >> 4), ((lane >> 5) & 1) == n)
-        to_lane = jnp.where(inside, 0.0625, 0.0).astype(BF16)
+        to_lane = to_lanes[n]
         high, low = halves(jnp.broadcast_to(mean, (8, 512)))
         means += dot(high, to_lane) + dot(low, to_lane)
     matrix_high, matrix_low = halves(total_sum(6))

time: 70 us -> 70 us (level)
  no operation moved by 1% of the time
where the time goes in v10:
time: 70 us; the launch traced here: 69.9 us
  Pallas kernels  65.5 us (94%)
  local copies, waits for them, and re-layouts  3.73 us (5%)
    pallas_call x1, Pallas kernels, shards(): pl.pallas_call(functools.partial(kernel, wide_count, narrow_count), out_s...  65.5 us
    unnamed x4, local copies, waits for them, and re-layouts  3.73 us

profile of v10, /device:TPU:0, one launch (start us, length us, event | category | flops | bytes accessed | tf_op | source)
XLA Modules:
  0.0 69.9 jit_solution(4482744541073919145)
XLA Ops:
  0.6 65.5 %whole_net.1 = (bf16[4,512,256]{2,1,0:T(8,128)(2,1)}, f32[4,512,256]{2,1,0:T(8,128)}) custom-call(bf16[4,32,16,256]{3,2,1,0:T(8,128)(2,1)} %x_in.1, f32[1,256]{1,0:T(1,128)} %bitcast.15, bf16[9,256,256]{2,1,0:T(8,128)(2,1)} %bitcast.11, bf16[256,512]{1,0:T(8,128)(2,1)} %down_mid_in.1, f32[1,512]{1,0:T(1,128)} %bitcast.13, bf16[9,512,512]{2,1,0:T(8,128)(2,1)} %bitcast.8, ...), custom_call_target="tpu_custom_call" | custom-call | tf_op jit(solution)/shard_map/whole_net/pallas_call | solution.py:1050
  66.2 0.0 copy-start
  66.2 2.4 %copy.21 = bf16[4,32,16,256]{3,2,1,0:T(8,128)(2,1)} copy(bf16[4,32,16,256]{3,2,1,0:T(8,128)(2,1)} %bitcast.12) | data formatting | bytes 2097152
  68.6 0.0 copy-done
  68.6 1.3 %copy.22 = f32[4,32,16,256]{3,2,1,0:T(8,128)} copy(f32[4,32,16,256]{3,2,1,0:T(8,128)S(1)} %bitcast.10) | data formatting | bytes 4194304
Async XLA Ops:
  66.2 2.4 %copy-start = (f32[4,512,256]{2,1,0:T(8,128)S(1)}, f32[4,512,256]{2,1,0:T(8,128)}, u32[]{:S(2)}) copy-start(f32[4,512,256]{2,1,0:T(8,128)} %get-tuple-element.5) | copy-start | bytes 6291460

commit v11 on v9

--- a/solution.py
+++ b/solution.py
@@ -605,8 +605,7 @@
     set_fields(0, fine_act)
     loads["windows"].wait()
 
-    @pl.loop(0, 4)
-    def _(f):
+    for f in range(4):
         sums = window(0, f, fine_act(fine_value(f)))
         high, low = halves(sums)
         window_sums[0, :, f] = high.reshape(9, 32, 256)
@@ -658,8 +657,7 @@
     total_middle(1)
     fine_forward(1)
 
-    @pl.loop(0, 4)
-    def _(f):
+    for f in range(4):
         bent = fine_slope[f]
         window_sums[0, :, f] = window(0, f, bent).astype(BF16).reshape(9, 32, 256)
         bent = bent * fine_scaled(fine_value(f))

time: 70 us -> 69.4 us (level)
  no operation moved by 1% of the time
where the time goes in v11:
time: 69.4 us; the launch traced here: 69.3 us
  Pallas kernels  64.9 us (94%)
  local copies, waits for them, and re-layouts  3.73 us (5%)
    pallas_call x1, Pallas kernels, shards(): pl.pallas_call(functools.partial(kernel, wide_count, narrow_count), out_s...  64.9 us
    unnamed x4, local copies, waits for them, and re-layouts  3.73 us

profile of v11, /device:TPU:0, one launch (start us, length us, event | category | flops | bytes accessed | tf_op | source)
XLA Modules:
  0.0 69.3 jit_solution(13639927498226462519)
XLA Ops:
  0.6 64.9 %whole_net.1 = (bf16[4,512,256]{2,1,0:T(8,128)(2,1)}, f32[4,512,256]{2,1,0:T(8,128)}) custom-call(bf16[4,32,16,256]{3,2,1,0:T(8,128)(2,1)} %x_in.1, f32[1,256]{1,0:T(1,128)} %bitcast.15, bf16[9,256,256]{2,1,0:T(8,128)(2,1)} %bitcast.11, bf16[256,512]{1,0:T(8,128)(2,1)} %down_mid_in.1, f32[1,512]{1,0:T(1,128)} %bitcast.13, bf16[9,512,512]{2,1,0:T(8,128)(2,1)} %bitcast.8, ...), custom_call_target="tpu_custom_call" | custom-call | tf_op jit(solution)/shard_map/whole_net/pallas_call | solution.py:1040
  65.6 0.0 copy-start
  65.6 2.4 %copy.21 = bf16[4,32,16,256]{3,2,1,0:T(8,128)(2,1)} copy(bf16[4,32,16,256]{3,2,1,0:T(8,128)(2,1)} %bitcast.12) | data formatting | bytes 2097152
  68.0 0.0 copy-done
  68.0 1.3 %copy.22 = f32[4,32,16,256]{3,2,1,0:T(8,128)} copy(f32[4,32,16,256]{3,2,1,0:T(8,128)S(1)} %bitcast.10) | data formatting | bytes 4194304
Async XLA Ops:
  65.6 2.4 %copy-start = (f32[4,512,256]{2,1,0:T(8,128)S(1)}, f32[4,512,256]{2,1,0:T(8,128)}, u32[]{:S(2)}) copy-start(f32[4,512,256]{2,1,0:T(8,128)} %get-tuple-element.5) | copy-start | bytes 6291460

commit v12 on v11

--- a/solution.py
+++ b/solution.py
@@ -638,8 +638,7 @@
     send_mid(mid_pack, mid_halo, mid_cor, 6)
     begin_loads("down_coarse", "gain_coarse", "kernel_coarse", "stretch")
 
-    @pl.loop(0, 4)
-    def _(f):
+    for f in range(4):
         fine_slope[f] = slope(fine_scaled(fine_value(f)), s_fine)
 
     set_fields(0, lambda v: slope(fine_scaled(v), s_fine))

time: 69.4 us -> 69.3 us (level)
  no operation moved by 1% of the time
where the time goes in v12:
time: 69.3 us; the launch traced here: 69.1 us
  Pallas kernels  64.8 us (94%)
  local copies, waits for them, and re-layouts  3.73 us (5%)
    pallas_call x1, Pallas kernels, shards(): pl.pallas_call(functools.partial(kernel, wide_count, narrow_count), out_s...  64.8 us
    unnamed x4, local copies, waits for them, and re-layouts  3.73 us

profile of v12, /device:TPU:0, one launch (start us, length us, event | category | flops | bytes accessed | tf_op | source)
XLA Modules:
  0.0 69.1 jit_solution(4233025253145943386)
XLA Ops:
  0.6 64.8 %whole_net.1 = (bf16[4,512,256]{2,1,0:T(8,128)(2,1)}, f32[4,512,256]{2,1,0:T(8,128)}) custom-call(bf16[4,32,16,256]{3,2,1,0:T(8,128)(2,1)} %x_in.1, f32[1,256]{1,0:T(1,128)} %bitcast.15, bf16[9,256,256]{2,1,0:T(8,128)(2,1)} %bitcast.11, bf16[256,512]{1,0:T(8,128)(2,1)} %down_mid_in.1, f32[1,512]{1,0:T(1,128)} %bitcast.13, bf16[9,512,512]{2,1,0:T(8,128)(2,1)} %bitcast.8, ...), custom_call_target="tpu_custom_call" | custom-call | tf_op jit(solution)/shard_map/whole_net/pallas_call | solution.py:1039
  65.4 0.0 copy-start
  65.4 2.4 %copy.21 = bf16[4,32,16,256]{3,2,1,0:T(8,128)(2,1)} copy(bf16[4,32,16,256]{3,2,1,0:T(8,128)(2,1)} %bitcast.12) | data formatting | bytes 2097152
  67.8 0.0 copy-done
  67.8 1.3 %copy.22 = f32[4,32,16,256]{3,2,1,0:T(8,128)} copy(f32[4,32,16,256]{3,2,1,0:T(8,128)S(1)} %bitcast.10) | data formatting | bytes 4194304
Async XLA Ops:
  65.4 2.4 %copy-start = (f32[4,512,256]{2,1,0:T(8,128)S(1)}, f32[4,512,256]{2,1,0:T(8,128)}, u32[]{:S(2)}) copy-start(f32[4,512,256]{2,1,0:T(8,128)} %get-tuple-element.5) | copy-start | bytes 6291460
